TPU v7x, 256 devices: a whole 4x4x8 slice. The times are simulated.
256 devices in a mesh: gx: 32 (over x, y, core), gy: 8 (over z).
Axes of the slice: x: 4, y: 4, z: 8, core: 2. Of those that a mesh axis runs over, the one named last changes fastest.
Arguments:
- pressure: float32 [10, 512, 2048], P(None, 'gx', 'gy'), may hold values from -6 to 6
- conductivity: float32 [10, 512, 2048], P(None, 'gx', 'gy'), may hold values from 0.1 to 10
- storage: float32 [10, 512, 2048], P(None, 'gx', 'gy'), may hold values from 0.5 to 2
- source: float32 [10, 512, 2048], P(None, 'gx', 'gy'), may hold values from -6 to 6
- particles: float32 [32, 8, 104, 8, 128], P('gx', 'gy'), may hold values from 0 to 1
- crossing: int32 [32, 8, 4], P('gx', 'gy'), may hold values from 0 to 16, as said below
- particle_cell: int32 [32, 8, 104, 128], P('gx', 'gy'), may hold values from 0 to 40959
- river_source: int32 [32, 8, 4, 2, 128], P('gx', 'gy'), may hold values from 0 to 4095
- river_target: int32 [32, 8, 4, 2, 128], P('gx', 'gy'), may hold values from 0 to 4095
Outputs:
- pressure_next: float32 [10, 512, 2048], P(None, 'gx', 'gy')
- particles_next: float32 [32, 8, 144, 8, 128], P('gx', 'gy')
- stream_inflow: float32 [512, 2048], P('gx', 'gy')
Inputs may be any that keep to these rules, and one draw needn't show every extreme that they name: `crossing`: entries for east and west are at most 16, for north and south at most 4; in every draw some tile sends the most in each direction.
All inputs are finite; a program needn't handle non-finite values.
Results may differ from a plain program's by a relative error of at most 0.0003.
Values sent between devices are 32-bit elements; how exact they have to be, the bound alone decides.
No kernel may reach another device: no remote copies, remote signals or barrier semaphores. Data moves between devices by JAX's collectives and lax.ppermute only.
A program may use at most 64 MiB of HBM per device.

v0:
```python
import jax
import jax.numpy as jnp
from jax import lax
from jax.sharding import PartitionSpec as P

ITERS = 4
CAPX = 16
CAPY = 4


OMEGA_RELAX = 0.8
VERTICAL = 4.0
POROSITY = 0.4
RESIDUAL_SAT = 0.1
TIME_STEP = 0.01
DECAY_RATE = 20.0


def with_halo(x, sides, width):
    for axis, dim in sides:
        size, length = (lax.axis_size(axis), x.shape[dim])
        up = [(i, (i + 1) % size) for i in range(size - 1)]
        down = [(j, i) for i, j in up]
        last = lax.slice_in_dim(x, length - width, length, axis=dim)
        initial = lax.slice_in_dim(x, 0, width, axis=dim)
        before = lax.ppermute(last, axis, up)
        after = lax.ppermute(initial, axis, down)
        x = jnp.concatenate([before, x, after], axis=dim)
    return x


def harmonic(left, right):
    total = left + right
    return 2.0 * left * right / (total + (total == 0.0).astype(total.dtype))


def vertical_pair(field):
    zero_layer = jnp.zeros_like(field[:1])
    above = jnp.concatenate([field[1:], zero_layer], 0)
    below = jnp.concatenate([zero_layer, field[:-1]], 0)
    return (above, below)


def beside_all(extended):
    middle = extended[:, :, 1:-1]
    center = middle[:, 1:-1]
    east = middle[:, 2:]
    west = middle[:, :-2]
    north = jnp.concatenate([center[:, :, 1:], extended[:, 1:-1, -1:]], 2)
    south = jnp.concatenate([extended[:, 1:-1, :1], center[:, :, :-1]], 2)
    return (center, east, west, north, south)


def jacobi_sweep(press_ext, cond_ext, stor, rhs):
    center, p_east, p_west, p_north, p_south = beside_all(press_ext)
    cond_mid, c_east, c_west, c_north, c_south = beside_all(cond_ext)
    press_up, press_down = vertical_pair(center)
    cond_up, cond_down = vertical_pair(cond_mid)
    pairs = [
        (p_east, c_east, 1.0),
        (p_west, c_west, 1.0),
        (p_north, c_north, 1.0),
        (p_south, c_south, 1.0),
        (press_up, cond_up, VERTICAL),
        (press_down, cond_down, VERTICAL),
    ]
    applied = stor * center
    diagonal = stor
    for neighbour, cond_near, factor in pairs:
        weight = factor * harmonic(cond_mid, cond_near)
        applied = applied + weight * (center - neighbour)
        diagonal = diagonal + weight
    return center + OMEGA_RELAX * (rhs - applied) / (
        diagonal + (diagonal == 0.0).astype(diagonal.dtype)
    )


def face_table(press_ext, cond_ext):
    center, p_east, p_west, p_north, p_south = beside_all(press_ext)
    cond_mid, c_east, c_west, c_north, c_south = beside_all(cond_ext)
    press_up, press_down = vertical_pair(center)
    cond_up, cond_down = vertical_pair(cond_mid)
    east = -harmonic(cond_mid, c_east) * (p_east - center)
    west = -harmonic(cond_mid, c_west) * (center - p_west)
    north = -harmonic(cond_mid, c_north) * (p_north - center)
    south = -harmonic(cond_mid, c_south) * (center - p_south)
    top = -VERTICAL * harmonic(cond_mid, cond_up) * (press_up - center + 1.0)
    bottom = -VERTICAL * harmonic(cond_mid, cond_down) * (center - press_down + 1.0)
    suction = jnp.maximum(-center, 0.0)
    saturation = RESIDUAL_SAT + (1.0 - RESIDUAL_SAT) * lax.rsqrt(1.0 + suction * suction)
    scale = 1.0 / (POROSITY * saturation)
    return jnp.stack(
        [
            west * scale,
            east * scale,
            south * scale,
            north * scale,
            bottom * scale,
            top * scale,
            saturation,
        ]
    )


def advance_records(records, sampled):
    pos_x = records[..., 0, :]
    pos_y = records[..., 1, :]
    pos_z = records[..., 2, :]
    speed_x = sampled[0] + pos_x * (sampled[1] - sampled[0])
    speed_y = sampled[2] + pos_y * (sampled[3] - sampled[2])
    speed_z = sampled[4] + pos_z * (sampled[5] - sampled[4])
    saturation = sampled[6]
    fields = [
        pos_x + TIME_STEP * speed_x,
        pos_y + TIME_STEP * speed_y,
        pos_z + TIME_STEP * speed_z,
        records[..., 3, :] + TIME_STEP,
        records[..., 4, :] * jnp.exp(-DECAY_RATE * TIME_STEP * saturation),
        saturation,
        records[..., 6, :] + TIME_STEP * speed_x,
        records[..., 7, :] + TIME_STEP * speed_y,
    ]
    return jnp.stack(fields, axis=-2)


def rim_pressure(field):
    return with_halo(field, (("gx", 1), ("gy", 2)), 1)


def body(
    pressure,
    conductivity,
    storage,
    source,
    particles,
    crossing,
    particle_cell,
    river_source,
    river_target,
):
    rhs = storage * pressure + source
    both_ext = with_halo(jnp.stack([pressure, conductivity]), (("gx", 2), ("gy", 3)), 1)
    cond_ext = both_ext[1]
    head = jacobi_sweep(both_ext[0], cond_ext, storage, rhs)
    for sweep_index in range(ITERS - 1):
        head = jacobi_sweep(rim_pressure(head), cond_ext, storage, rhs)
    table = face_table(rim_pressure(head), cond_ext)
    records = particles[0, 0]
    blocks = records.shape[0]
    starts = [0, CAPX, 2 * CAPX, 2 * CAPX + CAPY]
    caps = [CAPX, CAPX, CAPY, CAPY]
    cells = head.shape[0] * head.shape[1] * head.shape[2]
    flat_table = table.reshape(-1)
    field_offset = (jnp.arange(7, dtype=jnp.int32) * cells)[:, None, None]
    sampled = jnp.take(flat_table, particle_cell[0, 0][None] + field_offset)
    advanced = advance_records(records, sampled)
    slot = jnp.arange(blocks, dtype=jnp.int32)
    counts = crossing[0, 0]
    live = jnp.zeros((blocks,), bool)
    for index in range(4):
        inside = (slot >= starts[index]) & (slot < starts[index] + caps[index])
        live = live | inside & (slot - starts[index] < counts[index])
    kept = jnp.where(live[:, None, None], 0.0, advanced)
    sent = jnp.where(live[:, None, None], advanced, 0.0)
    top_layer = head[head.shape[0] - 1].reshape(-1)
    flow = jax.nn.softplus(top_layer[river_source[0, 0]])

    def payload(index):
        return jnp.concatenate(
            [sent[starts[index] : starts[index] + caps[index]].reshape(-1), flow[index].reshape(-1)]
        )

    along_x = jnp.stack([payload(1), payload(0)])
    got_x = with_halo(along_x, (("gx", 0),), 1)
    along_y = jnp.stack([payload(3), payload(2)])
    got_y = with_halo(along_y, (("gy", 0),), 1)
    arrivals = [got_x[0], got_x[3], got_y[0], got_y[3]]
    incoming = []
    flows_in = []
    for index in range(4):
        record_len = caps[index] * advanced.shape[1] * advanced.shape[2]
        piece = arrivals[index]
        incoming.append(
            piece[:record_len].reshape(caps[index], advanced.shape[1], advanced.shape[2])
        )
        flows_in.append(piece[record_len:].reshape(flow.shape[1], flow.shape[2]))
    arriving_flow = jnp.stack(flows_in)
    particles_next = jnp.concatenate([kept] + incoming, axis=0)[None, None]
    width_x = head.shape[1]
    width_y = head.shape[2]
    stream_inflow = (
        jnp.zeros((width_x * width_y,), jnp.float32)
        .at[river_target[0, 0].reshape(-1)]
        .add(arriving_flow.reshape(-1))
        .reshape(width_x, width_y)
    )
    return (head, particles_next, stream_inflow)


def solution(mesh):
    in_specs = (
        P(None, "gx", "gy"),
        P(None, "gx", "gy"),
        P(None, "gx", "gy"),
        P(None, "gx", "gy"),
        P("gx", "gy", None, None, None),
        P("gx", "gy", None),
        P("gx", "gy", None, None),
        P("gx", "gy", None, None, None),
        P("gx", "gy", None, None, None),
    )
    out_specs = (P(None, "gx", "gy"), P("gx", "gy", None, None, None), P("gx", "gy"))
    return jax.shard_map(body, mesh=mesh, in_specs=in_specs, out_specs=out_specs, check_vma=False)
```

profile of v0, /device:TPU:38, one launch (start us, length us, event | category | flops | bytes accessed | tf_op | source)
XLA Modules:
  0.0 656.2 jit_solution(12071731633067482595)
XLA Ops:
  1.8 1.9 collective-permute-start
  3.7 5.8 collective-permute-start.1
  11.4 3.8 collective-permute-start.2
  15.3 2.0 collective-permute-start.3
  17.3 2.6 and_or_fusion
  20.5 3.7 collective-permute-done.3
  26.4 4.3 collective-permute-start.4
  30.7 1.9 collective-permute-start.5
  32.7 5.1 collective-permute-done.5
  37.9 2.0 collective-permute-start.6
  40.0 4.8 collective-permute-start.7
  47.6 1.9 collective-permute-start.8
  49.6 2.4 collective-permute-start.9
  52.1 4.6 collective-permute-done.9
  56.8 1.9 collective-permute-start.10
  58.7 5.1 collective-permute-start.11
  68.6 2.4 collective-permute-start.13
  71.2 4.6 collective-permute-done.13
  77.8 5.1 collective-permute-start.15
  85.9 1.9 collective-permute-start.16
  87.9 5.8 collective-permute-start.17
  93.6 6.2 gather_fusion.1
  100.0 5.6 collective-permute-start.18
  105.6 1.9 collective-permute-start.19
  108.1 5.8 collective-permute-done.19
  115.0 515.5 %gather_fusion = f32[93184]{0:T(1024)S(1)} fusion(f32[286720]{0:T(1024)S(1)} %bitcast.147, s32[93184]{0:T(1024)S(1)} %broadcast_clamp_fusion), kind=kCustom, calls=%fused_computation | custom fusion | bytes 1118208 | tf_op jit(solution)/shard_map/jit(_take)/gather | solution.py:155
  631.0 1.9 collective-permute-start.23
  633.0 5.6 collective-permute-start.22
  638.7 1.9 collective-permute-start.21
  640.7 2.4 collective-permute-start.20
  643.3 5.2 collective-permute-done.20
  648.4 5.9 scatter_custom_fusion
  (138 shorter events, 23.0 us)
Async XLA Ops:
  0.6 10.6 %copy-start.1 = (f32[10,16,256]{2,1,0:T(8,128)S(1)}, f32[10,16,256]{2,1,0:T(8,128)}, u32[]{:S(2)}) copy-start(f32[10,16,256]{2,1,0:T(8,128)} %param.9) | copy-start | bytes 491524
  0.6 10.6 %copy-start.4 = (f32[10,16,256]{2,1,0:T(8,128)S(1)}, f32[10,16,256]{2,1,0:T(8,128)}, u32[]{:S(2)}) copy-start(f32[10,16,256]{2,1,0:T(8,128)} %param.10) | copy-start | bytes 491524
  0.7 9.9 %copy-start.8 = (s32[1,1,4,2,128]{4,3,2,1,0:T(2,128)S(1)}, s32[1,1,4,2,128]{4,3,2,1,0:T(2,128)}, u32[]{:S(2)}) copy-start(s32[1,1,4,2,128]{4,3,2,1,0:T(2,128)} %param.16) | copy-start | bytes 12292
  0.7 9.9 %copy-start.7 = (s32[1,1,4]{2,1,0:T(1,128)S(1)}, s32[1,1,4]{2,1,0:T(1,128)}, u32[]{:S(2)}) copy-start(s32[1,1,4]{2,1,0:T(1,128)} %param.14) | copy-start | bytes 52
  1.8 9.4 %collective-permute-start = (f32[2,10,1,256]{3,2,1,0:T(1,128)S(1)}, f32[2,10,1,256]{3,2,1,0:T(1,128)S(1)}, u32[]{:S(2)}, u32[]{:S(2)}) collective-permute-start(f32[2,10,1,256]{3,2,1,0:T(1,128)S(1)} %get-tuple-element.30), channel_id=1, source_target_pairs={{0,8},{8,16},{16,24},{24,32},{32,40},{40,48},{48,56},{56,64},{64,7... | collective-permute-start | bytes 61448 | tf_op jit(solution)/shard_map/ppermute | solution.py:26
  3.7 7.5 %collective-permute-start.1 = (f32[2,10,1,256]{3,2,1,0:T(1,128)S(1)}, f32[2,10,1,256]{3,2,1,0:T(1,128)S(1)}, u32[]{:S(2)}, u32[]{:S(2)}) collective-permute-start(f32[2,10,1,256]{3,2,1,0:T(1,128)S(1)} %get-tuple-element.31), channel_id=1, source_target_pairs={{8,0},{16,8},{24,16},{32,24},{40,32},{48,40},{56,48},{64,56},{72,6... | collective-permute-start | bytes 61448 | tf_op jit(solution)/shard_map/ppermute | solution.py:27
  10.4 9.4 %copy-start.5 = (f32[1,1,104,8,128]{4,3,2,1,0:T(8,128)S(1)}, f32[1,1,104,8,128]{4,3,2,1,0:T(8,128)}, u32[]{:S(2)}) copy-start(f32[1,1,104,8,128]{4,3,2,1,0:T(8,128)} %param.13) | copy-start | bytes 1277956
  11.4 9.0 %collective-permute-start.2 = (f32[2,10,18,1]{3,2,1,0:T(8,128)S(1)}, f32[2,10,18,1]{3,2,1,0:T(8,128)S(1)}, u32[]{:S(2)}, u32[]{:S(2)}) collective-permute-start(f32[2,10,18,1]{3,2,1,0:T(8,128)S(1)} %get-tuple-element.18), channel_id=1, source_target_pairs={{0,1},{1,2},{2,3},{3,4},{4,5},{5,6},{6,7},{8,9},{9,10},{10,11},{11... | collective-permute-start | bytes 4328 | tf_op jit(solution)/shard_map/ppermute | solution.py:26
  15.3 9.0 %collective-permute-start.3 = (f32[2,10,18,1]{3,2,1,0:T(8,128)S(1)}, f32[2,10,18,1]{3,2,1,0:T(8,128)S(1)}, u32[]{:S(2)}, u32[]{:S(2)}) collective-permute-start(f32[2,10,18,1]{3,2,1,0:T(8,128)S(1)} %get-tuple-element.19), channel_id=1, source_target_pairs={{1,0},{2,1},{3,2},{4,3},{5,4},{6,5},{7,6},{9,8},{10,9},{11,10},{12... | collective-permute-start | bytes 4328 | tf_op jit(solution)/shard_map/ppermute | solution.py:27
  26.4 6.3 collective-permute-start.4
  30.7 7.1 %collective-permute-start.5 = (f32[10,1,256]{2,1,0:T(1,128)S(1)}, f32[10,1,256]{2,1,0:T(1,128)S(1)}, u32[]{:S(2)}, u32[]{:S(2)}) collective-permute-start(f32[10,1,256]{2,1,0:T(1,128)S(1)} %get-tuple-element.63), channel_id=1, source_target_pairs={{0,8},{8,16},{16,24},{24,32},{32,40},{40,48},{48,56},{56,64},{64,7... | collective-permute-start | bytes 30728 | tf_op jit(solution)/shard_map/ppermute | solution.py:26
  37.9 7.8 %collective-permute-start.6 = (f32[10,18,1]{2,1,0:T(8,128)S(1)}, f32[10,18,1]{2,1,0:T(8,128)S(1)}, u32[]{:S(2)}, u32[]{:S(2)}) collective-permute-start(f32[10,18,1]{2,1,0:T(8,128)S(1)} %get-tuple-element.39), channel_id=1, source_target_pairs={{1,0},{2,1},{3,2},{4,3},{5,4},{6,5},{7,6},{9,8},{10,9},{11,10},{12... | collective-permute-start | bytes 2168 | tf_op jit(solution)/shard_map/ppermute | solution.py:27
  40.0 7.3 %collective-permute-start.7 = (f32[10,18,1]{2,1,0:T(8,128)S(1)}, f32[10,18,1]{2,1,0:T(8,128)S(1)}, u32[]{:S(2)}, u32[]{:S(2)}) collective-permute-start(f32[10,18,1]{2,1,0:T(8,128)S(1)} %get-tuple-element.38), channel_id=1, source_target_pairs={{0,1},{1,2},{2,3},{3,4},{4,5},{5,6},{6,7},{8,9},{9,10},{10,11},{11... | collective-permute-start | bytes 2168 | tf_op jit(solution)/shard_map/ppermute | solution.py:26
  47.6 4.5 collective-permute-start.8
  49.6 7.1 %collective-permute-start.9 = (f32[10,1,256]{2,1,0:T(1,128)S(1)}, f32[10,1,256]{2,1,0:T(1,128)S(1)}, u32[]{:S(2)}, u32[]{:S(2)}) collective-permute-start(f32[10,1,256]{2,1,0:T(1,128)S(1)} %get-tuple-element.57), channel_id=1, source_target_pairs={{0,8},{8,16},{16,24},{24,32},{32,40},{40,48},{48,56},{56,64},{64,7... | collective-permute-start | bytes 30728 | tf_op jit(solution)/shard_map/ppermute | solution.py:26
  56.8 8.0 %collective-permute-start.10 = (f32[10,18,1]{2,1,0:T(8,128)S(1)}, f32[10,18,1]{2,1,0:T(8,128)S(1)}, u32[]{:S(2)}, u32[]{:S(2)}) collective-permute-start(f32[10,18,1]{2,1,0:T(8,128)S(1)} %get-tuple-element.37), channel_id=1, source_target_pairs={{1,0},{2,1},{3,2},{4,3},{5,4},{6,5},{7,6},{9,8},{10,9},{11,10},{12... | collective-permute-start | bytes 2168 | tf_op jit(solution)/shard_map/ppermute | solution.py:27
  58.7 7.6 %collective-permute-start.11 = (f32[10,18,1]{2,1,0:T(8,128)S(1)}, f32[10,18,1]{2,1,0:T(8,128)S(1)}, u32[]{:S(2)}, u32[]{:S(2)}) collective-permute-start(f32[10,18,1]{2,1,0:T(8,128)S(1)} %get-tuple-element.36), channel_id=1, source_target_pairs={{0,1},{1,2},{2,3},{3,4},{4,5},{5,6},{6,7},{8,9},{9,10},{10,11},{11... | collective-permute-start | bytes 2168 | tf_op jit(solution)/shard_map/ppermute | solution.py:26
  66.7 4.5 collective-permute-start.12
  68.6 7.1 %collective-permute-start.13 = (f32[10,1,256]{2,1,0:T(1,128)S(1)}, f32[10,1,256]{2,1,0:T(1,128)S(1)}, u32[]{:S(2)}, u32[]{:S(2)}) collective-permute-start(f32[10,1,256]{2,1,0:T(1,128)S(1)} %get-tuple-element.51), channel_id=1, source_target_pairs={{0,8},{8,16},{16,24},{24,32},{32,40},{40,48},{48,56},{56,64},{64,7... | collective-permute-start | bytes 30728 | tf_op jit(solution)/shard_map/ppermute | solution.py:26
  75.9 8.0 %collective-permute-start.14 = (f32[10,18,1]{2,1,0:T(8,128)S(1)}, f32[10,18,1]{2,1,0:T(8,128)S(1)}, u32[]{:S(2)}, u32[]{:S(2)}) collective-permute-start(f32[10,18,1]{2,1,0:T(8,128)S(1)} %get-tuple-element.35), channel_id=1, source_target_pairs={{1,0},{2,1},{3,2},{4,3},{5,4},{6,5},{7,6},{9,8},{10,9},{11,10},{12... | collective-permute-start | bytes 2168 | tf_op jit(solution)/shard_map/ppermute | solution.py:27
  77.8 7.6 %collective-permute-start.15 = (f32[10,18,1]{2,1,0:T(8,128)S(1)}, f32[10,18,1]{2,1,0:T(8,128)S(1)}, u32[]{:S(2)}, u32[]{:S(2)}) collective-permute-start(f32[10,18,1]{2,1,0:T(8,128)S(1)} %get-tuple-element.34), channel_id=1, source_target_pairs={{0,1},{1,2},{2,3},{3,4},{4,5},{5,6},{6,7},{8,9},{9,10},{10,11},{11... | collective-permute-start | bytes 2168 | tf_op jit(solution)/shard_map/ppermute | solution.py:26
  85.8 28.5 %copy-start = (f32[10,16,256]{2,1,0:T(8,128)}, f32[10,16,256]{2,1,0:T(8,128)S(1)}, u32[]{:S(2)}) copy-start(f32[10,16,256]{2,1,0:T(8,128)S(1)} %fusion.24) | copy-start | bytes 491524
  85.9 13.9 %collective-permute-start.16 = (f32[10,1,256]{2,1,0:T(1,128)S(1)}, f32[10,1,256]{2,1,0:T(1,128)S(1)}, u32[]{:S(2)}, u32[]{:S(2)}) collective-permute-start(f32[10,1,256]{2,1,0:T(1,128)S(1)} %get-tuple-element.45), channel_id=1, source_target_pairs={{0,8},{8,16},{16,24},{24,32},{32,40},{40,48},{48,56},{56,64},{64,7... | collective-permute-start | bytes 30728 | tf_op jit(solution)/shard_map/ppermute | solution.py:26
  87.9 12.0 %collective-permute-start.17 = (f32[10,1,256]{2,1,0:T(1,128)S(1)}, f32[10,1,256]{2,1,0:T(1,128)S(1)}, u32[]{:S(2)}, u32[]{:S(2)}) collective-permute-start(f32[10,1,256]{2,1,0:T(1,128)S(1)} %get-tuple-element.44), channel_id=1, source_target_pairs={{8,0},{16,8},{24,16},{32,24},{40,32},{48,40},{56,48},{64,56},{72,6... | collective-permute-start | bytes 30728 | tf_op jit(solution)/shard_map/ppermute | solution.py:27
  100.0 8.0 %collective-permute-start.18 = (f32[10,18,1]{2,1,0:T(8,128)S(1)}, f32[10,18,1]{2,1,0:T(8,128)S(1)}, u32[]{:S(2)}, u32[]{:S(2)}) collective-permute-start(f32[10,18,1]{2,1,0:T(8,128)S(1)} %get-tuple-element.33), channel_id=1, source_target_pairs={{0,1},{1,2},{2,3},{3,4},{4,5},{5,6},{6,7},{8,9},{9,10},{10,11},{11... | collective-permute-start | bytes 2168 | tf_op jit(solution)/shard_map/ppermute | solution.py:26
  105.6 8.4 %collective-permute-start.19 = (f32[10,18,1]{2,1,0:T(8,128)S(1)}, f32[10,18,1]{2,1,0:T(8,128)S(1)}, u32[]{:S(2)}, u32[]{:S(2)}) collective-permute-start(f32[10,18,1]{2,1,0:T(8,128)S(1)} %get-tuple-element.32), channel_id=1, source_target_pairs={{1,0},{2,1},{3,2},{4,3},{5,4},{6,5},{7,6},{9,8},{10,9},{11,10},{12... | collective-permute-start | bytes 2168 | tf_op jit(solution)/shard_map/ppermute | solution.py:27
  114.9 515.5 %copy-start.6 = (s32[1,1,104,128]{3,2,1,0:T(8,128)S(1)}, s32[1,1,104,128]{3,2,1,0:T(8,128)}, u32[]{:S(2)}) copy-start(s32[1,1,104,128]{3,2,1,0:T(8,128)} %param.15) | copy-start | bytes 159748
  630.8 12.3 %copy-start.9 = (s32[1,1,4,2,128]{4,3,2,1,0:T(2,128)S(1)}, s32[1,1,4,2,128]{4,3,2,1,0:T(2,128)}, u32[]{:S(2)}) copy-start(s32[1,1,4,2,128]{4,3,2,1,0:T(2,128)} %param.17) | copy-start | bytes 12292
  631.0 12.1 %collective-permute-start.23 = (f32[1,4352]{1,0:T(1,128)S(1)}, f32[1,4352]{1,0:T(1,128)S(1)}, u32[]{:S(2)}, u32[]{:S(2)}) collective-permute-start(f32[1,4352]{1,0:T(1,128)S(1)} %stack.73), channel_id=1, source_target_pairs={{1,0},{2,1},{3,2},{4,3},{5,4},{6,5},{7,6},{9,8},{10,9},{11,10},{12... | collective-permute-start | bytes 52232 | tf_op jit(solution)/shard_map/ppermute | solution.py:27
  633.0 10.2 %collective-permute-start.22 = (f32[1,4352]{1,0:T(1,128)S(1)}, f32[1,4352]{1,0:T(1,128)S(1)}, u32[]{:S(2)}, u32[]{:S(2)}) collective-permute-start(f32[1,4352]{1,0:T(1,128)S(1)} %stack.72), channel_id=1, source_target_pairs={{0,1},{1,2},{2,3},{3,4},{4,5},{5,6},{6,7},{8,9},{9,10},{10,11},{11... | collective-permute-start | bytes 52232 | tf_op jit(solution)/shard_map/ppermute | solution.py:26
  638.7 4.6 collective-permute-start.21
  640.7 7.7 %collective-permute-start.20 = (f32[1,16640]{1,0:T(1,128)S(1)}, f32[1,16640]{1,0:T(1,128)S(1)}, u32[]{:S(2)}, u32[]{:S(2)}) collective-permute-start(f32[1,16640]{1,0:T(1,128)S(1)} %stack.70), channel_id=1, source_target_pairs={{0,8},{8,16},{16,24},{24,32},{32,40},{40,48},{48,56},{56,64},{64,7... | collective-permute-start | bytes 199688 | tf_op jit(solution)/shard_map/ppermute | solution.py:26
  (2 other events, 1.9 us)
where the time goes:
time: 660 us; the launch traced here: 656 us
  local copies, waits for them, and re-layouts  527 us (80%)
  starting transfers between devices  76.3 us (12%)
  waiting for transfers between devices  36.9 us (6%)
  other arithmetic  14.2 us (2%)
    gather x1, local copies, waits for them, and re-layouts, body(): sampled = jnp.take(flat_table, particle_cell[0, 0][None] + field_offset)  515 us
    ppermute x12, starting transfers between devices, with_halo(): before = lax.ppermute(last, axis, up)  43 us
    ppermute x12, starting transfers between devices, with_halo(): after = lax.ppermute(initial, axis, down)  33.3 us
    ppermute x12, waiting for transfers between devices, with_halo(): before = lax.ppermute(last, axis, up)  24.6 us
  transfers between devices with their start and end apart: 24, of which 14 were waited for; matrix products, arithmetic and copies ran while one was open for 2% of the time, Pallas kernels for 0%

commit v1 on v0

v1 whole, which is shorter than its diff:
```python
import functools

import jax
import jax.numpy as jnp
from jax import lax
from jax.experimental import pallas as pl
from jax.experimental.pallas import tpu as pltpu
from jax.sharding import PartitionSpec as P

F32 = jnp.float32
BF16 = jnp.bfloat16

ITERS = 4
CAPX = 16
CAPY = 4
NZ = 10
CX = 16
CY = 256
PB = 104
SENT = 2 * CAPX + 2 * CAPY
KEEP = PB - SENT
OUT = PB + SENT
GROUP = 8

OMEGA_RELAX = 0.8
VERTICAL = 4.0
POROSITY = 0.4
RESIDUAL_SAT = 0.1
TIME_STEP = 0.01
DECAY_RATE = 20.0

ROWS = CX + 8
LANES = CY + 128

EAST = 0
NORTH = 176
SOUTH = 336
LEVEL = 496
SATUR = 640
TABLE = 800


def harmonic(left, right):
    total = left + right
    return 2.0 * left * right / (total + (total == 0.0).astype(total.dtype))


def index_of(shape, axis):
    return lax.broadcasted_iota(jnp.int32, shape, axis)


def roll(x, shift, axis):
    return pltpu.roll(x, shift % x.shape[axis], axis)


def edge_rows_kernel(par_ref, p_ref, c_ref, s_ref, q_ref, even_ref, odd_ref):
    parity = par_ref[0]
    row = index_of((1, 8, CY), 1)
    pieces = []
    for start, step, outer in ((0, -1, 3), (8, 1, 4)):
        tile = slice(start, start + 8)
        p, c, s, q = (ref[:, tile, :] for ref in (p_ref, c_ref, s_ref, q_ref))
        weight = jnp.where(row == outer, harmonic(c, roll(c, step, 1)), 0.0)
        rhs = s * p + q + weight * roll(p, step, 1)
        side = slice(0, 4) if start == 0 else slice(4, 8)
        pieces.append(jnp.concatenate([p[:, side], c[:, side], (s + weight)[:, side], rhs[:, side]], axis=1))
    west, east = pieces
    even_ref[...] = jnp.where(parity == 0, east, west)
    odd_ref[...] = jnp.where(parity == 0, west, east)


def edge_lanes_kernel(par_ref, p_ref, c_ref, s_ref, q_ref, re_ref, ro_ref, ext_ref, even_ref, odd_ref):
    par_x = par_ref[0]
    par_y = par_ref[1]
    own = [p_ref[...], c_ref[...], s_ref[...], s_ref[...] * p_ref[...] + q_ref[...]]
    from_even = re_ref[...]
    from_odd = ro_ref[...]
    east = jnp.where(par_x == 0, from_even, from_odd)
    west = jnp.where(par_x == 0, from_odd, from_even)
    for f in range(4):
        ext_ref[f, :, 0:CX, :] = own[f]
        ext_ref[f, :, CX:ROWS, :] = jnp.concatenate(
            [east[:, 4 * f : 4 * f + 4], west[:, 4 * f : 4 * f + 4]], axis=1
        )
    lane = index_of((1, 1, 128), 2)
    packed = []
    for start, step, outer, low in ((0, -1, 3, 0), (128, 1, 124, 124)):
        p, c, s, r = (ext_ref[f, :, :, start : start + 128] for f in range(4))
        weight = jnp.where(lane == outer, harmonic(c, roll(c, step, 2)), 0.0)
        fields = [p, c, s + weight, r + weight * roll(p, step, 2)]
        inside = (lane >= low) & (lane < low + 4)
        total = [jnp.zeros((8, 128), F32) for _ in range(4)]
        for f in range(4):
            rows = jnp.where(inside, fields[f], 0.0).reshape(30, 8, 128)
            for i in range(30):
                slot = 8 * f + i % 8
                total[i // 8] = total[i // 8] + roll(rows[i], 4 * slot - low, 1)
        packed.append(total)
    south, north = packed
    for j in range(4):
        even_ref[j] = jnp.where(par_y == 0, north[j], south[j])
        odd_ref[j] = jnp.where(par_y == 0, south[j], north[j])


def one_hot(values, size, lanes):
    return jnp.where(index_of((size, lanes), 0) == values, 1.0, 0.0).astype(BF16)


def split(x, parts):
    out = []
    for _ in range(parts):
        piece = x.astype(BF16)
        out.append(piece)
        x = x - piece.astype(F32)
    return out


def sample(tab_ref, cells, found_ref):
    lanes = cells.shape[1]
    hot = one_hot(cells & (CY - 1), CY, lanes)
    found_ref[...] = jnp.dot(tab_ref[...], jnp.concatenate([hot, hot], 0), preferred_element_type=F32)
    high = cells >> 8
    column = high & (CX - 1)
    west_row = jnp.where(column == 0, NZ * CX + (high >> 4), high - 1)
    row = index_of((8, lanes), 0)
    here = high - row
    beside = west_row - row
    west = east = north = south = top = bottom = satur = jnp.zeros((8, lanes), F32)
    for g in range(22):
        at = 8 * g
        face = found_ref[at : at + 8, :]
        west = west + jnp.where(beside == at, face, 0.0)
        if g < 20:
            mask = here == at
            east = east + jnp.where(mask, face, 0.0)
            north = north + jnp.where(mask, found_ref[NORTH + at : NORTH + at + 8, :], 0.0)
            south = south + jnp.where(mask, found_ref[SOUTH + at : SOUTH + at + 8, :], 0.0)
            satur = satur + jnp.where(mask, found_ref[SATUR + at : SATUR + at + 8, :], 0.0)
            if g < 18:
                top = top + jnp.where(mask, found_ref[LEVEL + at : LEVEL + at + 8, :], 0.0)
            if g >= 2:
                bottom = bottom + jnp.where(mask, found_ref[LEVEL + at - 16 : LEVEL + at - 8, :], 0.0)
    return [jnp.sum(v, axis=0, keepdims=True) for v in (west, east, south, north, bottom, top, satur)]


def advance(record, sampled):
    west, east, south, north, bottom, top, satur = sampled
    scale = TIME_STEP / (POROSITY * satur)
    move_x = scale * (west + record[0:1] * (east - west))
    move_y = scale * (south + record[1:2] * (north - south))
    move_z = scale * (bottom + record[2:3] * (top - bottom))
    row = index_of(record.shape, 0)
    step = jnp.where(
        (row == 0) | (row == 6),
        move_x,
        jnp.where((row == 1) | (row == 7), move_y, jnp.where(row == 2, move_z, TIME_STEP)),
    )
    decayed = record * jnp.exp(-DECAY_RATE * TIME_STEP * satur)
    return jnp.where(row == 4, decayed, jnp.where(row == 5, satur, record + step))


def advance_group(tab_ref, cell_ref, rec_ref, found_ref, first, store):
    cells = jnp.concatenate([cell_ref[pl.ds(first + j, 1), :] for j in range(GROUP)], axis=1)
    sampled = sample(tab_ref, cells, found_ref)
    for j in range(GROUP):
        mine = [v[:, 128 * j : 128 * j + 128] for v in sampled]
        store(first + j, advance(rec_ref[first + j], mine))


def sweep_kernel(
    par_ref, cross_ref, ext_ref, re_ref, ro_ref, rec_ref, cell_ref, source_ref,
    head_ref, tab_ref, next_ref, xe_ref, xo_ref, ye_ref, yo_ref,
    h0, h1, cond, rhs, inv, wx, wy, wz, flat, found, kept, sent, sem,
):
    par_x = par_ref[0]
    par_y = par_ref[1]
    lane = index_of((1, 128), 1)
    fields = (h0, cond, inv, rhs)
    north = [jnp.where(par_y == 0, re_ref[j], ro_ref[j]) for j in range(4)]
    south = [jnp.where(par_y == 0, ro_ref[j], re_ref[j]) for j in range(4)]
    for f in range(4):
        for k in range(NZ):
            fields[f][k, :, 0:CY] = ext_ref[f, k]
            for t in range(3):
                i = 3 * k + t
                slot = 8 * f + i % 8
                up = roll(north[i // 8], -4 * slot, 1)
                down = roll(south[i // 8], 124 - 4 * slot, 1)
                fields[f][k, 8 * t : 8 * t + 8, CY:LANES] = jnp.where(
                    lane < 4, up, jnp.where(lane >= 124, down, 0.0)
                )
    row = index_of((ROWS, 1), 0)
    for k in range(NZ):
        c = cond[k]
        w_x = jnp.where(row == CX + 3, 0.0, harmonic(c, roll(c, -1, 0)))
        w_y = harmonic(c, roll(c, -1, 1))
        diag = inv[k] + w_x + roll(w_x, 1, 0) + w_y + roll(w_y, 1, 1)
        if k > 0:
            diag = diag + wz[k - 1]
        if k < NZ - 1:
            w_z = VERTICAL * harmonic(c, cond[k + 1])
            wz[k] = w_z
            diag = diag + w_z
        wx[k] = w_x
        wy[k] = w_y
        inv[k] = OMEGA_RELAX / (diag + (diag == 0.0).astype(F32))
    old, new = h0, h1
    for _ in range(ITERS):
        for k in range(NZ):
            h = old[k]
            w_x = wx[k]
            w_y = wy[k]
            total = rhs[k] + w_x * roll(h, -1, 0) + roll(w_x * h, 1, 0)
            total = total + w_y * roll(h, -1, 1) + roll(w_y * h, 1, 1)
            if k > 0:
                total = total + wz[k - 1] * old[k - 1]
            if k < NZ - 1:
                total = total + wz[k] * old[k + 1]
            new[k] = (1.0 - OMEGA_RELAX) * h + inv[k] * total
        old, new = new, old
    flat[NZ * CX : NORTH, :] = jnp.zeros((16, CY), F32)
    for k in range(NZ):
        h = old[k]
        at = slice(CX * k, CX * k + CX)
        face_x = -wx[k] * (roll(h, -1, 0) - h)
        face_y = -wy[k] * (roll(h, -1, 1) - h)
        mine = h[0:CX, 0:CY]
        head_ref[k] = mine
        flat[EAST + CX * k : EAST + CX * k + CX, :] = face_x[0:CX, 0:CY]
        flat[NZ * CX + k : NZ * CX + k + 1, :] = face_x[ROWS - 1 : ROWS, 0:CY]
        flat[NORTH + CX * k : NORTH + CX * k + CX, :] = face_y[0:CX, 0:CY]
        flat[SOUTH + CX * k : SOUTH + CX * k + CX, :] = roll(face_y, 1, 1)[0:CX, 0:CY]
        if k < NZ - 1:
            face_z = -wz[k, 0:CX, 0:CY] * (old[k + 1, 0:CX, 0:CY] - mine + 1.0)
            flat[LEVEL + CX * k : LEVEL + CX * k + CX, :] = face_z
        suction = jnp.maximum(-mine, 0.0)
        flat[SATUR + CX * k : SATUR + CX * k + CX, :] = RESIDUAL_SAT + (1.0 - RESIDUAL_SAT) * lax.rsqrt(
            1.0 + suction * suction
        )
    coarse, fine = split(flat[...], 2)
    tab_ref[:, 0:CY] = coarse
    tab_ref[:, CY : 2 * CY] = fine

    def store(slot, record):
        group = jnp.where(slot < CAPX, 0, jnp.where(slot < 2 * CAPX, 1, jnp.where(slot < 2 * CAPX + CAPY, 2, 3)))
        start = jnp.where(slot < CAPX, 0, jnp.where(slot < 2 * CAPX, CAPX, jnp.where(slot < 2 * CAPX + CAPY, 2 * CAPX, 2 * CAPX + CAPY)))
        live = slot - start < cross_ref[group]
        kept[slot] = jnp.where(live, 0.0, record)
        sent[slot] = jnp.where(live, record, 0.0)

    def group_step(i, carry):
        advance_group(tab_ref, cell_ref, rec_ref, found, i * GROUP, store)
        return carry

    lax.fori_loop(0, SENT // GROUP, group_step, 0)
    copy = pltpu.make_async_copy(kept, next_ref.at[pl.ds(0, SENT)], sem)
    copy.start()
    links = jnp.concatenate([source_ref[j : j + 1, :] for j in range(8)], axis=1)
    surface = jnp.concatenate(split(old[NZ - 1, 0:CX, 0:CY], 3), axis=0)
    at_links = jnp.dot(surface, one_hot(links & (CY - 1), CY, 1024), preferred_element_type=F32)
    at_links = at_links[0:CX] + at_links[CX : 2 * CX] + at_links[2 * CX : 3 * CX]
    picked = jnp.where(index_of((CX, 1024), 0) == (links >> 8), at_links, 0.0)
    value = jnp.sum(picked, axis=0, keepdims=True)
    flow = jnp.maximum(value, 0.0) + jnp.log1p(jnp.exp(-jnp.abs(value)))
    flows = [
        jnp.concatenate([flow[:, 256 * d : 256 * d + 128], flow[:, 256 * d + 128 : 256 * d + 256]] * 4, axis=0)
        for d in range(4)
    ]
    for ref, par, low, cap in (
        (xe_ref, par_x, 0, CAPX),
        (xo_ref, 1 - par_x, 0, CAPX),
        (ye_ref, par_y, 2, CAPY),
        (yo_ref, 1 - par_y, 2, CAPY),
    ):
        base = 2 * CAPX if low else 0
        ref[0:cap] = sent[pl.ds(base + par * cap, cap)]
        ref[cap] = jnp.where(par == 0, flows[low], flows[low + 1])
    copy.wait()


def rest_kernel(tab_ref, rec_ref, cell_ref, prev_ref, next_ref, found, kept, sem):
    def store(slot, record):
        kept[slot - SENT] = record

    def group_step(i, carry):
        advance_group(tab_ref, cell_ref, rec_ref, found, SENT + i * GROUP, store)
        return carry

    lax.fori_loop(0, KEEP // GROUP, group_step, 0)
    copy = pltpu.make_async_copy(kept, next_ref.at[pl.ds(SENT, KEEP)], sem)
    copy.start()
    copy.wait()


def arrive_kernel(par_ref, target_ref, xe_ref, xo_ref, ye_ref, yo_ref, prev_ref, next_ref, inflow_ref, sems):
    par_x = par_ref[0]
    par_y = par_ref[1]
    copies = []
    for n, (ref, par, base, cap) in enumerate(
        (
            (xe_ref, 1 - par_x, PB, CAPX),
            (xo_ref, par_x, PB, CAPX),
            (ye_ref, 1 - par_y, PB + 2 * CAPX, CAPY),
            (yo_ref, par_y, PB + 2 * CAPX, CAPY),
        )
    ):
        copies.append(
            pltpu.make_async_copy(ref.at[pl.ds(0, cap)], next_ref.at[pl.ds(base + par * cap, cap)], sems.at[n])
        )
    for copy in copies:
        copy.start()
    x_even, x_odd = xe_ref[CAPX], xo_ref[CAPX]
    y_even, y_odd = ye_ref[CAPY], yo_ref[CAPY]
    arrivals = [
        jnp.where(par_x == 0, x_odd, x_even),
        jnp.where(par_x == 0, x_even, x_odd),
        jnp.where(par_y == 0, y_odd, y_even),
        jnp.where(par_y == 0, y_even, y_odd),
    ]
    flow = jnp.concatenate([a[r : r + 1] for a in arrivals for r in range(2)], axis=1)
    links = jnp.concatenate([target_ref[j : j + 1, :] for j in range(8)], axis=1)
    spread = jnp.where(index_of((CX, 1024), 0) == (links >> 8), flow, 0.0)
    parts = jnp.concatenate(split(spread, 3), axis=0)
    hot = one_hot(links & (CY - 1), CY, 1024)
    total = lax.dot_general(parts, hot, (((1,), (1,)), ((), ())), preferred_element_type=F32)
    inflow_ref[...] = total[0:CX] + total[CX : 2 * CX] + total[2 * CX : 3 * CX]
    for copy in copies:
        copy.wait()


VMEM = pl.BlockSpec(memory_space=pltpu.VMEM)
SMEM = pl.BlockSpec(memory_space=pltpu.SMEM)
ANY = pl.BlockSpec(memory_space=pl.ANY)
LIMIT = pltpu.CompilerParams(vmem_limit_bytes=32 << 20)


def swap(size, first):
    pairs = []
    for i in range(first, size - 1, 2):
        pairs += [(i, i + 1), (i + 1, i)]
    return pairs


def exchange(even, odd, axis):
    size = lax.axis_size(axis)
    return lax.ppermute(even, axis, swap(size, 0)), lax.ppermute(odd, axis, swap(size, 1))


def shape(*dims, dtype=F32):
    return jax.ShapeDtypeStruct(dims, dtype)


def body(
    pressure, conductivity, storage, source, particles, crossing, particle_cell, river_source, river_target
):
    parity = jnp.stack([lax.axis_index("gx") % 2, lax.axis_index("gy") % 2]).astype(jnp.int32)
    grid = (pressure, conductivity, storage, source)
    x_even, x_odd = pl.pallas_call(
        edge_rows_kernel,
        out_shape=(shape(NZ, 16, CY), shape(NZ, 16, CY)),
        in_specs=[SMEM] + [VMEM] * 4,
        out_specs=(VMEM, VMEM),
        compiler_params=LIMIT,
        name="edge_rows",
    )(parity, *grid)
    x_even, x_odd = exchange(x_even, x_odd, "gx")
    extended, y_even, y_odd = pl.pallas_call(
        edge_lanes_kernel,
        out_shape=(shape(4, NZ, ROWS, CY), shape(4, 8, 128), shape(4, 8, 128)),
        in_specs=[SMEM] + [VMEM] * 6,
        out_specs=(VMEM,) * 3,
        compiler_params=LIMIT,
        name="edge_lanes",
    )(parity, *grid, x_even, x_odd)
    y_even, y_odd = exchange(y_even, y_odd, "gy")
    records = particles[0, 0]
    cells = particle_cell[0, 0]
    field = pltpu.VMEM((NZ, ROWS, LANES), F32)
    found = pltpu.VMEM((TABLE, 128 * GROUP), F32)
    head, table, moved, x_even, x_odd, y_even, y_odd = pl.pallas_call(
        sweep_kernel,
        out_shape=(
            shape(NZ, CX, CY),
            shape(TABLE, 2 * CY, dtype=BF16),
            shape(OUT, 8, 128),
            shape(CAPX + 1, 8, 128),
            shape(CAPX + 1, 8, 128),
            shape(CAPY + 1, 8, 128),
            shape(CAPY + 1, 8, 128),
        ),
        in_specs=[SMEM, SMEM] + [VMEM] * 6,
        out_specs=(VMEM, VMEM, ANY) + (VMEM,) * 4,
        scratch_shapes=[field] * 8
        + [
            pltpu.VMEM((TABLE, CY), F32),
            found,
            pltpu.VMEM((SENT, 8, 128), F32),
            pltpu.VMEM((SENT, 8, 128), F32),
            pltpu.SemaphoreType.DMA,
        ],
        compiler_params=LIMIT,
        name="sweep",
    )(
        parity, crossing[0, 0], extended, y_even, y_odd, records, cells,
        river_source.reshape(8, 128),
    )
    x_even, x_odd = exchange(x_even, x_odd, "gx")
    y_even, y_odd = exchange(y_even, y_odd, "gy")
    moved = pl.pallas_call(
        rest_kernel,
        out_shape=shape(OUT, 8, 128),
        in_specs=[VMEM] * 3 + [ANY],
        out_specs=ANY,
        scratch_shapes=[found, pltpu.VMEM((KEEP, 8, 128), F32), pltpu.SemaphoreType.DMA],
        input_output_aliases={3: 0},
        compiler_params=LIMIT,
        cost_estimate=pl.CostEstimate(
            flops=2 * TABLE * 512 * 128 * KEEP, bytes_accessed=4 << 20, transcendentals=0
        ),
        name="rest",
    )(table, records, cells, moved)
    moved, inflow = pl.pallas_call(
        arrive_kernel,
        out_shape=(shape(OUT, 8, 128), shape(CX, CY)),
        in_specs=[SMEM] + [VMEM] * 5 + [ANY],
        out_specs=(ANY, VMEM),
        scratch_shapes=[pltpu.SemaphoreType.DMA((4,))],
        input_output_aliases={6: 0},
        compiler_params=LIMIT,
        name="arrive",
    )(parity, river_target.reshape(8, 128), x_even, x_odd, y_even, y_odd, moved)
    return head, moved[None, None], inflow


def solution(mesh):
    in_specs = (
        P(None, "gx", "gy"),
        P(None, "gx", "gy"),
        P(None, "gx", "gy"),
        P(None, "gx", "gy"),
        P("gx", "gy", None, None, None),
        P("gx", "gy", None),
        P("gx", "gy", None, None),
        P("gx", "gy", None, None, None),
        P("gx", "gy", None, None, None),
    )
    out_specs = (P(None, "gx", "gy"), P("gx", "gy", None, None, None), P("gx", "gy"))
    return jax.shard_map(body, mesh=mesh, in_specs=in_specs, out_specs=out_specs, check_vma=False)
```

time: 660 us -> 56.2 us (0.09)
  local copies, waits for them, and re-layouts: 527 us -> 4.36 us
  starting transfers between devices: 76.3 us -> 21.1 us
  waiting for transfers between devices: 36.9 us -> 5.18 us
  Pallas kernels: 0 us -> 24.3 us
  other arithmetic: 14.2 us -> 0.08 us
    gather x2 -> x0, local copies, waits for them, and re-layouts: 522 us -> none  [the longest x1 515 us: body(): sampled = jnp.take(flat_table, particle_cell[0, 0][None] + field_offset)]
    ppermute x24 -> x8, starting transfers between devices: 76.3 us -> 21.1 us  [the longest x4 20.6 us: exchange(): lax.ppermute(odd, axis, swap(size, 1))]
    ppermute x24 -> x8, waiting for transfers between devices: 36.9 us -> 5.18 us  [the longest x4 5.17 us: exchange(): lax.ppermute(odd, axis, swap(size, 1))]
    pallas_call x0 -> x5, Pallas kernels: none -> 24.3 us  [the longest x1 10.7 us: body(): pl.pallas_call(sweep_kernel, out_shape=(shape(NZ, CX, CY), shape(TABLE, 2...]
  transfers between devices with their start and end apart: 24 -> 8, of which waited for: 14 -> 2; matrix products, arithmetic and copies ran while one was open for 2% -> 0% of each run, Pallas kernels for 0% -> 18%
where the time goes in v1:
time: 56.2 us; the launch traced here: 55.9 us
  Pallas kernels  24.3 us (43%)
  starting transfers between devices  21.1 us (38%)
  waiting for transfers between devices  5.18 us (9%)
  local copies, waits for them, and re-layouts  4.36 us (8%)
  between operations  0.82 us (1%)
    ppermute x4, starting transfers between devices, exchange(): lax.ppermute(odd, axis, swap(size, 1))  20.6 us
    pallas_call x1, Pallas kernels, body(): pl.pallas_call(sweep_kernel, out_shape=(shape(NZ, CX, CY), shape(TABLE, 2...  10.7 us
    pallas_call x1, Pallas kernels, body(): pl.pallas_call(rest_kernel, out_shape=shape(OUT, 8, 128), in_specs=[VMEM]...  10.1 us
    ppermute x4, waiting for transfers between devices, exchange(): lax.ppermute(odd, axis, swap(size, 1))  5.17 us
    unnamed x18, local copies, waits for them, and re-layouts  4.36 us
    pallas_call x1, Pallas kernels, body(): pl.pallas_call(arrive_kernel, out_shape=(shape(OUT, 8, 128), shape(CX, CY...  1.87 us
  transfers between devices with their start and end apart: 8, of which 2 were waited for; matrix products, arithmetic and copies ran while one was open for 0% of the time, Pallas kernels for 18%

profile of v1, /device:TPU:38, one launch (start us, length us, event | category | flops | bytes accessed | tf_op | source)
XLA Modules:
  0.0 55.9 jit_solution(11087809248809616348)
XLA Ops:
  0.6 0.1 pad_add_fusion.par_ref
  0.7 0.9 %copy-done = f32[10,16,256]{2,1,0:T(8,128)S(1)} copy-done((f32[10,16,256]{2,1,0:T(8,128)S(1)}, f32[10,16,256]{2,1,0:T(8,128)}, u32[]{:S(2)}) %copy-start) | copy-done | bytes 163864
  1.6 0.9 %copy-done.1 = f32[10,16,256]{2,1,0:T(8,128)S(1)} copy-done((f32[10,16,256]{2,1,0:T(8,128)S(1)}, f32[10,16,256]{2,1,0:T(8,128)}, u32[]{:S(2)}) %copy-start.1) | copy-done | bytes 163864
  2.6 0.9 %copy-done.2 = f32[10,16,256]{2,1,0:T(8,128)S(1)} copy-done((f32[10,16,256]{2,1,0:T(8,128)S(1)}, f32[10,16,256]{2,1,0:T(8,128)}, u32[]{:S(2)}) %copy-start.2) | copy-done | bytes 163864
  3.5 0.9 %copy-done.3 = f32[10,16,256]{2,1,0:T(8,128)S(1)} copy-done((f32[10,16,256]{2,1,0:T(8,128)S(1)}, f32[10,16,256]{2,1,0:T(8,128)}, u32[]{:S(2)}) %copy-start.3) | copy-done | bytes 163864
  4.4 0.7 %edge_rows.1 = (f32[10,16,256]{2,1,0:T(8,128)S(1)}, f32[10,16,256]{2,1,0:T(8,128)S(1)}) custom-call(s32[2]{0:T(128)S(1)} %pad_add_fusion.par_ref, f32[10,16,256]{2,1,0:T(8,128)S(1)} %copy-done, f32[10,16,256]{2,1,0:T(8,128)S(1)} %copy-done.1, f32[10,16,256]{2,1,0:T(8,128)S(1)} %copy-done.2, f32[10,16,256]{2,1,0:T(8,128)S(1)} %copy-done.3), custom_call_target="tpu_custom_call" | custom-call | tf_op jit(solution)/shard_map/edge_rows/pallas_call | solution.py:358
  5.1 0.1 collective-permute-start
  5.2 0.0 copy-start.4
  5.2 0.0 copy-start.5
  5.2 5.4 %collective-permute-start.1 = (f32[10,16,256]{2,1,0:T(8,128)S(1)}, f32[10,16,256]{2,1,0:T(8,128)S(1)}, u32[]{:S(2)}, u32[]{:S(2)}) collective-permute-start(f32[10,16,256]{2,1,0:T(8,128)S(1)} %get-tuple-element.18), channel_id=1, source_target_pairs={{8,16},{16,8},{24,32},{32,24},{40,48},{48,40},{56,64},{64,56},{72,... | collective-permute-start | bytes 491528 | tf_op jit(solution)/shard_map/ppermute | solution.py:346
  10.6 0.0 collective-permute-done.re_ref
  10.6 3.5 %collective-permute-done.1.ro_ref = f32[10,16,256]{2,1,0:T(8,128)S(1)} collective-permute-done((f32[10,16,256]{2,1,0:T(8,128)S(1)}, f32[10,16,256]{2,1,0:T(8,128)S(1)}, u32[]{:S(2)}, u32[]{:S(2)}) %collective-permute-start.1) | collective-permute-done | bytes 163872 | tf_op jit(solution)/shard_map/ppermute | solution.py:346
  14.1 1.0 %edge_lanes.1 = (f32[4,10,24,256]{3,2,1,0:T(8,128)S(1)}, f32[4,8,128]{2,1,0:T(8,128)S(1)}, f32[4,8,128]{2,1,0:T(8,128)S(1)}) custom-call(s32[2]{0:T(128)S(1)} %pad_add_fusion.par_ref, f32[10,16,256]{2,1,0:T(8,128)S(1)} %copy-done, f32[10,16,256]{2,1,0:T(8,128)S(1)} %copy-done.1, f32[10,16,256]{2,1,0:T(8,128)S(1)} %copy-done.2, f32[10,16,256]{2,1,0:T(8,128)S(1)} %copy-done.3, ...), custom_call_target="tpu_custom_call" | custom-call | tf_op jit(solution)/shard_map/edge_lanes/pallas_call | solution.py:367
  15.1 0.2 collective-permute-start.2
  15.3 5.6 %collective-permute-start.3 = (f32[4,8,128]{2,1,0:T(8,128)S(1)}, f32[4,8,128]{2,1,0:T(8,128)S(1)}, u32[]{:S(2)}, u32[]{:S(2)}) collective-permute-start(f32[4,8,128]{2,1,0:T(8,128)S(1)} %get-tuple-element.21), channel_id=1, source_target_pairs={{1,2},{2,1},{3,4},{4,3},{5,6},{6,5},{9,10},{10,9},{11,12},{12,11},... | collective-permute-start | bytes 49160 | tf_op jit(solution)/shard_map/ppermute | solution.py:346
  20.9 0.0 collective-permute-done.2.re_ref
  20.9 1.7 %collective-permute-done.3.ro_ref = f32[4,8,128]{2,1,0:T(8,128)S(1)} collective-permute-done((f32[4,8,128]{2,1,0:T(8,128)S(1)}, f32[4,8,128]{2,1,0:T(8,128)S(1)}, u32[]{:S(2)}, u32[]{:S(2)}) %collective-permute-start.3) | collective-permute-done | bytes 16416 | tf_op jit(solution)/shard_map/ppermute | solution.py:346
  22.6 0.0 copy-done.4
  22.6 0.0 copy-done.5
  22.6 0.7 %copy-done.6 = s32[1,1,4,2,128]{4,3,2,1,0:T(2,128)S(1)} copy-done((s32[1,1,4,2,128]{4,3,2,1,0:T(2,128)S(1)}, s32[1,1,4,2,128]{4,3,2,1,0:T(2,128)}, u32[]{:S(2)}) %copy-start.6) | copy-done | bytes 4120
  23.3 10.7 %sweep.1 = (f32[10,16,256]{2,1,0:T(8,128)}, bf16[800,512]{1,0:T(8,128)(2,1)S(1)}, f32[144,8,128]{2,1,0:T(8,128)}, f32[17,8,128]{2,1,0:T(8,128)S(1)}, f32[17,8,12...) custom-call(s32[2]{0:T(128)S(1)} %pad_add_fusion.par_ref, s32[4]{0:T(128)S(1)} %bitcast.14, ...), custom_call_target="tpu_custom_call" | custom-call | tf_op jit(solution)/shard_map/sweep/pallas_call | solution.py:380
  34.0 0.1 collective-permute-start.6
  34.1 6.0 %collective-permute-start.7 = (f32[5,8,128]{2,1,0:T(8,128)S(1)}, f32[5,8,128]{2,1,0:T(8,128)S(1)}, u32[]{:S(2)}, u32[]{:S(2)}) collective-permute-start(f32[5,8,128]{2,1,0:T(8,128)S(1)} %get-tuple-element.26), channel_id=1, source_target_pairs={{1,2},{2,1},{3,4},{4,3},{5,6},{6,5},{9,10},{10,9},{11,12},{12,11},... | collective-permute-start | bytes 61448 | tf_op jit(solution)/shard_map/ppermute | solution.py:346
  40.1 0.1 collective-permute-start.4
  40.2 3.6 %collective-permute-start.5 = (f32[17,8,128]{2,1,0:T(8,128)S(1)}, f32[17,8,128]{2,1,0:T(8,128)S(1)}, u32[]{:S(2)}, u32[]{:S(2)}) collective-permute-start(f32[17,8,128]{2,1,0:T(8,128)S(1)} %get-tuple-element.24), channel_id=1, source_target_pairs={{8,16},{16,8},{24,32},{32,24},{40,48},{48,40},{56,64},{64,56},{72,... | collective-permute-start | bytes 208904 | tf_op jit(solution)/shard_map/ppermute | solution.py:346
  43.8 0.0 copy-start.7
  43.8 10.1 %rest.1.prev_ref = f32[144,8,128]{2,1,0:T(8,128)} custom-call(bf16[800,512]{1,0:T(8,128)(2,1)S(1)} %get-tuple-element.27.tab_ref, f32[104,8,128]{2,1,0:T(8,128)S(1)} %bitcast.9, s32[104,128]{1,0:T(8,128)S(1)} %bitcast.11, f32[144,8,128]{2,1,0:T(8,128)} %get-tuple-element.28.prev_ref), custom_call_target="tpu_custom_call", output_to_operand_aliasing={{}: (3, {})} | custom-call | flops 6710886400 | bytes 4194304 | tf_op jit(solution)/shard_map/rest/pallas_call | solution.py:409
  53.9 0.0 collective-permute-done.6.ye_ref
  54.0 0.0 collective-permute-done.7.yo_ref
  54.0 0.0 collective-permute-done.4.xe_ref
  54.0 0.0 collective-permute-done.5.xo_ref
  54.0 1.9 %arrive.1 = (f32[144,8,128]{2,1,0:T(8,128)}, f32[16,256]{1,0:T(8,128)}) custom-call(s32[2]{0:T(128)S(1)} %pad_add_fusion.par_ref, s32[8,128]{1,0:T(8,128)S(1)} %bitcast.13, f32[17,8,128]{2,1,0:T(8,128)S(1)} %collective-permute-done.4.xe_ref, f32[17,8,128]{2,1,0:T(8,128)S(1)} %collective-permute-done.5.xo_ref, ...), custom_call_target="tpu_custom_call", output_to_operand_aliasing={{0}: (6, {})} | custom-call | tf_op jit(solution)/shard_map/arrive/pallas_call | solution.py:422
  (8 shorter events, 0.0 us)
Async XLA Ops:
  0.7 0.9 %copy-start = (f32[10,16,256]{2,1,0:T(8,128)S(1)}, f32[10,16,256]{2,1,0:T(8,128)}, u32[]{:S(2)}) copy-start(f32[10,16,256]{2,1,0:T(8,128)} %p_ref.3) | copy-start | bytes 491524
  1.6 0.9 %copy-start.1 = (f32[10,16,256]{2,1,0:T(8,128)S(1)}, f32[10,16,256]{2,1,0:T(8,128)}, u32[]{:S(2)}) copy-start(f32[10,16,256]{2,1,0:T(8,128)} %c_ref.3) | copy-start | bytes 491524
  2.6 0.9 %copy-start.2 = (f32[10,16,256]{2,1,0:T(8,128)S(1)}, f32[10,16,256]{2,1,0:T(8,128)}, u32[]{:S(2)}) copy-start(f32[10,16,256]{2,1,0:T(8,128)} %s_ref.3) | copy-start | bytes 491524
  3.5 0.9 %copy-start.3 = (f32[10,16,256]{2,1,0:T(8,128)S(1)}, f32[10,16,256]{2,1,0:T(8,128)}, u32[]{:S(2)}) copy-start(f32[10,16,256]{2,1,0:T(8,128)} %q_ref.3) | copy-start | bytes 491524
  5.1 5.5 %collective-permute-start = (f32[10,16,256]{2,1,0:T(8,128)S(1)}, f32[10,16,256]{2,1,0:T(8,128)S(1)}, u32[]{:S(2)}, u32[]{:S(2)}) collective-permute-start(f32[10,16,256]{2,1,0:T(8,128)S(1)} %get-tuple-element.17), channel_id=1, source_target_pairs={{0,8},{8,0},{16,24},{24,16},{32,40},{40,32},{48,56},{56,48},{64,72... | collective-permute-start | bytes 491528 | tf_op jit(solution)/shard_map/ppermute | solution.py:346
  5.2 17.4 %copy-start.4 = (f32[1,1,104,8,128]{4,3,2,1,0:T(8,128)S(1)}, f32[1,1,104,8,128]{4,3,2,1,0:T(8,128)}, u32[]{:S(2)}) copy-start(f32[1,1,104,8,128]{4,3,2,1,0:T(8,128)} %param.13) | copy-start | bytes 1277956
  5.2 17.4 %copy-start.5 = (s32[1,1,104,128]{3,2,1,0:T(8,128)S(1)}, s32[1,1,104,128]{3,2,1,0:T(8,128)}, u32[]{:S(2)}) copy-start(s32[1,1,104,128]{3,2,1,0:T(8,128)} %param.15) | copy-start | bytes 159748
  5.2 8.9 %collective-permute-start.1 = (f32[10,16,256]{2,1,0:T(8,128)S(1)}, f32[10,16,256]{2,1,0:T(8,128)S(1)}, u32[]{:S(2)}, u32[]{:S(2)}) collective-permute-start(f32[10,16,256]{2,1,0:T(8,128)S(1)} %get-tuple-element.18), channel_id=1, source_target_pairs={{8,16},{16,8},{24,32},{32,24},{40,48},{48,40},{56,64},{64,56},{72,... | collective-permute-start | bytes 491528 | tf_op jit(solution)/shard_map/ppermute | solution.py:346
  15.1 5.8 %collective-permute-start.2 = (f32[4,8,128]{2,1,0:T(8,128)S(1)}, f32[4,8,128]{2,1,0:T(8,128)S(1)}, u32[]{:S(2)}, u32[]{:S(2)}) collective-permute-start(f32[4,8,128]{2,1,0:T(8,128)S(1)} %get-tuple-element.20), channel_id=1, source_target_pairs={{0,1},{1,0},{2,3},{3,2},{4,5},{5,4},{6,7},{7,6},{8,9},{9,8},{10,11... | collective-permute-start | bytes 49160 | tf_op jit(solution)/shard_map/ppermute | solution.py:346
  15.3 7.3 %collective-permute-start.3 = (f32[4,8,128]{2,1,0:T(8,128)S(1)}, f32[4,8,128]{2,1,0:T(8,128)S(1)}, u32[]{:S(2)}, u32[]{:S(2)}) collective-permute-start(f32[4,8,128]{2,1,0:T(8,128)S(1)} %get-tuple-element.21), channel_id=1, source_target_pairs={{1,2},{2,1},{3,4},{4,3},{5,6},{6,5},{9,10},{10,9},{11,12},{12,11},... | collective-permute-start | bytes 49160 | tf_op jit(solution)/shard_map/ppermute | solution.py:346
  22.6 0.7 %copy-start.6 = (s32[1,1,4,2,128]{4,3,2,1,0:T(2,128)S(1)}, s32[1,1,4,2,128]{4,3,2,1,0:T(2,128)}, u32[]{:S(2)}) copy-start(s32[1,1,4,2,128]{4,3,2,1,0:T(2,128)} %param.16) | copy-start | bytes 12292
  22.6 0.7 %copy-start.8 = (s32[1,1,4]{2,1,0:T(1,128)S(1)}, s32[1,1,4]{2,1,0:T(1,128)}, u32[]{:S(2)}) copy-start(s32[1,1,4]{2,1,0:T(1,128)} %param.14) | copy-start | bytes 52
  34.0 20.0 %collective-permute-start.6 = (f32[5,8,128]{2,1,0:T(8,128)S(1)}, f32[5,8,128]{2,1,0:T(8,128)S(1)}, u32[]{:S(2)}, u32[]{:S(2)}) collective-permute-start(f32[5,8,128]{2,1,0:T(8,128)S(1)} %get-tuple-element.25), channel_id=1, source_target_pairs={{0,1},{1,0},{2,3},{3,2},{4,5},{5,4},{6,7},{7,6},{8,9},{9,8},{10,11... | collective-permute-start | bytes 61448 | tf_op jit(solution)/shard_map/ppermute | solution.py:346
  34.1 19.9 %collective-permute-start.7 = (f32[5,8,128]{2,1,0:T(8,128)S(1)}, f32[5,8,128]{2,1,0:T(8,128)S(1)}, u32[]{:S(2)}, u32[]{:S(2)}) collective-permute-start(f32[5,8,128]{2,1,0:T(8,128)S(1)} %get-tuple-element.26), channel_id=1, source_target_pairs={{1,2},{2,1},{3,4},{4,3},{5,6},{6,5},{9,10},{10,9},{11,12},{12,11},... | collective-permute-start | bytes 61448 | tf_op jit(solution)/shard_map/ppermute | solution.py:346
  40.1 13.8 %collective-permute-start.4 = (f32[17,8,128]{2,1,0:T(8,128)S(1)}, f32[17,8,128]{2,1,0:T(8,128)S(1)}, u32[]{:S(2)}, u32[]{:S(2)}) collective-permute-start(f32[17,8,128]{2,1,0:T(8,128)S(1)} %get-tuple-element.23), channel_id=1, source_target_pairs={{0,8},{8,0},{16,24},{24,16},{32,40},{40,32},{48,56},{56,48},{64,72... | collective-permute-start | bytes 208904 | tf_op jit(solution)/shard_map/ppermute | solution.py:346
  40.2 13.8 %collective-permute-start.5 = (f32[17,8,128]{2,1,0:T(8,128)S(1)}, f32[17,8,128]{2,1,0:T(8,128)S(1)}, u32[]{:S(2)}, u32[]{:S(2)}) collective-permute-start(f32[17,8,128]{2,1,0:T(8,128)S(1)} %get-tuple-element.24), channel_id=1, source_target_pairs={{8,16},{16,8},{24,32},{32,24},{40,48},{48,40},{56,64},{64,56},{72,... | collective-permute-start | bytes 208904 | tf_op jit(solution)/shard_map/ppermute | solution.py:346
  43.8 10.2 %copy-start.7 = (s32[1,1,4,2,128]{4,3,2,1,0:T(2,128)S(1)}, s32[1,1,4,2,128]{4,3,2,1,0:T(2,128)}, u32[]{:S(2)}) copy-start(s32[1,1,4,2,128]{4,3,2,1,0:T(2,128)} %param.17) | copy-start | bytes 12292

commit v2 on v1

--- a/solution.py
+++ b/solution.py
@@ -20,7 +20,8 @@
 SENT = 2 * CAPX + 2 * CAPY
 KEEP = PB - SENT
 OUT = PB + SENT
-GROUP = 8
+GROUP_SENT = 20
+GROUP_KEEP = 16
 
 OMEGA_RELAX = 0.8
 VERTICAL = 4.0
@@ -53,39 +54,58 @@
     return pltpu.roll(x, shift % x.shape[axis], axis)
 
 
-def edge_rows_kernel(par_ref, p_ref, c_ref, s_ref, q_ref, even_ref, odd_ref):
-    parity = par_ref[0]
+def parities():
+    return lax.rem(lax.axis_index("gx"), 2), lax.rem(lax.axis_index("gy"), 2)
+
+
+def edge_rows_kernel(p_hbm, c_hbm, s_hbm, q_hbm, even_hbm, odd_hbm, p_ref, c_ref, s_ref, q_ref, even_ref, odd_ref, sems):
+    halves = (slice(0, NZ // 2), slice(NZ // 2, NZ))
+    loads = []
+    for h, part in enumerate(halves):
+        pairs = ((p_hbm, p_ref), (c_hbm, c_ref), (s_hbm, s_ref), (q_hbm, q_ref))
+        loads.append([pltpu.make_async_copy(a.at[part], b.at[part], sems.at[h, n]) for n, (a, b) in enumerate(pairs)])
+        for copy in loads[h]:
+            copy.start()
+    parity = parities()[0]
     row = index_of((1, 8, CY), 1)
-    pieces = []
-    for start, step, outer in ((0, -1, 3), (8, 1, 4)):
-        tile = slice(start, start + 8)
-        p, c, s, q = (ref[:, tile, :] for ref in (p_ref, c_ref, s_ref, q_ref))
-        weight = jnp.where(row == outer, harmonic(c, roll(c, step, 1)), 0.0)
-        rhs = s * p + q + weight * roll(p, step, 1)
-        side = slice(0, 4) if start == 0 else slice(4, 8)
-        pieces.append(jnp.concatenate([p[:, side], c[:, side], (s + weight)[:, side], rhs[:, side]], axis=1))
-    west, east = pieces
-    even_ref[...] = jnp.where(parity == 0, east, west)
-    odd_ref[...] = jnp.where(parity == 0, west, east)
-
-
-def edge_lanes_kernel(par_ref, p_ref, c_ref, s_ref, q_ref, re_ref, ro_ref, ext_ref, even_ref, odd_ref):
-    par_x = par_ref[0]
-    par_y = par_ref[1]
-    own = [p_ref[...], c_ref[...], s_ref[...], s_ref[...] * p_ref[...] + q_ref[...]]
-    from_even = re_ref[...]
-    from_odd = ro_ref[...]
+    stores = []
+    for h, part in enumerate(halves):
+        for copy in loads[h]:
+            copy.wait()
+        pieces = []
+        for start, step, outer in ((0, -1, 3), (8, 1, 4)):
+            tile = slice(start, start + 8)
+            p, c, s, q = (ref[part, tile, :] for ref in (p_ref, c_ref, s_ref, q_ref))
+            weight = jnp.where(row == outer, harmonic(c, roll(c, step, 1)), 0.0)
+            rhs = s * p + q + weight * roll(p, step, 1)
+            side = slice(0, 4) if start == 0 else slice(4, 8)
+            pieces.append(jnp.concatenate([p[:, side], c[:, side], (s + weight)[:, side], rhs[:, side]], axis=1))
+        west, east = pieces
+        even_ref[part] = jnp.where(parity == 0, east, west)
+        odd_ref[part] = jnp.where(parity == 0, west, east)
+        for n, (a, b) in enumerate(((even_ref, even_hbm), (odd_ref, odd_hbm))):
+            copy = pltpu.make_async_copy(a.at[part], b.at[part], sems.at[h, 4 + n])
+            copy.start()
+            stores.append(copy)
+    for copy in stores:
+        copy.wait()
+
+
+def beside_rows(from_even, from_odd, par_x):
     east = jnp.where(par_x == 0, from_even, from_odd)
     west = jnp.where(par_x == 0, from_odd, from_even)
-    for f in range(4):
-        ext_ref[f, :, 0:CX, :] = own[f]
-        ext_ref[f, :, CX:ROWS, :] = jnp.concatenate(
-            [east[:, 4 * f : 4 * f + 4], west[:, 4 * f : 4 * f + 4]], axis=1
-        )
+    return [jnp.concatenate([east[:, 4 * f : 4 * f + 4], west[:, 4 * f : 4 * f + 4]], axis=1) for f in range(4)]
+
+
+def edge_lanes_kernel(p_ref, c_ref, s_ref, q_ref, re_ref, ro_ref, links_ref, cross_ref, even_ref, odd_ref):
+    par_x, par_y = parities()
     lane = index_of((1, 1, 128), 2)
     packed = []
     for start, step, outer, low in ((0, -1, 3, 0), (128, 1, 124, 124)):
-        p, c, s, r = (ext_ref[f, :, :, start : start + 128] for f in range(4))
+        at = slice(start, start + 128)
+        near = beside_rows(re_ref[:, :, at], ro_ref[:, :, at], par_x)
+        p, c, s, q = (ref[:, :, at] for ref in (p_ref, c_ref, s_ref, q_ref))
+        p, c, s, r = (jnp.concatenate(pair, axis=1) for pair in zip((p, c, s, s * p + q), near))
         weight = jnp.where(lane == outer, harmonic(c, roll(c, step, 2)), 0.0)
         fields = [p, c, s + weight, r + weight * roll(p, step, 2)]
         inside = (lane >= low) & (lane < low + 4)
@@ -102,8 +122,9 @@
         odd_ref[j] = jnp.where(par_y == 0, south[j], north[j])
 
 
-def one_hot(values, size, lanes):
-    return jnp.where(index_of((size, lanes), 0) == values, 1.0, 0.0).astype(BF16)
+def one_hot(values, lanes):
+    hit = index_of((CY, lanes), 0).astype(BF16) == values.astype(BF16)
+    return jnp.where(hit, jnp.ones((), BF16), jnp.zeros((), BF16))
 
 
 def split(x, parts):
@@ -117,30 +138,36 @@
 
 def sample(tab_ref, cells, found_ref):
     lanes = cells.shape[1]
-    hot = one_hot(cells & (CY - 1), CY, lanes)
+    hot = one_hot(cells & (CY - 1), lanes)
     found_ref[...] = jnp.dot(tab_ref[...], jnp.concatenate([hot, hot], 0), preferred_element_type=F32)
     high = cells >> 8
     column = high & (CX - 1)
     west_row = jnp.where(column == 0, NZ * CX + (high >> 4), high - 1)
-    row = index_of((8, lanes), 0)
-    here = high - row
-    beside = west_row - row
+    here = jnp.broadcast_to(high >> 3, (8, lanes))
+    beside = jnp.broadcast_to(west_row >> 3, (8, lanes))
     west = east = north = south = top = bottom = satur = jnp.zeros((8, lanes), F32)
     for g in range(22):
         at = 8 * g
         face = found_ref[at : at + 8, :]
-        west = west + jnp.where(beside == at, face, 0.0)
+        west = jnp.where(beside == g, face, west)
         if g < 20:
-            mask = here == at
-            east = east + jnp.where(mask, face, 0.0)
-            north = north + jnp.where(mask, found_ref[NORTH + at : NORTH + at + 8, :], 0.0)
-            south = south + jnp.where(mask, found_ref[SOUTH + at : SOUTH + at + 8, :], 0.0)
-            satur = satur + jnp.where(mask, found_ref[SATUR + at : SATUR + at + 8, :], 0.0)
+            mask = here == g
+            east = jnp.where(mask, face, east)
+            north = jnp.where(mask, found_ref[NORTH + at : NORTH + at + 8, :], north)
+            south = jnp.where(mask, found_ref[SOUTH + at : SOUTH + at + 8, :], south)
+            satur = jnp.where(mask, found_ref[SATUR + at : SATUR + at + 8, :], satur)
             if g < 18:
-                top = top + jnp.where(mask, found_ref[LEVEL + at : LEVEL + at + 8, :], 0.0)
+                top = jnp.where(mask, found_ref[LEVEL + at : LEVEL + at + 8, :], top)
             if g >= 2:
-                bottom = bottom + jnp.where(mask, found_ref[LEVEL + at - 16 : LEVEL + at - 8, :], 0.0)
-    return [jnp.sum(v, axis=0, keepdims=True) for v in (west, east, south, north, bottom, top, satur)]
+                bottom = jnp.where(mask, found_ref[LEVEL + at - 16 : LEVEL + at - 8, :], bottom)
+    row = index_of((8, lanes), 0)
+    own = row == (high & 7)
+    other = row == (west_row & 7)
+
+    def pick(mask, rows):
+        return jnp.sum(jnp.where(mask, rows, 0.0), axis=0, keepdims=True)
+
+    return [pick(other, west)] + [pick(own, v) for v in (east, south, north, bottom, top, satur)]
 
 
 def advance(record, sampled):
@@ -159,36 +186,38 @@
     return jnp.where(row == 4, decayed, jnp.where(row == 5, satur, record + step))
 
 
-def advance_group(tab_ref, cell_ref, rec_ref, found_ref, first, store):
-    cells = jnp.concatenate([cell_ref[pl.ds(first + j, 1), :] for j in range(GROUP)], axis=1)
+def advance_group(tab_ref, cell_ref, rec_ref, found_ref, first, size, store):
+    cells = jnp.concatenate([cell_ref[pl.ds(first + j, 1), :] for j in range(size)], axis=1)
     sampled = sample(tab_ref, cells, found_ref)
-    for j in range(GROUP):
+    for j in range(size):
         mine = [v[:, 128 * j : 128 * j + 128] for v in sampled]
         store(first + j, advance(rec_ref[first + j], mine))
 
 
 def sweep_kernel(
-    par_ref, cross_ref, ext_ref, re_ref, ro_ref, rec_ref, cell_ref, source_ref,
+    cross_ref, p_ref, c_ref, s_ref, q_ref, rxe_ref, rxo_ref, rye_ref, ryo_ref, rec_ref, cell_ref, source_ref,
     head_ref, tab_ref, next_ref, xe_ref, xo_ref, ye_ref, yo_ref,
-    h0, h1, cond, rhs, inv, wx, wy, wz, flat, found, kept, sent, sem,
+    h0, h1, cond, rhs, inv, wx, wy, wz, flat, found, kept, sent, final, sems,
 ):
-    par_x = par_ref[0]
-    par_y = par_ref[1]
+    par_x, par_y = parities()
     lane = index_of((1, 128), 1)
     fields = (h0, cond, inv, rhs)
-    north = [jnp.where(par_y == 0, re_ref[j], ro_ref[j]) for j in range(4)]
-    south = [jnp.where(par_y == 0, ro_ref[j], re_ref[j]) for j in range(4)]
+    near = beside_rows(rxe_ref[...], rxo_ref[...], par_x)
+    h0[:, 0:CX, 0:CY] = p_ref[...]
+    cond[:, 0:CX, 0:CY] = c_ref[...]
+    inv[:, 0:CX, 0:CY] = s_ref[...]
+    rhs[:, 0:CX, 0:CY] = s_ref[...] * p_ref[...] + q_ref[...]
+    north = [jnp.where(par_y == 0, rye_ref[j], ryo_ref[j]) for j in range(4)]
+    south = [jnp.where(par_y == 0, ryo_ref[j], rye_ref[j]) for j in range(4)]
     for f in range(4):
-        for k in range(NZ):
-            fields[f][k, :, 0:CY] = ext_ref[f, k]
-            for t in range(3):
-                i = 3 * k + t
-                slot = 8 * f + i % 8
-                up = roll(north[i // 8], -4 * slot, 1)
-                down = roll(south[i // 8], 124 - 4 * slot, 1)
-                fields[f][k, 8 * t : 8 * t + 8, CY:LANES] = jnp.where(
-                    lane < 4, up, jnp.where(lane >= 124, down, 0.0)
-                )
+        fields[f][:, CX:ROWS, 0:CY] = near[f]
+        for i in range(30):
+            slot = 8 * f + i % 8
+            up = roll(north[i // 8], -4 * slot, 1)
+            down = roll(south[i // 8], 124 - 4 * slot, 1)
+            fields[f][i // 3, 8 * (i % 3) : 8 * (i % 3) + 8, CY:LANES] = jnp.where(
+                lane < 4, up, jnp.where(lane >= 124, down, 0.0)
+            )
     row = index_of((ROWS, 1), 0)
     for k in range(NZ):
         c = cond[k]
@@ -225,7 +254,7 @@
         face_x = -wx[k] * (roll(h, -1, 0) - h)
         face_y = -wy[k] * (roll(h, -1, 1) - h)
         mine = h[0:CX, 0:CY]
-        head_ref[k] = mine
+        final[k] = mine
         flat[EAST + CX * k : EAST + CX * k + CX, :] = face_x[0:CX, 0:CY]
         flat[NZ * CX + k : NZ * CX + k + 1, :] = face_x[ROWS - 1 : ROWS, 0:CY]
         flat[NORTH + CX * k : NORTH + CX * k + CX, :] = face_y[0:CX, 0:CY]
@@ -237,6 +266,8 @@
         flat[SATUR + CX * k : SATUR + CX * k + CX, :] = RESIDUAL_SAT + (1.0 - RESIDUAL_SAT) * lax.rsqrt(
             1.0 + suction * suction
         )
+    head_copy = pltpu.make_async_copy(final, head_ref, sems.at[0])
+    head_copy.start()
     coarse, fine = split(flat[...], 2)
     tab_ref[:, 0:CY] = coarse
     tab_ref[:, CY : 2 * CY] = fine
@@ -249,15 +280,15 @@
         sent[slot] = jnp.where(live, record, 0.0)
 
     def group_step(i, carry):
-        advance_group(tab_ref, cell_ref, rec_ref, found, i * GROUP, store)
+        advance_group(tab_ref, cell_ref, rec_ref, found, i * GROUP_SENT, GROUP_SENT, store)
         return carry
 
-    lax.fori_loop(0, SENT // GROUP, group_step, 0)
-    copy = pltpu.make_async_copy(kept, next_ref.at[pl.ds(0, SENT)], sem)
+    lax.fori_loop(0, SENT // GROUP_SENT, group_step, 0)
+    copy = pltpu.make_async_copy(kept, next_ref.at[pl.ds(0, SENT)], sems.at[1])
     copy.start()
     links = jnp.concatenate([source_ref[j : j + 1, :] for j in range(8)], axis=1)
     surface = jnp.concatenate(split(old[NZ - 1, 0:CX, 0:CY], 3), axis=0)
-    at_links = jnp.dot(surface, one_hot(links & (CY - 1), CY, 1024), preferred_element_type=F32)
+    at_links = jnp.dot(surface, one_hot(links & (CY - 1), 1024), preferred_element_type=F32)
     at_links = at_links[0:CX] + at_links[CX : 2 * CX] + at_links[2 * CX : 3 * CX]
     picked = jnp.where(index_of((CX, 1024), 0) == (links >> 8), at_links, 0.0)
     value = jnp.sum(picked, axis=0, keepdims=True)
@@ -276,6 +307,7 @@
         ref[0:cap] = sent[pl.ds(base + par * cap, cap)]
         ref[cap] = jnp.where(par == 0, flows[low], flows[low + 1])
     copy.wait()
+    head_copy.wait()
 
 
 def rest_kernel(tab_ref, rec_ref, cell_ref, prev_ref, next_ref, found, kept, sem):
@@ -283,18 +315,17 @@
         kept[slot - SENT] = record
 
     def group_step(i, carry):
-        advance_group(tab_ref, cell_ref, rec_ref, found, SENT + i * GROUP, store)
+        advance_group(tab_ref, cell_ref, rec_ref, found, SENT + i * GROUP_KEEP, GROUP_KEEP, store)
         return carry
 
-    lax.fori_loop(0, KEEP // GROUP, group_step, 0)
+    lax.fori_loop(0, KEEP // GROUP_KEEP, group_step, 0)
     copy = pltpu.make_async_copy(kept, next_ref.at[pl.ds(SENT, KEEP)], sem)
     copy.start()
     copy.wait()
 
 
-def arrive_kernel(par_ref, target_ref, xe_ref, xo_ref, ye_ref, yo_ref, prev_ref, next_ref, inflow_ref, sems):
-    par_x = par_ref[0]
-    par_y = par_ref[1]
+def arrive_kernel(target_ref, xe_ref, xo_ref, ye_ref, yo_ref, prev_ref, next_ref, inflow_ref, sems):
+    par_x, par_y = parities()
     copies = []
     for n, (ref, par, base, cap) in enumerate(
         (
@@ -321,7 +352,7 @@
     links = jnp.concatenate([target_ref[j : j + 1, :] for j in range(8)], axis=1)
     spread = jnp.where(index_of((CX, 1024), 0) == (links >> 8), flow, 0.0)
     parts = jnp.concatenate(split(spread, 3), axis=0)
-    hot = one_hot(links & (CY - 1), CY, 1024)
+    hot = one_hot(links & (CY - 1), 1024)
     total = lax.dot_general(parts, hot, (((1,), (1,)), ((), ())), preferred_element_type=F32)
     inflow_ref[...] = total[0:CX] + total[CX : 2 * CX] + total[2 * CX : 3 * CX]
     for copy in copies:
@@ -343,7 +374,9 @@
 
 def exchange(even, odd, axis):
     size = lax.axis_size(axis)
-    return lax.ppermute(even, axis, swap(size, 0)), lax.ppermute(odd, axis, swap(size, 1))
+    from_odd = lax.ppermute(odd, axis, swap(size, 1))
+    from_even = lax.ppermute(even, axis, swap(size, 0))
+    return from_even, from_odd
 
 
 def shape(*dims, dtype=F32):
@@ -353,30 +386,31 @@
 def body(
     pressure, conductivity, storage, source, particles, crossing, particle_cell, river_source, river_target
 ):
-    parity = jnp.stack([lax.axis_index("gx") % 2, lax.axis_index("gy") % 2]).astype(jnp.int32)
+    links = river_source.reshape(8, 128)
     grid = (pressure, conductivity, storage, source)
+    tile = pltpu.VMEM((NZ, CX, CY), F32)
     x_even, x_odd = pl.pallas_call(
         edge_rows_kernel,
-        out_shape=(shape(NZ, 16, CY), shape(NZ, 16, CY)),
-        in_specs=[SMEM] + [VMEM] * 4,
+        out_shape=(shape(NZ, CX, CY), shape(NZ, CX, CY)),
+        in_specs=[ANY] * 4,
+        out_specs=(ANY, ANY),
+        scratch_shapes=[tile] * 6 + [pltpu.SemaphoreType.DMA((2, 6))],
+        compiler_params=pltpu.CompilerParams(vmem_limit_bytes=60 << 20),
+        name="edge_rows",
+    )(*grid)
+    halo_x = exchange(x_even, x_odd, "gx")
+    y_even, y_odd = pl.pallas_call(
+        edge_lanes_kernel,
+        out_shape=(shape(4, 8, 128), shape(4, 8, 128)),
+        in_specs=[VMEM] * 7 + [SMEM],
         out_specs=(VMEM, VMEM),
         compiler_params=LIMIT,
-        name="edge_rows",
-    )(parity, *grid)
-    x_even, x_odd = exchange(x_even, x_odd, "gx")
-    extended, y_even, y_odd = pl.pallas_call(
-        edge_lanes_kernel,
-        out_shape=(shape(4, NZ, ROWS, CY), shape(4, 8, 128), shape(4, 8, 128)),
-        in_specs=[SMEM] + [VMEM] * 6,
-        out_specs=(VMEM,) * 3,
-        compiler_params=LIMIT,
         name="edge_lanes",
-    )(parity, *grid, x_even, x_odd)
-    y_even, y_odd = exchange(y_even, y_odd, "gy")
+    )(*grid, *halo_x, links, crossing[0, 0])
+    halo_y = exchange(y_even, y_odd, "gy")
     records = particles[0, 0]
     cells = particle_cell[0, 0]
     field = pltpu.VMEM((NZ, ROWS, LANES), F32)
-    found = pltpu.VMEM((TABLE, 128 * GROUP), F32)
     head, table, moved, x_even, x_odd, y_even, y_odd = pl.pallas_call(
         sweep_kernel,
         out_shape=(
@@ -388,22 +422,20 @@
             shape(CAPY + 1, 8, 128),
             shape(CAPY + 1, 8, 128),
         ),
-        in_specs=[SMEM, SMEM] + [VMEM] * 6,
-        out_specs=(VMEM, VMEM, ANY) + (VMEM,) * 4,
+        in_specs=[SMEM] + [VMEM] * 11,
+        out_specs=(ANY, VMEM, ANY) + (VMEM,) * 4,
         scratch_shapes=[field] * 8
         + [
             pltpu.VMEM((TABLE, CY), F32),
-            found,
+            pltpu.VMEM((TABLE, 128 * GROUP_SENT), F32),
             pltpu.VMEM((SENT, 8, 128), F32),
             pltpu.VMEM((SENT, 8, 128), F32),
-            pltpu.SemaphoreType.DMA,
+            tile,
+            pltpu.SemaphoreType.DMA((2,)),
         ],
         compiler_params=LIMIT,
         name="sweep",
-    )(
-        parity, crossing[0, 0], extended, y_even, y_odd, records, cells,
-        river_source.reshape(8, 128),
-    )
+    )(crossing[0, 0], *grid, *halo_x, *halo_y, records, cells, links)
     x_even, x_odd = exchange(x_even, x_odd, "gx")
     y_even, y_odd = exchange(y_even, y_odd, "gy")
     moved = pl.pallas_call(
@@ -411,7 +443,7 @@
         out_shape=shape(OUT, 8, 128),
         in_specs=[VMEM] * 3 + [ANY],
         out_specs=ANY,
-        scratch_shapes=[found, pltpu.VMEM((KEEP, 8, 128), F32), pltpu.SemaphoreType.DMA],
+        scratch_shapes=[pltpu.VMEM((TABLE, 128 * GROUP_KEEP), F32), pltpu.VMEM((KEEP, 8, 128), F32), pltpu.SemaphoreType.DMA],
         input_output_aliases={3: 0},
         compiler_params=LIMIT,
         cost_estimate=pl.CostEstimate(
@@ -422,13 +454,13 @@
     moved, inflow = pl.pallas_call(
         arrive_kernel,
         out_shape=(shape(OUT, 8, 128), shape(CX, CY)),
-        in_specs=[SMEM] + [VMEM] * 5 + [ANY],
+        in_specs=[VMEM] * 5 + [ANY],
         out_specs=(ANY, VMEM),
         scratch_shapes=[pltpu.SemaphoreType.DMA((4,))],
-        input_output_aliases={6: 0},
+        input_output_aliases={5: 0},
         compiler_params=LIMIT,
         name="arrive",
-    )(parity, river_target.reshape(8, 128), x_even, x_odd, y_even, y_odd, moved)
+    )(river_target.reshape(8, 128), x_even, x_odd, y_even, y_odd, moved)
     return head, moved[None, None], inflow
 
 

time: 56.2 us -> 49.7 us (0.88)
  local copies, waits for them, and re-layouts: 4.36 us -> 0.66 us
  Pallas kernels: 24.3 us -> 21.6 us
    unnamed x18, local copies, waits for them, and re-layouts: 4.36 us -> 0.66 us
    pallas_call x1, Pallas kernels: 10.7 us -> 8.86 us  [body(): pl.pallas_call(sweep_kernel, out_shape=(shape(NZ, CX, CY), shape(TABLE, 2...]
    pallas_call x1, Pallas kernels: 10.1 us -> 8.38 us  [body(): pl.pallas_call(rest_kernel, out_shape=shape(OUT, 8, 128), in_specs=[VMEM]...]
    pallas_call x2, Pallas kernels: 1.66 us -> 3.04 us  [the longest x1 2.05 us: body(): pl.pallas_call(edge_rows_kernel, out_shape=(shape(NZ, CX, CY), shape(NZ,...]
  transfers between devices with their start and end apart: 8 -> 8, of which waited for: 2 -> 2; matrix products, arithmetic and copies ran while one was open for 0% -> 0% of each run, Pallas kernels for 18% -> 17%
where the time goes in v2:
time: 49.7 us; the launch traced here: 49.5 us
  Pallas kernels  21.6 us (43%)
  starting transfers between devices  21 us (42%)
  waiting for transfers between devices  5.37 us (11%)
  between operations  0.84 us (2%)
  local copies, waits for them, and re-layouts  0.66 us (1%)
    ppermute x4, starting transfers between devices, exchange(): from_odd = lax.ppermute(odd, axis, swap(size, 1))  20.5 us
    pallas_call x1, Pallas kernels, body(): pl.pallas_call(sweep_kernel, out_shape=(shape(NZ, CX, CY), shape(TABLE, 2...  8.86 us
    pallas_call x1, Pallas kernels, body(): pl.pallas_call(rest_kernel, out_shape=shape(OUT, 8, 128), in_specs=[VMEM]...  8.38 us
    ppermute x4, waiting for transfers between devices, exchange(): from_odd = lax.ppermute(odd, axis, swap(size, 1))  5.36 us
    pallas_call x1, Pallas kernels, body(): pl.pallas_call(edge_rows_kernel, out_shape=(shape(NZ, CX, CY), shape(NZ,...  2.05 us
    pallas_call x1, Pallas kernels, body(): pl.pallas_call(arrive_kernel, out_shape=(shape(OUT, 8, 128), shape(CX, CY...  1.34 us
  transfers between devices with their start and end apart: 8, of which 2 were waited for; matrix products, arithmetic and copies ran while one was open for 0% of the time, Pallas kernels for 17%

profile of v2, /device:TPU:38, one launch (start us, length us, event | category | flops | bytes accessed | tf_op | source)
XLA Modules:
  0.0 49.5 jit_solution(17448771919433121994)
XLA Ops:
  0.6 0.0 copy-start.3
  0.6 0.0 copy-start.2
  0.7 0.0 copy-start.1
  0.7 0.0 copy-start
  0.7 2.1 %edge_rows.1 = (f32[10,16,256]{2,1,0:T(8,128)}, f32[10,16,256]{2,1,0:T(8,128)}) custom-call(f32[10,16,256]{2,1,0:T(8,128)} %p_ref.3, f32[10,16,256]{2,1,0:T(8,128)} %c_ref.3, f32[10,16,256]{2,1,0:T(8,128)} %s_ref.3, f32[10,16,256]{2,1,0:T(8,128)} %q_ref.3), custom_call_target="tpu_custom_call" | custom-call | tf_op jit(solution)/shard_map/edge_rows/pallas_call | solution.py:392
  2.7 0.0 copy-start.6
  2.7 0.1 collective-permute-start
  2.8 5.3 %collective-permute-start.1 = (f32[10,16,256]{2,1,0:T(8,128)}, f32[10,16,256]{2,1,0:T(8,128)S(1)}, u32[]{:S(2)}, u32[]{:S(2)}) collective-permute-start(f32[10,16,256]{2,1,0:T(8,128)} %get-tuple-element.17), channel_id=1, source_target_pairs={{8,16},{16,8},{24,32},{32,24},{40,48},{48,40},{56,64},{64,56},{72,... | collective-permute-start | bytes 491528 | tf_op jit(solution)/shard_map/ppermute | solution.py:377
  8.1 0.0 collective-permute-done.re_ref.rxe_ref
  8.1 3.7 %collective-permute-done.1.ro_ref.rxo_ref = f32[10,16,256]{2,1,0:T(8,128)S(1)} collective-permute-done((f32[10,16,256]{2,1,0:T(8,128)}, f32[10,16,256]{2,1,0:T(8,128)S(1)}, u32[]{:S(2)}, u32[]{:S(2)}) %collective-permute-start.1) | collective-permute-done | bytes 163872 | tf_op jit(solution)/shard_map/ppermute | solution.py:377
  11.8 0.0 copy-done.3
  11.8 0.0 copy-done.2
  11.8 0.0 copy-done
  11.8 0.0 copy-done.6
  11.8 0.6 %copy-done.8 = s32[1,1,4]{2,1,0:T(1,128)S(1)} copy-done((s32[1,1,4]{2,1,0:T(1,128)S(1)}, s32[1,1,4]{2,1,0:T(1,128)}, u32[]{:S(2)}) %copy-start.8) | copy-done | bytes 40
  12.5 1.0 %edge_lanes.1 = (f32[4,8,128]{2,1,0:T(8,128)S(1)}, f32[4,8,128]{2,1,0:T(8,128)S(1)}) custom-call(f32[10,16,256]{2,1,0:T(8,128)S(1)} %copy-done, f32[10,16,256]{2,1,0:T(8,128)S(1)} %copy-done.1, f32[10,16,256]{2,1,0:T(8,128)S(1)} %copy-done.2, f32[10,16,256]{2,1,0:T(8,128)S(1)} %copy-done.3, f32[10,16,256]{2,1,0:T(8,128)S(1)} %collective-permute-done.re_ref.rxe_ref, ...), custom_call_target="tpu_custom_call" | custom-call | tf_op jit(solution)/shard_map/edge_lanes/pallas_call | solution.py:402
  13.5 0.2 collective-permute-start.2
  13.6 5.6 %collective-permute-start.3 = (f32[4,8,128]{2,1,0:T(8,128)S(1)}, f32[4,8,128]{2,1,0:T(8,128)S(1)}, u32[]{:S(2)}, u32[]{:S(2)}) collective-permute-start(f32[4,8,128]{2,1,0:T(8,128)S(1)} %get-tuple-element.19), channel_id=1, source_target_pairs={{1,2},{2,1},{3,4},{4,3},{5,6},{6,5},{9,10},{10,9},{11,12},{12,11},... | collective-permute-start | bytes 49160 | tf_op jit(solution)/shard_map/ppermute | solution.py:377
  19.3 0.0 collective-permute-done.2.rye_ref
  19.3 1.7 %collective-permute-done.3.ryo_ref = f32[4,8,128]{2,1,0:T(8,128)S(1)} collective-permute-done((f32[4,8,128]{2,1,0:T(8,128)S(1)}, f32[4,8,128]{2,1,0:T(8,128)S(1)}, u32[]{:S(2)}, u32[]{:S(2)}) %collective-permute-start.3) | collective-permute-done | bytes 16416 | tf_op jit(solution)/shard_map/ppermute | solution.py:377
  21.0 8.9 %sweep.1 = (f32[10,16,256]{2,1,0:T(8,128)}, bf16[800,512]{1,0:T(8,128)(2,1)S(1)}, f32[144,8,128]{2,1,0:T(8,128)}, f32[17,8,128]{2,1,0:T(8,128)S(1)}, f32[17,8,12...) custom-call(s32[4]{0:T(128)S(1)} %bitcast.14, f32[10,16,256]{2,1,0:T(8,128)S(1)} %copy-done, ...), custom_call_target="tpu_custom_call" | custom-call | tf_op jit(solution)/shard_map/sweep/pallas_call | solution.py:414
  29.9 0.1 collective-permute-start.6
  30.0 6.0 %collective-permute-start.7 = (f32[5,8,128]{2,1,0:T(8,128)S(1)}, f32[5,8,128]{2,1,0:T(8,128)S(1)}, u32[]{:S(2)}, u32[]{:S(2)}) collective-permute-start(f32[5,8,128]{2,1,0:T(8,128)S(1)} %get-tuple-element.24), channel_id=1, source_target_pairs={{1,2},{2,1},{3,4},{4,3},{5,6},{6,5},{9,10},{10,9},{11,12},{12,11},... | collective-permute-start | bytes 61448 | tf_op jit(solution)/shard_map/ppermute | solution.py:377
  36.0 0.1 collective-permute-start.4
  36.1 3.6 %collective-permute-start.5 = (f32[17,8,128]{2,1,0:T(8,128)S(1)}, f32[17,8,128]{2,1,0:T(8,128)S(1)}, u32[]{:S(2)}, u32[]{:S(2)}) collective-permute-start(f32[17,8,128]{2,1,0:T(8,128)S(1)} %get-tuple-element.22), channel_id=1, source_target_pairs={{8,16},{16,8},{24,32},{32,24},{40,48},{48,40},{56,64},{64,56},{72,... | collective-permute-start | bytes 208904 | tf_op jit(solution)/shard_map/ppermute | solution.py:377
  39.7 0.0 copy-start.7
  39.7 8.4 %rest.1.prev_ref = f32[144,8,128]{2,1,0:T(8,128)} custom-call(bf16[800,512]{1,0:T(8,128)(2,1)S(1)} %get-tuple-element.25.tab_ref, f32[104,8,128]{2,1,0:T(8,128)S(1)} %bitcast.7, s32[104,128]{1,0:T(8,128)S(1)} %bitcast.9, f32[144,8,128]{2,1,0:T(8,128)} %get-tuple-element.26.prev_ref), custom_call_target="tpu_custom_call", output_to_operand_aliasing={{}: (3, {})} | custom-call | flops 6710886400 | bytes 4194304 | tf_op jit(solution)/shard_map/rest/pallas_call | solution.py:441
  48.1 0.0 collective-permute-done.6.ye_ref
  48.1 0.0 collective-permute-done.7.yo_ref
  48.1 0.0 collective-permute-done.4.xe_ref
  48.1 0.0 collective-permute-done.5.xo_ref
  48.1 1.3 %arrive.1 = (f32[144,8,128]{2,1,0:T(8,128)}, f32[16,256]{1,0:T(8,128)}) custom-call(s32[8,128]{1,0:T(8,128)S(1)} %bitcast.12, f32[17,8,128]{2,1,0:T(8,128)S(1)} %collective-permute-done.4.xe_ref, f32[17,8,128]{2,1,0:T(8,128)S(1)} %collective-permute-done.5.xo_ref, f32[5,8,128]{2,1,0:T(8,128)S(1)} %collective-permute-done.6.ye_ref, ...), custom_call_target="tpu_custom_call", output_to_operand_aliasing={{0}: (5, {})} | custom-call | tf_op jit(solution)/shard_map/arrive/pallas_call | solution.py:454
  (7 shorter events, 0.0 us)
Async XLA Ops:
  0.6 11.2 %copy-start.3 = (f32[10,16,256]{2,1,0:T(8,128)S(1)}, f32[10,16,256]{2,1,0:T(8,128)}, u32[]{:S(2)}) copy-start(f32[10,16,256]{2,1,0:T(8,128)} %q_ref.3) | copy-start | bytes 491524
  0.6 11.2 %copy-start.2 = (f32[10,16,256]{2,1,0:T(8,128)S(1)}, f32[10,16,256]{2,1,0:T(8,128)}, u32[]{:S(2)}) copy-start(f32[10,16,256]{2,1,0:T(8,128)} %s_ref.3) | copy-start | bytes 491524
  0.7 11.2 %copy-start.1 = (f32[10,16,256]{2,1,0:T(8,128)S(1)}, f32[10,16,256]{2,1,0:T(8,128)}, u32[]{:S(2)}) copy-start(f32[10,16,256]{2,1,0:T(8,128)} %c_ref.3) | copy-start | bytes 491524
  0.7 11.2 %copy-start = (f32[10,16,256]{2,1,0:T(8,128)S(1)}, f32[10,16,256]{2,1,0:T(8,128)}, u32[]{:S(2)}) copy-start(f32[10,16,256]{2,1,0:T(8,128)} %p_ref.3) | copy-start | bytes 491524
  2.7 9.1 %copy-start.6 = (s32[1,1,4,2,128]{4,3,2,1,0:T(2,128)S(1)}, s32[1,1,4,2,128]{4,3,2,1,0:T(2,128)}, u32[]{:S(2)}) copy-start(s32[1,1,4,2,128]{4,3,2,1,0:T(2,128)} %param.16) | copy-start | bytes 12292
  2.7 5.4 %collective-permute-start = (f32[10,16,256]{2,1,0:T(8,128)}, f32[10,16,256]{2,1,0:T(8,128)S(1)}, u32[]{:S(2)}, u32[]{:S(2)}) collective-permute-start(f32[10,16,256]{2,1,0:T(8,128)} %get-tuple-element.16), channel_id=1, source_target_pairs={{0,8},{8,0},{16,24},{24,16},{32,40},{40,32},{48,56},{56,48},{64,72... | collective-permute-start | bytes 491528 | tf_op jit(solution)/shard_map/ppermute | solution.py:378
  2.8 9.0 %collective-permute-start.1 = (f32[10,16,256]{2,1,0:T(8,128)}, f32[10,16,256]{2,1,0:T(8,128)S(1)}, u32[]{:S(2)}, u32[]{:S(2)}) collective-permute-start(f32[10,16,256]{2,1,0:T(8,128)} %get-tuple-element.17), channel_id=1, source_target_pairs={{8,16},{16,8},{24,32},{32,24},{40,48},{48,40},{56,64},{64,56},{72,... | collective-permute-start | bytes 491528 | tf_op jit(solution)/shard_map/ppermute | solution.py:377
  11.8 0.7 %copy-start.8 = (s32[1,1,4]{2,1,0:T(1,128)S(1)}, s32[1,1,4]{2,1,0:T(1,128)}, u32[]{:S(2)}) copy-start(s32[1,1,4]{2,1,0:T(1,128)} %param.14) | copy-start | bytes 52
  12.5 8.5 %copy-start.4 = (f32[1,1,104,8,128]{4,3,2,1,0:T(8,128)S(1)}, f32[1,1,104,8,128]{4,3,2,1,0:T(8,128)}, u32[]{:S(2)}) copy-start(f32[1,1,104,8,128]{4,3,2,1,0:T(8,128)} %param.13) | copy-start | bytes 1277956
  12.5 8.5 %copy-start.5 = (s32[1,1,104,128]{3,2,1,0:T(8,128)S(1)}, s32[1,1,104,128]{3,2,1,0:T(8,128)}, u32[]{:S(2)}) copy-start(s32[1,1,104,128]{3,2,1,0:T(8,128)} %param.15) | copy-start | bytes 159748
  13.5 5.8 %collective-permute-start.2 = (f32[4,8,128]{2,1,0:T(8,128)S(1)}, f32[4,8,128]{2,1,0:T(8,128)S(1)}, u32[]{:S(2)}, u32[]{:S(2)}) collective-permute-start(f32[4,8,128]{2,1,0:T(8,128)S(1)} %get-tuple-element.18), channel_id=1, source_target_pairs={{0,1},{1,0},{2,3},{3,2},{4,5},{5,4},{6,7},{7,6},{8,9},{9,8},{10,11... | collective-permute-start | bytes 49160 | tf_op jit(solution)/shard_map/ppermute | solution.py:378
  13.6 7.3 %collective-permute-start.3 = (f32[4,8,128]{2,1,0:T(8,128)S(1)}, f32[4,8,128]{2,1,0:T(8,128)S(1)}, u32[]{:S(2)}, u32[]{:S(2)}) collective-permute-start(f32[4,8,128]{2,1,0:T(8,128)S(1)} %get-tuple-element.19), channel_id=1, source_target_pairs={{1,2},{2,1},{3,4},{4,3},{5,6},{6,5},{9,10},{10,9},{11,12},{12,11},... | collective-permute-start | bytes 49160 | tf_op jit(solution)/shard_map/ppermute | solution.py:377
  29.9 18.2 %collective-permute-start.6 = (f32[5,8,128]{2,1,0:T(8,128)S(1)}, f32[5,8,128]{2,1,0:T(8,128)S(1)}, u32[]{:S(2)}, u32[]{:S(2)}) collective-permute-start(f32[5,8,128]{2,1,0:T(8,128)S(1)} %get-tuple-element.23), channel_id=1, source_target_pairs={{0,1},{1,0},{2,3},{3,2},{4,5},{5,4},{6,7},{7,6},{8,9},{9,8},{10,11... | collective-permute-start | bytes 61448 | tf_op jit(solution)/shard_map/ppermute | solution.py:378
  30.0 18.1 %collective-permute-start.7 = (f32[5,8,128]{2,1,0:T(8,128)S(1)}, f32[5,8,128]{2,1,0:T(8,128)S(1)}, u32[]{:S(2)}, u32[]{:S(2)}) collective-permute-start(f32[5,8,128]{2,1,0:T(8,128)S(1)} %get-tuple-element.24), channel_id=1, source_target_pairs={{1,2},{2,1},{3,4},{4,3},{5,6},{6,5},{9,10},{10,9},{11,12},{12,11},... | collective-permute-start | bytes 61448 | tf_op jit(solution)/shard_map/ppermute | solution.py:377
  36.0 12.1 %collective-permute-start.4 = (f32[17,8,128]{2,1,0:T(8,128)S(1)}, f32[17,8,128]{2,1,0:T(8,128)S(1)}, u32[]{:S(2)}, u32[]{:S(2)}) collective-permute-start(f32[17,8,128]{2,1,0:T(8,128)S(1)} %get-tuple-element.21), channel_id=1, source_target_pairs={{0,8},{8,0},{16,24},{24,16},{32,40},{40,32},{48,56},{56,48},{64,72... | collective-permute-start | bytes 208904 | tf_op jit(solution)/shard_map/ppermute | solution.py:378
  36.1 12.0 %collective-permute-start.5 = (f32[17,8,128]{2,1,0:T(8,128)S(1)}, f32[17,8,128]{2,1,0:T(8,128)S(1)}, u32[]{:S(2)}, u32[]{:S(2)}) collective-permute-start(f32[17,8,128]{2,1,0:T(8,128)S(1)} %get-tuple-element.22), channel_id=1, source_target_pairs={{8,16},{16,8},{24,32},{32,24},{40,48},{48,40},{56,64},{64,56},{72,... | collective-permute-start | bytes 208904 | tf_op jit(solution)/shard_map/ppermute | solution.py:377
  39.7 8.4 %copy-start.7 = (s32[1,1,4,2,128]{4,3,2,1,0:T(2,128)S(1)}, s32[1,1,4,2,128]{4,3,2,1,0:T(2,128)}, u32[]{:S(2)}) copy-start(s32[1,1,4,2,128]{4,3,2,1,0:T(2,128)} %param.17) | copy-start | bytes 12292

commit v3 on v2

--- a/solution.py
+++ b/solution.py
@@ -31,7 +31,10 @@
 DECAY_RATE = 20.0
 
 ROWS = CX + 8
-LANES = CY + 128
+TALL = 8 + ROWS + 8
+MID = slice(8, 8 + ROWS)
+OWN = slice(12, 12 + CX)
+INNER = slice(4, 4 + CX)
 
 EAST = 0
 NORTH = 176
@@ -97,7 +100,7 @@
     return [jnp.concatenate([east[:, 4 * f : 4 * f + 4], west[:, 4 * f : 4 * f + 4]], axis=1) for f in range(4)]
 
 
-def edge_lanes_kernel(p_ref, c_ref, s_ref, q_ref, re_ref, ro_ref, links_ref, cross_ref, even_ref, odd_ref):
+def edge_lanes_kernel(p_ref, c_ref, s_ref, q_ref, re_ref, ro_ref, even_ref, odd_ref):
     par_x, par_y = parities()
     lane = index_of((1, 1, 128), 2)
     packed = []
@@ -194,88 +197,114 @@
         store(first + j, advance(rec_ref[first + j], mine))
 
 
+def beside_lanes(tiles):
+    lane = index_of(tiles[0].shape, 1)
+    ahead = [roll(t, -1, 1) for t in tiles]
+    back = [roll(t, 1, 1) for t in tiles]
+    after = [jnp.where(lane == 127, ahead[(j + 1) % 3], ahead[j]) for j in range(3)]
+    before = [jnp.where(lane == 0, back[(j + 2) % 3], back[j]) for j in range(3)]
+    return after, before
+
+
 def sweep_kernel(
-    cross_ref, p_ref, c_ref, s_ref, q_ref, rxe_ref, rxo_ref, rye_ref, ryo_ref, rec_ref, cell_ref, source_ref,
+    small_ref, p_ref, c_ref, s_ref, q_ref, rxe_ref, rxo_ref, rye_ref, ryo_ref, rec_ref, cell_ref,
     head_ref, tab_ref, next_ref, xe_ref, xo_ref, ye_ref, yo_ref,
-    h0, h1, cond, rhs, inv, wx, wy, wz, flat, found, kept, sent, final, sems,
+    h0, h1, cond, wx, rhs, inv, wy, wy_back, wz, flat, found, kept, sent, final, live_ref, sems,
 ):
     par_x, par_y = parities()
-    lane = index_of((1, 128), 1)
-    fields = (h0, cond, inv, rhs)
-    near = beside_rows(rxe_ref[...], rxo_ref[...], par_x)
-    h0[:, 0:CX, 0:CY] = p_ref[...]
-    cond[:, 0:CX, 0:CY] = c_ref[...]
-    inv[:, 0:CX, 0:CY] = s_ref[...]
-    rhs[:, 0:CX, 0:CY] = s_ref[...] * p_ref[...] + q_ref[...]
+    edge = jnp.zeros((NZ, 3, 8, 128), F32)
+    for ref in (h0, h1, cond, wx):
+        ref[:, :, 0:8, :] = edge
+        ref[:, :, 8 + ROWS : TALL, :] = edge
+    east = jnp.where(par_x == 0, rxe_ref[...], rxo_ref[...])
+    west = jnp.where(par_x == 0, rxo_ref[...], rxe_ref[...])
     north = [jnp.where(par_y == 0, rye_ref[j], ryo_ref[j]) for j in range(4)]
     south = [jnp.where(par_y == 0, ryo_ref[j], rye_ref[j]) for j in range(4)]
-    for f in range(4):
-        fields[f][:, CX:ROWS, 0:CY] = near[f]
+    lane = index_of((1, 128), 1)
+    for f, (ref, base) in enumerate(((h0, 8), (cond, 8), (inv, 0), (rhs, 0))):
+        for j in range(2):
+            at = slice(128 * j, 128 * j + 128)
+            own = (p_ref, c_ref, s_ref)[f][:, :, at] if f < 3 else s_ref[:, :, at] * p_ref[:, :, at] + q_ref[:, :, at]
+            ref[:, j, base : base + 4, :] = west[:, 4 * f : 4 * f + 4, at]
+            ref[:, j, base + 4 : base + 4 + CX, :] = own
+            ref[:, j, base + 4 + CX : base + ROWS, :] = east[:, 4 * f : 4 * f + 4, at]
         for i in range(30):
+            k, t = divmod(i, 3)
             slot = 8 * f + i % 8
             up = roll(north[i // 8], -4 * slot, 1)
             down = roll(south[i // 8], 124 - 4 * slot, 1)
-            fields[f][i // 3, 8 * (i % 3) : 8 * (i % 3) + 8, CY:LANES] = jnp.where(
-                lane < 4, up, jnp.where(lane >= 124, down, 0.0)
-            )
-    row = index_of((ROWS, 1), 0)
+            rows = jnp.where(lane < 4, up, jnp.where(lane >= 124, down, 0.0))
+            if t < 2:
+                ref[k, 2, base + 4 + 8 * t : base + 12 + 8 * t, :] = rows
+            else:
+                ref[k, 2, base + 4 + CX : base + ROWS, :] = rows[0:4]
+                ref[k, 2, base : base + 4, :] = rows[4:8]
     for k in range(NZ):
-        c = cond[k]
-        w_x = jnp.where(row == CX + 3, 0.0, harmonic(c, roll(c, -1, 0)))
-        w_y = harmonic(c, roll(c, -1, 1))
-        diag = inv[k] + w_x + roll(w_x, 1, 0) + w_y + roll(w_y, 1, 1)
-        if k > 0:
-            diag = diag + wz[k - 1]
-        if k < NZ - 1:
-            w_z = VERTICAL * harmonic(c, cond[k + 1])
-            wz[k] = w_z
-            diag = diag + w_z
-        wx[k] = w_x
-        wy[k] = w_y
-        inv[k] = OMEGA_RELAX / (diag + (diag == 0.0).astype(F32))
+        c = [cond[k, j, MID, :] for j in range(3)]
+        after, _ = beside_lanes(c)
+        w_y = [harmonic(c[j], after[j]) for j in range(3)]
+        _, w_back = beside_lanes(w_y)
+        for j in range(3):
+            wx[k, j, MID, :] = harmonic(c[j], cond[k, j, 9 : 9 + ROWS, :])
+            wy[k, j] = w_y[j]
+            wy_back[k, j] = w_back[j]
+            diag = inv[k, j] + wx[k, j, MID, :] + wx[k, j, 7 : 7 + ROWS, :] + w_y[j] + w_back[j]
+            if k > 0:
+                diag = diag + wz[k - 1, j]
+            if k < NZ - 1:
+                w_z = VERTICAL * harmonic(c[j], cond[k + 1, j, MID, :])
+                wz[k, j] = w_z
+                diag = diag + w_z
+            inv[k, j] = OMEGA_RELAX / (diag + (diag == 0.0).astype(F32))
     old, new = h0, h1
     for _ in range(ITERS):
         for k in range(NZ):
-            h = old[k]
-            w_x = wx[k]
-            w_y = wy[k]
-            total = rhs[k] + w_x * roll(h, -1, 0) + roll(w_x * h, 1, 0)
-            total = total + w_y * roll(h, -1, 1) + roll(w_y * h, 1, 1)
-            if k > 0:
-                total = total + wz[k - 1] * old[k - 1]
-            if k < NZ - 1:
-                total = total + wz[k] * old[k + 1]
-            new[k] = (1.0 - OMEGA_RELAX) * h + inv[k] * total
+            h = [old[k, j, MID, :] for j in range(3)]
+            after, before = beside_lanes(h)
+            for j in range(3):
+                total = rhs[k, j]
+                if k > 0:
+                    total = total + wz[k - 1, j] * old[k - 1, j, MID, :]
+                if k < NZ - 1:
+                    total = total + wz[k, j] * old[k + 1, j, MID, :]
+                along_x = wx[k, j, MID, :] * old[k, j, 9 : 9 + ROWS, :] + wx[k, j, 7 : 7 + ROWS, :] * old[k, j, 7 : 7 + ROWS, :]
+                along_y = wy[k, j] * after[j] + wy_back[k, j] * before[j]
+                new[k, j, MID, :] = (1.0 - OMEGA_RELAX) * h[j] + inv[k, j] * (along_x + along_y + total)
         old, new = new, old
     flat[NZ * CX : NORTH, :] = jnp.zeros((16, CY), F32)
     for k in range(NZ):
-        h = old[k]
+        h = [old[k, j, OWN, :] for j in range(3)]
+        after, before = beside_lanes(h)
         at = slice(CX * k, CX * k + CX)
-        face_x = -wx[k] * (roll(h, -1, 0) - h)
-        face_y = -wy[k] * (roll(h, -1, 1) - h)
-        mine = h[0:CX, 0:CY]
-        final[k] = mine
-        flat[EAST + CX * k : EAST + CX * k + CX, :] = face_x[0:CX, 0:CY]
-        flat[NZ * CX + k : NZ * CX + k + 1, :] = face_x[ROWS - 1 : ROWS, 0:CY]
-        flat[NORTH + CX * k : NORTH + CX * k + CX, :] = face_y[0:CX, 0:CY]
-        flat[SOUTH + CX * k : SOUTH + CX * k + CX, :] = roll(face_y, 1, 1)[0:CX, 0:CY]
-        if k < NZ - 1:
-            face_z = -wz[k, 0:CX, 0:CY] * (old[k + 1, 0:CX, 0:CY] - mine + 1.0)
-            flat[LEVEL + CX * k : LEVEL + CX * k + CX, :] = face_z
-        suction = jnp.maximum(-mine, 0.0)
-        flat[SATUR + CX * k : SATUR + CX * k + CX, :] = RESIDUAL_SAT + (1.0 - RESIDUAL_SAT) * lax.rsqrt(
-            1.0 + suction * suction
-        )
+        for j in range(2):
+            lanes = slice(128 * j, 128 * j + 128)
+
+            def put(first, value):
+                flat[first + CX * k : first + CX * k + CX, lanes] = value
+
+            final[k, :, lanes] = h[j]
+            put(EAST, -wx[k, j, OWN, :] * (old[k, j, 13 : 13 + CX, :] - h[j]))
+            flat[NZ * CX + k : NZ * CX + k + 1, lanes] = -wx[k, j, 11:12, :] * (h[j][0:1] - old[k, j, 11:12, :])
+            put(NORTH, -wy[k, j, INNER, :] * (after[j] - h[j]))
+            put(SOUTH, -wy_back[k, j, INNER, :] * (h[j] - before[j]))
+            if k < NZ - 1:
+                put(LEVEL, -wz[k, j, INNER, :] * (old[k + 1, j, OWN, :] - h[j] + 1.0))
+            suction = jnp.maximum(-h[j], 0.0)
+            put(SATUR, RESIDUAL_SAT + (1.0 - RESIDUAL_SAT) * lax.rsqrt(1.0 + suction * suction))
     head_copy = pltpu.make_async_copy(final, head_ref, sems.at[0])
     head_copy.start()
     coarse, fine = split(flat[...], 2)
     tab_ref[:, 0:CY] = coarse
     tab_ref[:, CY : 2 * CY] = fine
+    counts = small_ref[16:17, :]
+    first = 0
+    for d, cap in enumerate((CAPX, CAPX, CAPY, CAPY)):
+        count = jnp.sum(jnp.where(lane == d, counts, 0), axis=1, keepdims=True)
+        live_ref[first : first + cap, :] = (index_of((cap, 128), 0) < count).astype(F32)
+        first += cap
 
     def store(slot, record):
-        group = jnp.where(slot < CAPX, 0, jnp.where(slot < 2 * CAPX, 1, jnp.where(slot < 2 * CAPX + CAPY, 2, 3)))
-        start = jnp.where(slot < CAPX, 0, jnp.where(slot < 2 * CAPX, CAPX, jnp.where(slot < 2 * CAPX + CAPY, 2 * CAPX, 2 * CAPX + CAPY)))
-        live = slot - start < cross_ref[group]
+        live = live_ref[pl.ds(slot, 1), :] > 0.0
         kept[slot] = jnp.where(live, 0.0, record)
         sent[slot] = jnp.where(live, record, 0.0)
 
@@ -286,8 +315,8 @@
     lax.fori_loop(0, SENT // GROUP_SENT, group_step, 0)
     copy = pltpu.make_async_copy(kept, next_ref.at[pl.ds(0, SENT)], sems.at[1])
     copy.start()
-    links = jnp.concatenate([source_ref[j : j + 1, :] for j in range(8)], axis=1)
-    surface = jnp.concatenate(split(old[NZ - 1, 0:CX, 0:CY], 3), axis=0)
+    links = jnp.concatenate([small_ref[j : j + 1, :] for j in range(8)], axis=1)
+    surface = jnp.concatenate(split(final[NZ - 1], 3), axis=0)
     at_links = jnp.dot(surface, one_hot(links & (CY - 1), 1024), preferred_element_type=F32)
     at_links = at_links[0:CX] + at_links[CX : 2 * CX] + at_links[2 * CX : 3 * CX]
     picked = jnp.where(index_of((CX, 1024), 0) == (links >> 8), at_links, 0.0)
@@ -310,21 +339,27 @@
     head_copy.wait()
 
 
-def rest_kernel(tab_ref, rec_ref, cell_ref, prev_ref, next_ref, found, kept, sem):
+def rest_kernel(tab_ref, rec_ref, cell_ref, prev_ref, next_ref, found, kept, sems):
     def store(slot, record):
         kept[slot - SENT] = record
 
+    def copy_of(i):
+        first = i * GROUP_KEEP
+        return pltpu.make_async_copy(
+            kept.at[pl.ds(first, GROUP_KEEP)], next_ref.at[pl.ds(SENT + first, GROUP_KEEP)], sems.at[i]
+        )
+
     def group_step(i, carry):
         advance_group(tab_ref, cell_ref, rec_ref, found, SENT + i * GROUP_KEEP, GROUP_KEEP, store)
+        copy_of(i).start()
         return carry
 
     lax.fori_loop(0, KEEP // GROUP_KEEP, group_step, 0)
-    copy = pltpu.make_async_copy(kept, next_ref.at[pl.ds(SENT, KEEP)], sem)
-    copy.start()
-    copy.wait()
-
-
-def arrive_kernel(target_ref, xe_ref, xo_ref, ye_ref, yo_ref, prev_ref, next_ref, inflow_ref, sems):
+    for i in range(KEEP // GROUP_KEEP):
+        copy_of(i).wait()
+
+
+def arrive_kernel(small_ref, xe_ref, xo_ref, ye_ref, yo_ref, prev_ref, next_ref, inflow_ref, sems):
     par_x, par_y = parities()
     copies = []
     for n, (ref, par, base, cap) in enumerate(
@@ -349,7 +384,7 @@
         jnp.where(par_y == 0, y_even, y_odd),
     ]
     flow = jnp.concatenate([a[r : r + 1] for a in arrivals for r in range(2)], axis=1)
-    links = jnp.concatenate([target_ref[j : j + 1, :] for j in range(8)], axis=1)
+    links = jnp.concatenate([small_ref[j : j + 1, :] for j in range(8, 16)], axis=1)
     spread = jnp.where(index_of((CX, 1024), 0) == (links >> 8), flow, 0.0)
     parts = jnp.concatenate(split(spread, 3), axis=0)
     hot = one_hot(links & (CY - 1), 1024)
@@ -360,7 +395,6 @@
 
 
 VMEM = pl.BlockSpec(memory_space=pltpu.VMEM)
-SMEM = pl.BlockSpec(memory_space=pltpu.SMEM)
 ANY = pl.BlockSpec(memory_space=pl.ANY)
 LIMIT = pltpu.CompilerParams(vmem_limit_bytes=32 << 20)
 
@@ -386,7 +420,8 @@
 def body(
     pressure, conductivity, storage, source, particles, crossing, particle_cell, river_source, river_target
 ):
-    links = river_source.reshape(8, 128)
+    counts = jnp.pad(crossing.reshape(1, 4), ((0, 7), (0, 124)))
+    small = jnp.concatenate([river_source.reshape(8, 128), river_target.reshape(8, 128), counts], axis=0)
     grid = (pressure, conductivity, storage, source)
     tile = pltpu.VMEM((NZ, CX, CY), F32)
     x_even, x_odd = pl.pallas_call(
@@ -402,15 +437,16 @@
     y_even, y_odd = pl.pallas_call(
         edge_lanes_kernel,
         out_shape=(shape(4, 8, 128), shape(4, 8, 128)),
-        in_specs=[VMEM] * 7 + [SMEM],
+        in_specs=[VMEM] * 6,
         out_specs=(VMEM, VMEM),
         compiler_params=LIMIT,
         name="edge_lanes",
-    )(*grid, *halo_x, links, crossing[0, 0])
+    )(*grid, *halo_x)
     halo_y = exchange(y_even, y_odd, "gy")
     records = particles[0, 0]
     cells = particle_cell[0, 0]
-    field = pltpu.VMEM((NZ, ROWS, LANES), F32)
+    tall = pltpu.VMEM((NZ, 3, TALL, 128), F32)
+    field = pltpu.VMEM((NZ, 3, ROWS, 128), F32)
     head, table, moved, x_even, x_odd, y_even, y_odd = pl.pallas_call(
         sweep_kernel,
         out_shape=(
@@ -422,20 +458,22 @@
             shape(CAPY + 1, 8, 128),
             shape(CAPY + 1, 8, 128),
         ),
-        in_specs=[SMEM] + [VMEM] * 11,
+        in_specs=[VMEM] * 11,
         out_specs=(ANY, VMEM, ANY) + (VMEM,) * 4,
-        scratch_shapes=[field] * 8
+        scratch_shapes=[tall] * 4
+        + [field] * 5
         + [
             pltpu.VMEM((TABLE, CY), F32),
             pltpu.VMEM((TABLE, 128 * GROUP_SENT), F32),
             pltpu.VMEM((SENT, 8, 128), F32),
             pltpu.VMEM((SENT, 8, 128), F32),
             tile,
+            pltpu.VMEM((SENT, 128), F32),
             pltpu.SemaphoreType.DMA((2,)),
         ],
         compiler_params=LIMIT,
         name="sweep",
-    )(crossing[0, 0], *grid, *halo_x, *halo_y, records, cells, links)
+    )(small, *grid, *halo_x, *halo_y, records, cells)
     x_even, x_odd = exchange(x_even, x_odd, "gx")
     y_even, y_odd = exchange(y_even, y_odd, "gy")
     moved = pl.pallas_call(
@@ -443,7 +481,7 @@
         out_shape=shape(OUT, 8, 128),
         in_specs=[VMEM] * 3 + [ANY],
         out_specs=ANY,
-        scratch_shapes=[pltpu.VMEM((TABLE, 128 * GROUP_KEEP), F32), pltpu.VMEM((KEEP, 8, 128), F32), pltpu.SemaphoreType.DMA],
+        scratch_shapes=[pltpu.VMEM((TABLE, 128 * GROUP_KEEP), F32), pltpu.VMEM((KEEP, 8, 128), F32), pltpu.SemaphoreType.DMA((KEEP // GROUP_KEEP,))],
         input_output_aliases={3: 0},
         compiler_params=LIMIT,
         cost_estimate=pl.CostEstimate(
@@ -460,7 +498,7 @@
         input_output_aliases={5: 0},
         compiler_params=LIMIT,
         name="arrive",
-    )(river_target.reshape(8, 128), x_even, x_odd, y_even, y_odd, moved)
+    )(small, x_even, x_odd, y_even, y_odd, moved)
     return head, moved[None, None], inflow
 
 

time: 49.7 us -> 47.8 us (0.962)
  Pallas kernels: 21.6 us -> 20.2 us
  waiting for transfers between devices: 5.37 us -> 4.72 us
    pallas_call x1, Pallas kernels: 8.86 us -> 8.02 us  [body(): pl.pallas_call(sweep_kernel, out_shape=(shape(NZ, CX, CY), shape(TABLE, 2...]
    ppermute x4, waiting for transfers between devices: 5.36 us -> 4.71 us  [exchange(): from_odd = lax.ppermute(odd, axis, swap(size, 1))]
    pallas_call x1, Pallas kernels: 0.98 us -> 0.44 us  [body(): pl.pallas_call(edge_lanes_kernel, out_shape=(shape(4, 8, 128), shape(4, 8...]
  transfers between devices with their start and end apart: 8 -> 8, of which waited for: 2 -> 2; matrix products, arithmetic and copies ran while one was open for 0% -> 0% of each run, Pallas kernels for 17% -> 18%
where the time goes in v3:
time: 47.8 us; the launch traced here: 47.5 us
  starting transfers between devices  21.1 us (44%)
  Pallas kernels  20.2 us (42%)
  waiting for transfers between devices  4.72 us (10%)
  between operations  0.86 us (2%)
  local copies, waits for them, and re-layouts  0.67 us (1%)
    ppermute x4, starting transfers between devices, exchange(): from_odd = lax.ppermute(odd, axis, swap(size, 1))  20.6 us
    pallas_call x1, Pallas kernels, body(): pl.pallas_call(rest_kernel, out_shape=shape(OUT, 8, 128), in_specs=[VMEM]...  8.33 us
    pallas_call x1, Pallas kernels, body(): pl.pallas_call(sweep_kernel, out_shape=(shape(NZ, CX, CY), shape(TABLE, 2...  8.02 us
    ppermute x4, waiting for transfers between devices, exchange(): from_odd = lax.ppermute(odd, axis, swap(size, 1))  4.71 us
    pallas_call x1, Pallas kernels, body(): pl.pallas_call(edge_rows_kernel, out_shape=(shape(NZ, CX, CY), shape(NZ,...  2.05 us
    pallas_call x1, Pallas kernels, body(): pl.pallas_call(arrive_kernel, out_shape=(shape(OUT, 8, 128), shape(CX, CY...  1.34 us
  transfers between devices with their start and end apart: 8, of which 2 were waited for; matrix products, arithmetic and copies ran while one was open for 0% of the time, Pallas kernels for 18%

profile of v3, /device:TPU:38, one launch (start us, length us, event | category | flops | bytes accessed | tf_op | source)
XLA Modules:
  0.0 47.5 jit_solution(14335528011159323929)
XLA Ops:
  0.6 0.0 copy-start.3
  0.6 0.0 copy-start.2
  0.7 0.0 copy-start.1
  0.7 0.0 copy-start
  0.7 2.1 %edge_rows.1 = (f32[10,16,256]{2,1,0:T(8,128)}, f32[10,16,256]{2,1,0:T(8,128)}) custom-call(f32[10,16,256]{2,1,0:T(8,128)} %p_ref.3, f32[10,16,256]{2,1,0:T(8,128)} %c_ref.3, f32[10,16,256]{2,1,0:T(8,128)} %s_ref.3, f32[10,16,256]{2,1,0:T(8,128)} %q_ref.3), custom_call_target="tpu_custom_call" | custom-call | tf_op jit(solution)/shard_map/edge_rows/pallas_call | solution.py:427
  2.7 0.1 collective-permute-start
  2.8 0.0 copy-start.4
  2.8 5.4 %collective-permute-start.1 = (f32[10,16,256]{2,1,0:T(8,128)}, f32[10,16,256]{2,1,0:T(8,128)S(1)}, u32[]{:S(2)}, u32[]{:S(2)}) collective-permute-start(f32[10,16,256]{2,1,0:T(8,128)} %get-tuple-element.17), channel_id=1, source_target_pairs={{8,16},{16,8},{24,32},{32,24},{40,48},{48,40},{56,64},{64,56},{72,... | collective-permute-start | bytes 491528 | tf_op jit(solution)/shard_map/ppermute | solution.py:411
  8.2 0.0 collective-permute-done.re_ref.rxe_ref
  8.3 3.7 %collective-permute-done.1.ro_ref.rxo_ref = f32[10,16,256]{2,1,0:T(8,128)S(1)} collective-permute-done((f32[10,16,256]{2,1,0:T(8,128)}, f32[10,16,256]{2,1,0:T(8,128)S(1)}, u32[]{:S(2)}, u32[]{:S(2)}) %collective-permute-start.1) | collective-permute-done | bytes 163872 | tf_op jit(solution)/shard_map/ppermute | solution.py:411
  11.9 0.0 copy-done.2
  12.0 0.0 copy-start.5
  12.0 0.4 edge_lanes.1
  12.4 0.0 copy-start.7
  12.4 0.0 copy-start.6
  12.4 0.2 collective-permute-start.2
  12.6 5.6 %collective-permute-start.3 = (f32[4,8,128]{2,1,0:T(8,128)S(1)}, f32[4,8,128]{2,1,0:T(8,128)S(1)}, u32[]{:S(2)}, u32[]{:S(2)}) collective-permute-start(f32[4,8,128]{2,1,0:T(8,128)S(1)} %get-tuple-element.19), channel_id=1, source_target_pairs={{1,2},{2,1},{3,4},{4,3},{5,6},{6,5},{9,10},{10,9},{11,12},{12,11},... | collective-permute-start | bytes 49160 | tf_op jit(solution)/shard_map/ppermute | solution.py:411
  18.3 0.0 copy-start.8
  18.3 0.6 %copy-done.8 = s32[1,1,4]{2,1,0:T(1,128)S(1)} copy-done((s32[1,1,4]{2,1,0:T(1,128)S(1)}, s32[1,1,4]{2,1,0:T(1,128)}, u32[]{:S(2)}) %copy-start.8) | copy-done | bytes 40
  18.9 0.0 collective-permute-done.2.rye_ref
  18.9 1.0 %collective-permute-done.3.ryo_ref = f32[4,8,128]{2,1,0:T(8,128)S(1)} collective-permute-done((f32[4,8,128]{2,1,0:T(8,128)S(1)}, f32[4,8,128]{2,1,0:T(8,128)S(1)}, u32[]{:S(2)}, u32[]{:S(2)}) %collective-permute-start.3) | collective-permute-done | bytes 16416 | tf_op jit(solution)/shard_map/ppermute | solution.py:411
  20.0 8.0 %sweep.1 = (f32[10,16,256]{2,1,0:T(8,128)}, bf16[800,512]{1,0:T(8,128)(2,1)S(1)}, f32[144,8,128]{2,1,0:T(8,128)}, f32[17,8,128]{2,1,0:T(8,128)S(1)}, f32[17,8,12...) custom-call(s32[24,128]{1,0:T(8,128)S(1)} %pad_add_fusion.small_ref, ...), custom_call_target="tpu_custom_call" | custom-call | tf_op jit(solution)/shard_map/sweep/pallas_call | solution.py:450
  28.0 0.1 collective-permute-start.6
  28.1 6.0 %collective-permute-start.7 = (f32[5,8,128]{2,1,0:T(8,128)S(1)}, f32[5,8,128]{2,1,0:T(8,128)S(1)}, u32[]{:S(2)}, u32[]{:S(2)}) collective-permute-start(f32[5,8,128]{2,1,0:T(8,128)S(1)} %get-tuple-element.24), channel_id=1, source_target_pairs={{1,2},{2,1},{3,4},{4,3},{5,6},{6,5},{9,10},{10,9},{11,12},{12,11},... | collective-permute-start | bytes 61448 | tf_op jit(solution)/shard_map/ppermute | solution.py:411
  34.1 0.1 collective-permute-start.4
  34.2 3.6 %collective-permute-start.5 = (f32[17,8,128]{2,1,0:T(8,128)S(1)}, f32[17,8,128]{2,1,0:T(8,128)S(1)}, u32[]{:S(2)}, u32[]{:S(2)}) collective-permute-start(f32[17,8,128]{2,1,0:T(8,128)S(1)} %get-tuple-element.22), channel_id=1, source_target_pairs={{8,16},{16,8},{24,32},{32,24},{40,48},{48,40},{56,64},{64,56},{72,... | collective-permute-start | bytes 208904 | tf_op jit(solution)/shard_map/ppermute | solution.py:411
  37.8 8.3 %rest.1.prev_ref = f32[144,8,128]{2,1,0:T(8,128)} custom-call(bf16[800,512]{1,0:T(8,128)(2,1)S(1)} %get-tuple-element.25.tab_ref, f32[104,8,128]{2,1,0:T(8,128)S(1)} %bitcast.7, s32[104,128]{1,0:T(8,128)S(1)} %bitcast.9, f32[144,8,128]{2,1,0:T(8,128)} %get-tuple-element.26.prev_ref), custom_call_target="tpu_custom_call", output_to_operand_aliasing={{}: (3, {})} | custom-call | flops 6710886400 | bytes 4194304 | tf_op jit(solution)/shard_map/rest/pallas_call | solution.py:479
  46.2 0.0 collective-permute-done.6.ye_ref
  46.2 0.0 collective-permute-done.7.yo_ref
  46.2 0.0 collective-permute-done.4.xe_ref
  46.2 0.0 collective-permute-done.5.xo_ref
  46.2 1.3 %arrive.1 = (f32[144,8,128]{2,1,0:T(8,128)}, f32[16,256]{1,0:T(8,128)}) custom-call(s32[24,128]{1,0:T(8,128)S(1)} %pad_add_fusion.small_ref, f32[17,8,128]{2,1,0:T(8,128)S(1)} %collective-permute-done.4.xe_ref, f32[17,8,128]{2,1,0:T(8,128)S(1)} %collective-permute-done.5.xo_ref, ...), custom_call_target="tpu_custom_call", output_to_operand_aliasing={{0}: (5, {})} | custom-call | tf_op jit(solution)/shard_map/arrive/pallas_call | solution.py:492
  (8 shorter events, 0.0 us)
Async XLA Ops:
  0.6 11.3 %copy-start.3 = (f32[10,16,256]{2,1,0:T(8,128)S(1)}, f32[10,16,256]{2,1,0:T(8,128)}, u32[]{:S(2)}) copy-start(f32[10,16,256]{2,1,0:T(8,128)} %q_ref.3) | copy-start | bytes 491524
  0.6 11.3 %copy-start.2 = (f32[10,16,256]{2,1,0:T(8,128)S(1)}, f32[10,16,256]{2,1,0:T(8,128)}, u32[]{:S(2)}) copy-start(f32[10,16,256]{2,1,0:T(8,128)} %s_ref.3) | copy-start | bytes 491524
  0.7 11.3 %copy-start.1 = (f32[10,16,256]{2,1,0:T(8,128)S(1)}, f32[10,16,256]{2,1,0:T(8,128)}, u32[]{:S(2)}) copy-start(f32[10,16,256]{2,1,0:T(8,128)} %c_ref.3) | copy-start | bytes 491524
  0.7 11.3 %copy-start = (f32[10,16,256]{2,1,0:T(8,128)S(1)}, f32[10,16,256]{2,1,0:T(8,128)}, u32[]{:S(2)}) copy-start(f32[10,16,256]{2,1,0:T(8,128)} %p_ref.3) | copy-start | bytes 491524
  2.7 5.5 %collective-permute-start = (f32[10,16,256]{2,1,0:T(8,128)}, f32[10,16,256]{2,1,0:T(8,128)S(1)}, u32[]{:S(2)}, u32[]{:S(2)}) collective-permute-start(f32[10,16,256]{2,1,0:T(8,128)} %get-tuple-element.16), channel_id=1, source_target_pairs={{0,8},{8,0},{16,24},{24,16},{32,40},{40,32},{48,56},{56,48},{64,72... | collective-permute-start | bytes 491528 | tf_op jit(solution)/shard_map/ppermute | solution.py:412
  2.8 17.1 %copy-start.4 = (f32[1,1,104,8,128]{4,3,2,1,0:T(8,128)S(1)}, f32[1,1,104,8,128]{4,3,2,1,0:T(8,128)}, u32[]{:S(2)}) copy-start(f32[1,1,104,8,128]{4,3,2,1,0:T(8,128)} %param.13) | copy-start | bytes 1277956
  2.8 9.1 %collective-permute-start.1 = (f32[10,16,256]{2,1,0:T(8,128)}, f32[10,16,256]{2,1,0:T(8,128)S(1)}, u32[]{:S(2)}, u32[]{:S(2)}) collective-permute-start(f32[10,16,256]{2,1,0:T(8,128)} %get-tuple-element.17), channel_id=1, source_target_pairs={{8,16},{16,8},{24,32},{32,24},{40,48},{48,40},{56,64},{64,56},{72,... | collective-permute-start | bytes 491528 | tf_op jit(solution)/shard_map/ppermute | solution.py:411
  12.0 8.0 %copy-start.5 = (s32[1,1,104,128]{3,2,1,0:T(8,128)S(1)}, s32[1,1,104,128]{3,2,1,0:T(8,128)}, u32[]{:S(2)}) copy-start(s32[1,1,104,128]{3,2,1,0:T(8,128)} %param.15) | copy-start | bytes 159748
  12.4 5.9 %copy-start.7 = (s32[1,1,4,2,128]{4,3,2,1,0:T(2,128)S(1)}, s32[1,1,4,2,128]{4,3,2,1,0:T(2,128)}, u32[]{:S(2)}) copy-start(s32[1,1,4,2,128]{4,3,2,1,0:T(2,128)} %param.16) | copy-start | bytes 12292
  12.4 5.9 %copy-start.6 = (s32[1,1,4,2,128]{4,3,2,1,0:T(2,128)S(1)}, s32[1,1,4,2,128]{4,3,2,1,0:T(2,128)}, u32[]{:S(2)}) copy-start(s32[1,1,4,2,128]{4,3,2,1,0:T(2,128)} %param.17) | copy-start | bytes 12292
  12.4 6.5 %collective-permute-start.2 = (f32[4,8,128]{2,1,0:T(8,128)S(1)}, f32[4,8,128]{2,1,0:T(8,128)S(1)}, u32[]{:S(2)}, u32[]{:S(2)}) collective-permute-start(f32[4,8,128]{2,1,0:T(8,128)S(1)} %get-tuple-element.18), channel_id=1, source_target_pairs={{0,1},{1,0},{2,3},{3,2},{4,5},{5,4},{6,7},{7,6},{8,9},{9,8},{10,11... | collective-permute-start | bytes 49160 | tf_op jit(solution)/shard_map/ppermute | solution.py:412
  12.6 7.3 %collective-permute-start.3 = (f32[4,8,128]{2,1,0:T(8,128)S(1)}, f32[4,8,128]{2,1,0:T(8,128)S(1)}, u32[]{:S(2)}, u32[]{:S(2)}) collective-permute-start(f32[4,8,128]{2,1,0:T(8,128)S(1)} %get-tuple-element.19), channel_id=1, source_target_pairs={{1,2},{2,1},{3,4},{4,3},{5,6},{6,5},{9,10},{10,9},{11,12},{12,11},... | collective-permute-start | bytes 49160 | tf_op jit(solution)/shard_map/ppermute | solution.py:411
  18.3 0.7 %copy-start.8 = (s32[1,1,4]{2,1,0:T(1,128)S(1)}, s32[1,1,4]{2,1,0:T(1,128)}, u32[]{:S(2)}) copy-start(s32[1,1,4]{2,1,0:T(1,128)} %param.14) | copy-start | bytes 52
  28.0 18.2 %collective-permute-start.6 = (f32[5,8,128]{2,1,0:T(8,128)S(1)}, f32[5,8,128]{2,1,0:T(8,128)S(1)}, u32[]{:S(2)}, u32[]{:S(2)}) collective-permute-start(f32[5,8,128]{2,1,0:T(8,128)S(1)} %get-tuple-element.23), channel_id=1, source_target_pairs={{0,1},{1,0},{2,3},{3,2},{4,5},{5,4},{6,7},{7,6},{8,9},{9,8},{10,11... | collective-permute-start | bytes 61448 | tf_op jit(solution)/shard_map/ppermute | solution.py:412
  28.1 18.1 %collective-permute-start.7 = (f32[5,8,128]{2,1,0:T(8,128)S(1)}, f32[5,8,128]{2,1,0:T(8,128)S(1)}, u32[]{:S(2)}, u32[]{:S(2)}) collective-permute-start(f32[5,8,128]{2,1,0:T(8,128)S(1)} %get-tuple-element.24), channel_id=1, source_target_pairs={{1,2},{2,1},{3,4},{4,3},{5,6},{6,5},{9,10},{10,9},{11,12},{12,11},... | collective-permute-start | bytes 61448 | tf_op jit(solution)/shard_map/ppermute | solution.py:411
  34.1 12.0 %collective-permute-start.4 = (f32[17,8,128]{2,1,0:T(8,128)S(1)}, f32[17,8,128]{2,1,0:T(8,128)S(1)}, u32[]{:S(2)}, u32[]{:S(2)}) collective-permute-start(f32[17,8,128]{2,1,0:T(8,128)S(1)} %get-tuple-element.21), channel_id=1, source_target_pairs={{0,8},{8,0},{16,24},{24,16},{32,40},{40,32},{48,56},{56,48},{64,72... | collective-permute-start | bytes 208904 | tf_op jit(solution)/shard_map/ppermute | solution.py:412
  34.2 11.9 %collective-permute-start.5 = (f32[17,8,128]{2,1,0:T(8,128)S(1)}, f32[17,8,128]{2,1,0:T(8,128)S(1)}, u32[]{:S(2)}, u32[]{:S(2)}) collective-permute-start(f32[17,8,128]{2,1,0:T(8,128)S(1)} %get-tuple-element.22), channel_id=1, source_target_pairs={{8,16},{16,8},{24,32},{32,24},{40,48},{48,40},{56,64},{64,56},{72,... | collective-permute-start | bytes 208904 | tf_op jit(solution)/shard_map/ppermute | solution.py:411

commit v4 on v3

--- a/solution.py
+++ b/solution.py
@@ -57,6 +57,11 @@
     return pltpu.roll(x, shift % x.shape[axis], axis)
 
 
+def in_grid(axis):
+    here = lax.axis_index(axis)
+    return jnp.where((here == 0) | (here == lax.axis_size(axis) - 1), 0, 1)
+
+
 def parities():
     return lax.rem(lax.axis_index("gx"), 2), lax.rem(lax.axis_index("gy"), 2)
 
@@ -70,6 +75,7 @@
         for copy in loads[h]:
             copy.start()
     parity = parities()[0]
+    within = in_grid("gx")
     row = index_of((1, 8, CY), 1)
     stores = []
     for h, part in enumerate(halves):
@@ -85,7 +91,7 @@
             pieces.append(jnp.concatenate([p[:, side], c[:, side], (s + weight)[:, side], rhs[:, side]], axis=1))
         west, east = pieces
         even_ref[part] = jnp.where(parity == 0, east, west)
-        odd_ref[part] = jnp.where(parity == 0, west, east)
+        odd_ref[part] = jnp.where(within == 0, 0.0, jnp.where(parity == 0, west, east))
         for n, (a, b) in enumerate(((even_ref, even_hbm), (odd_ref, odd_hbm))):
             copy = pltpu.make_async_copy(a.at[part], b.at[part], sems.at[h, 4 + n])
             copy.start()
@@ -120,9 +126,10 @@
                 total[i // 8] = total[i // 8] + roll(rows[i], 4 * slot - low, 1)
         packed.append(total)
     south, north = packed
+    within = in_grid("gy")
     for j in range(4):
         even_ref[j] = jnp.where(par_y == 0, north[j], south[j])
-        odd_ref[j] = jnp.where(par_y == 0, south[j], north[j])
+        odd_ref[j] = jnp.where(within == 0, 0.0, jnp.where(par_y == 0, south[j], north[j]))
 
 
 def one_hot(values, lanes):
@@ -208,8 +215,8 @@
 
 def sweep_kernel(
     small_ref, p_ref, c_ref, s_ref, q_ref, rxe_ref, rxo_ref, rye_ref, ryo_ref, rec_ref, cell_ref,
-    head_ref, tab_ref, next_ref, xe_ref, xo_ref, ye_ref, yo_ref,
-    h0, h1, cond, wx, rhs, inv, wy, wy_back, wz, flat, found, kept, sent, final, live_ref, sems,
+    head_ref, tab_ref, kept, xe_ref, xo_ref, ye_ref, yo_ref,
+    h0, h1, cond, wx, rhs, inv, wy, wy_back, wz, flat, found, sent, final, live_ref, sem,
 ):
     par_x, par_y = parities()
     edge = jnp.zeros((NZ, 3, 8, 128), F32)
@@ -291,7 +298,7 @@
                 put(LEVEL, -wz[k, j, INNER, :] * (old[k + 1, j, OWN, :] - h[j] + 1.0))
             suction = jnp.maximum(-h[j], 0.0)
             put(SATUR, RESIDUAL_SAT + (1.0 - RESIDUAL_SAT) * lax.rsqrt(1.0 + suction * suction))
-    head_copy = pltpu.make_async_copy(final, head_ref, sems.at[0])
+    head_copy = pltpu.make_async_copy(final, head_ref, sem)
     head_copy.start()
     coarse, fine = split(flat[...], 2)
     tab_ref[:, 0:CY] = coarse
@@ -313,8 +320,6 @@
         return carry
 
     lax.fori_loop(0, SENT // GROUP_SENT, group_step, 0)
-    copy = pltpu.make_async_copy(kept, next_ref.at[pl.ds(0, SENT)], sems.at[1])
-    copy.start()
     links = jnp.concatenate([small_ref[j : j + 1, :] for j in range(8)], axis=1)
     surface = jnp.concatenate(split(final[NZ - 1], 3), axis=0)
     at_links = jnp.dot(surface, one_hot(links & (CY - 1), 1024), preferred_element_type=F32)
@@ -326,55 +331,50 @@
         jnp.concatenate([flow[:, 256 * d : 256 * d + 128], flow[:, 256 * d + 128 : 256 * d + 256]] * 4, axis=0)
         for d in range(4)
     ]
-    for ref, par, low, cap in (
-        (xe_ref, par_x, 0, CAPX),
-        (xo_ref, 1 - par_x, 0, CAPX),
-        (ye_ref, par_y, 2, CAPY),
-        (yo_ref, 1 - par_y, 2, CAPY),
+    for ref, par, low, cap, within in (
+        (xe_ref, par_x, 0, CAPX, None),
+        (xo_ref, 1 - par_x, 0, CAPX, in_grid("gx")),
+        (ye_ref, par_y, 2, CAPY, None),
+        (yo_ref, 1 - par_y, 2, CAPY, in_grid("gy")),
     ):
         base = 2 * CAPX if low else 0
-        ref[0:cap] = sent[pl.ds(base + par * cap, cap)]
-        ref[cap] = jnp.where(par == 0, flows[low], flows[low + 1])
-    copy.wait()
+        leaving = sent[pl.ds(base + par * cap, cap)]
+        flow_out = jnp.where(par == 0, flows[low], flows[low + 1])
+        ref[0:cap] = leaving if within is None else jnp.where(within == 0, 0.0, leaving)
+        ref[cap] = flow_out if within is None else jnp.where(within == 0, 0.0, flow_out)
     head_copy.wait()
 
 
-def rest_kernel(tab_ref, rec_ref, cell_ref, prev_ref, next_ref, found, kept, sems):
+def rest_kernel(first, tab_ref, rec_ref, cell_ref, *refs):
+    kept, found = refs[-2:]
+
     def store(slot, record):
-        kept[slot - SENT] = record
-
-    def copy_of(i):
-        first = i * GROUP_KEEP
-        return pltpu.make_async_copy(
-            kept.at[pl.ds(first, GROUP_KEEP)], next_ref.at[pl.ds(SENT + first, GROUP_KEEP)], sems.at[i]
-        )
-
-    def group_step(i, carry):
-        advance_group(tab_ref, cell_ref, rec_ref, found, SENT + i * GROUP_KEEP, GROUP_KEEP, store)
-        copy_of(i).start()
-        return carry
-
-    lax.fori_loop(0, KEEP // GROUP_KEEP, group_step, 0)
-    for i in range(KEEP // GROUP_KEEP):
-        copy_of(i).wait()
-
-
-def arrive_kernel(small_ref, xe_ref, xo_ref, ye_ref, yo_ref, prev_ref, next_ref, inflow_ref, sems):
+        kept[slot - first] = record
+
+    advance_group(tab_ref, cell_ref, rec_ref, found, first, GROUP_KEEP, store)
+
+
+def arrive_kernel(small_ref, xe_ref, xo_ref, ye_ref, yo_ref, *refs):
+    kept = refs[:-3]
+    next_ref, inflow_ref, sems = refs[-3:]
     par_x, par_y = parities()
     copies = []
-    for n, (ref, par, base, cap) in enumerate(
-        (
-            (xe_ref, 1 - par_x, PB, CAPX),
-            (xo_ref, par_x, PB, CAPX),
-            (ye_ref, 1 - par_y, PB + 2 * CAPX, CAPY),
-            (yo_ref, par_y, PB + 2 * CAPX, CAPY),
-        )
+
+    def send(source, first, count):
+        copy = pltpu.make_async_copy(source, next_ref.at[pl.ds(first, count)], sems.at[len(copies)])
+        copy.start()
+        copies.append(copy)
+
+    send(kept[0], 0, SENT)
+    for n, ref in enumerate(kept[1:]):
+        send(ref, SENT + n * GROUP_KEEP, GROUP_KEEP)
+    for ref, par, base, cap in (
+        (xe_ref, 1 - par_x, PB, CAPX),
+        (xo_ref, par_x, PB, CAPX),
+        (ye_ref, 1 - par_y, PB + 2 * CAPX, CAPY),
+        (yo_ref, par_y, PB + 2 * CAPX, CAPY),
     ):
-        copies.append(
-            pltpu.make_async_copy(ref.at[pl.ds(0, cap)], next_ref.at[pl.ds(base + par * cap, cap)], sems.at[n])
-        )
-    for copy in copies:
-        copy.start()
+        send(ref.at[pl.ds(0, cap)], base + par * cap, cap)
     x_even, x_odd = xe_ref[CAPX], xo_ref[CAPX]
     y_even, y_odd = ye_ref[CAPY], yo_ref[CAPY]
     arrivals = [
@@ -399,17 +399,31 @@
 LIMIT = pltpu.CompilerParams(vmem_limit_bytes=32 << 20)
 
 
-def swap(size, first):
+AXES = ("gx", "gy")
+
+
+def swap(value, axis, first):
+    sizes = [lax.axis_size(name) for name in AXES]
+    along, across = AXES.index(axis), 1 - AXES.index(axis)
+
+    def place(i, other):
+        at = (i, other) if along == 0 else (other, i)
+        return at[0] * sizes[1] + at[1]
+
     pairs = []
-    for i in range(first, size - 1, 2):
-        pairs += [(i, i + 1), (i + 1, i)]
-    return pairs
+    for other in range(sizes[across]):
+        for i in range(first, sizes[along] - 1, 2):
+            pairs.append((place(i, other), place(i + 1, other)))
+    if first:
+        for end in (0, sizes[along] - 1):
+            for other in range(0, sizes[across], 2):
+                pairs.append((place(end, other), place(end, other + 1)))
+    return lax.ppermute(value, AXES, pairs + [(b, a) for a, b in pairs])
 
 
 def exchange(even, odd, axis):
-    size = lax.axis_size(axis)
-    from_odd = lax.ppermute(odd, axis, swap(size, 1))
-    from_even = lax.ppermute(even, axis, swap(size, 0))
+    from_odd = swap(odd, axis, 1)
+    from_even = swap(even, axis, 0)
     return from_even, from_odd
 
 
@@ -447,58 +461,69 @@
     cells = particle_cell[0, 0]
     tall = pltpu.VMEM((NZ, 3, TALL, 128), F32)
     field = pltpu.VMEM((NZ, 3, ROWS, 128), F32)
-    head, table, moved, x_even, x_odd, y_even, y_odd = pl.pallas_call(
+    head, table, kept, x_even, x_odd, y_even, y_odd = pl.pallas_call(
         sweep_kernel,
         out_shape=(
             shape(NZ, CX, CY),
             shape(TABLE, 2 * CY, dtype=BF16),
-            shape(OUT, 8, 128),
+            shape(SENT, 8, 128),
             shape(CAPX + 1, 8, 128),
             shape(CAPX + 1, 8, 128),
             shape(CAPY + 1, 8, 128),
             shape(CAPY + 1, 8, 128),
         ),
         in_specs=[VMEM] * 11,
-        out_specs=(ANY, VMEM, ANY) + (VMEM,) * 4,
+        out_specs=(ANY,) + (VMEM,) * 6,
         scratch_shapes=[tall] * 4
         + [field] * 5
         + [
             pltpu.VMEM((TABLE, CY), F32),
             pltpu.VMEM((TABLE, 128 * GROUP_SENT), F32),
             pltpu.VMEM((SENT, 8, 128), F32),
-            pltpu.VMEM((SENT, 8, 128), F32),
             tile,
             pltpu.VMEM((SENT, 128), F32),
-            pltpu.SemaphoreType.DMA((2,)),
+            pltpu.SemaphoreType.DMA,
         ],
         compiler_params=LIMIT,
         name="sweep",
     )(small, *grid, *halo_x, *halo_y, records, cells)
-    x_even, x_odd = exchange(x_even, x_odd, "gx")
-    y_even, y_odd = exchange(y_even, y_odd, "gy")
-    moved = pl.pallas_call(
-        rest_kernel,
-        out_shape=shape(OUT, 8, 128),
-        in_specs=[VMEM] * 3 + [ANY],
-        out_specs=ANY,
-        scratch_shapes=[pltpu.VMEM((TABLE, 128 * GROUP_KEEP), F32), pltpu.VMEM((KEEP, 8, 128), F32), pltpu.SemaphoreType.DMA((KEEP // GROUP_KEEP,))],
-        input_output_aliases={3: 0},
-        compiler_params=LIMIT,
-        cost_estimate=pl.CostEstimate(
-            flops=2 * TABLE * 512 * 128 * KEEP, bytes_accessed=4 << 20, transcendentals=0
-        ),
-        name="rest",
-    )(table, records, cells, moved)
+    payloads = [
+        (x_odd, "gx", 1),
+        (y_even, "gy", 0),
+        (y_odd, "gy", 1),
+        (x_even, "gx", 0),
+    ]
+    received = []
+    done = [kept]
+    waiting = payloads[0][0]
+    for n, (_, axis, first) in enumerate(payloads):
+        received.append(swap(waiting, axis, first))
+        later = [payloads[n + 1][0]] if n + 1 < len(payloads) else []
+        outs = pl.pallas_call(
+            functools.partial(rest_kernel, SENT + n * GROUP_KEEP),
+            out_shape=[jax.ShapeDtypeStruct(v.shape, v.dtype) for v in later] + [shape(GROUP_KEEP, 8, 128)],
+            in_specs=[VMEM] * (3 + len(later)),
+            out_specs=[VMEM] * (1 + len(later)),
+            scratch_shapes=[pltpu.VMEM((TABLE, 128 * GROUP_KEEP), F32)],
+            input_output_aliases={3: 0} if later else {},
+            compiler_params=LIMIT,
+            cost_estimate=pl.CostEstimate(
+                flops=2 * TABLE * 512 * 128 * GROUP_KEEP, bytes_accessed=1 << 20, transcendentals=0
+            ),
+            name=f"rest_{n}",
+        )(table, records, cells, *later)
+        done.append(outs[-1])
+        waiting = outs[0]
+    from_x_odd, from_y_even, from_y_odd, from_x_even = received
     moved, inflow = pl.pallas_call(
         arrive_kernel,
         out_shape=(shape(OUT, 8, 128), shape(CX, CY)),
-        in_specs=[VMEM] * 5 + [ANY],
+        in_specs=[VMEM] * (5 + len(done)),
         out_specs=(ANY, VMEM),
-        scratch_shapes=[pltpu.SemaphoreType.DMA((4,))],
-        input_output_aliases={5: 0},
+        scratch_shapes=[pltpu.SemaphoreType.DMA((4 + len(done),))],
         compiler_params=LIMIT,
         name="arrive",
-    )(small, x_even, x_odd, y_even, y_odd, moved)
+    )(small, from_x_even, from_x_odd, from_y_even, from_y_odd, *done)
     return head, moved[None, None], inflow
 
 

time: 47.8 us -> 40.7 us (0.85)
  the two profiles are of different devices: /device:TPU:38 before, /device:TPU:39 now
where the time goes in v4:
time: 40.7 us; the launch traced here: 40.6 us
  Pallas kernels  19.3 us (47%)
  starting transfers between devices  15.2 us (37%)
  waiting for transfers between devices  4.43 us (11%)
  between operations  0.97 us (2%)
  local copies, waits for them, and re-layouts  0.69 us (2%)
    ppermute x8, starting transfers between devices, swap(): return lax.ppermute(value, AXES, pairs + [(b, a) for a, b in pairs])  15.2 us
    pallas_call x4, Pallas kernels, body(): pl.pallas_call(functools.partial(rest_kernel, SENT + n * GROUP_KEEP), out...  7.69 us
    pallas_call x1, Pallas kernels, body(): pl.pallas_call(sweep_kernel, out_shape=(shape(NZ, CX, CY), shape(TABLE, 2...  7.61 us
    ppermute x8, waiting for transfers between devices, swap(): return lax.ppermute(value, AXES, pairs + [(b, a) for a, b in pairs])  4.43 us
    pallas_call x1, Pallas kernels, body(): pl.pallas_call(edge_rows_kernel, out_shape=(shape(NZ, CX, CY), shape(NZ,...  2.05 us
    pallas_call x1, Pallas kernels, body(): pl.pallas_call(arrive_kernel, out_shape=(shape(OUT, 8, 128), shape(CX, CY...  1.5 us
  transfers between devices with their start and end apart: 8, of which 2 were waited for; matrix products, arithmetic and copies ran while one was open for 0% of the time, Pallas kernels for 19%

profile of v4, /device:TPU:39, one launch (start us, length us, event | category | flops | bytes accessed | tf_op | source)
XLA Modules:
  0.0 40.6 jit_solution(5728462658421892927)
XLA Ops:
  0.6 0.0 copy-start.3
  0.7 2.1 %edge_rows.1 = (f32[10,16,256]{2,1,0:T(8,128)}, f32[10,16,256]{2,1,0:T(8,128)}) custom-call(f32[10,16,256]{2,1,0:T(8,128)} %p_ref.3, f32[10,16,256]{2,1,0:T(8,128)} %c_ref.3, f32[10,16,256]{2,1,0:T(8,128)} %s_ref.3, f32[10,16,256]{2,1,0:T(8,128)} %q_ref.3), custom_call_target="tpu_custom_call" | custom-call | tf_op jit(solution)/shard_map/edge_rows/pallas_call | solution.py:441
  2.7 0.8 %collective-permute-start = (f32[10,16,256]{2,1,0:T(8,128)}, f32[10,16,256]{2,1,0:T(8,128)S(1)}, u32[]{:S(2)}, u32[]{:S(2)}) collective-permute-start(f32[10,16,256]{2,1,0:T(8,128)} %get-tuple-element.22), channel_id=1, source_target_pairs={{0,8},{16,24},{32,40},{48,56},{64,72},{80,88},{96,104},{112,120},{... | collective-permute-start | bytes 491528 | tf_op jit(solution)/shard_map/ppermute | solution.py:421
  3.5 1.3 %collective-permute-start.1 = (f32[10,16,256]{2,1,0:T(8,128)}, f32[10,16,256]{2,1,0:T(8,128)S(1)}, u32[]{:S(2)}, u32[]{:S(2)}) collective-permute-start(f32[10,16,256]{2,1,0:T(8,128)} %get-tuple-element.23), channel_id=1, source_target_pairs={{8,16},{24,32},{40,48},{56,64},{72,80},{88,96},{104,112},{120,128}... | collective-permute-start | bytes 491528 | tf_op jit(solution)/shard_map/ppermute | solution.py:421
  4.8 0.0 collective-permute-done.re_ref.rxe_ref
  4.8 4.0 %collective-permute-done.1.ro_ref.rxo_ref = f32[10,16,256]{2,1,0:T(8,128)S(1)} collective-permute-done((f32[10,16,256]{2,1,0:T(8,128)}, f32[10,16,256]{2,1,0:T(8,128)S(1)}, u32[]{:S(2)}, u32[]{:S(2)}) %collective-permute-start.1) | collective-permute-done | bytes 163872 | tf_op jit(solution)/shard_map/ppermute | solution.py:421
  8.8 0.0 copy-done
  8.8 0.0 copy-start.5
  8.8 0.4 %edge_lanes.1 = (f32[4,8,128]{2,1,0:T(8,128)S(1)}, f32[4,8,128]{2,1,0:T(8,128)S(1)}) custom-call(f32[10,16,256]{2,1,0:T(8,128)S(1)} %copy-done, f32[10,16,256]{2,1,0:T(8,128)S(1)} %copy-done.1, f32[10,16,256]{2,1,0:T(8,128)S(1)} %copy-done.2, f32[10,16,256]{2,1,0:T(8,128)S(1)} %copy-done.3, f32[10,16,256]{2,1,0:T(8,128)S(1)} %collective-permute-done.re_ref.rxe_ref, ...), custom_call_target="tpu_custom_call" | custom-call | tf_op jit(solution)/shard_map/edge_lanes/pallas_call | solution.py:451
  9.2 0.0 copy-start.7
  9.2 0.0 copy-start.6
  9.3 0.1 collective-permute-start.2
  9.4 3.3 %collective-permute-start.3 = (f32[4,8,128]{2,1,0:T(8,128)S(1)}, f32[4,8,128]{2,1,0:T(8,128)S(1)}, u32[]{:S(2)}, u32[]{:S(2)}) collective-permute-start(f32[4,8,128]{2,1,0:T(8,128)S(1)} %get-tuple-element.25), channel_id=1, source_target_pairs={{1,2},{3,4},{5,6},{9,10},{11,12},{13,14},{17,18},{19,20},{21,22},{... | collective-permute-start | bytes 49160 | tf_op jit(solution)/shard_map/ppermute | solution.py:421
  12.6 0.0 copy-done.7
  12.6 0.6 %copy-done.8 = s32[1,1,4]{2,1,0:T(1,128)S(1)} copy-done((s32[1,1,4]{2,1,0:T(1,128)S(1)}, s32[1,1,4]{2,1,0:T(1,128)}, u32[]{:S(2)}) %copy-start.8) | copy-done | bytes 40
  13.3 0.0 collective-permute-done.2.rye_ref
  13.3 0.5 %collective-permute-done.3.ryo_ref = f32[4,8,128]{2,1,0:T(8,128)S(1)} collective-permute-done((f32[4,8,128]{2,1,0:T(8,128)S(1)}, f32[4,8,128]{2,1,0:T(8,128)S(1)}, u32[]{:S(2)}, u32[]{:S(2)}) %collective-permute-start.3) | collective-permute-done | bytes 16416 | tf_op jit(solution)/shard_map/ppermute | solution.py:421
  13.7 0.0 copy-done.5
  13.7 7.6 %sweep.1 = (f32[10,16,256]{2,1,0:T(8,128)}, bf16[800,512]{1,0:T(8,128)(2,1)S(1)}, f32[40,8,128]{2,1,0:T(8,128)S(1)}, f32[17,8,128]{2,1,0:T(8,128)S(1)}, f32[17,8...) custom-call(s32[24,128]{1,0:T(8,128)S(1)} %pad_add_fusion.small_ref, ...), custom_call_target="tpu_custom_call" | custom-call | tf_op jit(solution)/shard_map/sweep/pallas_call | solution.py:464
  21.4 2.2 %collective-permute-start.5 = (f32[17,8,128]{2,1,0:T(8,128)S(1)}, f32[17,8,128]{2,1,0:T(8,128)S(1)}, u32[]{:S(2)}, u32[]{:S(2)}) collective-permute-start(f32[17,8,128]{2,1,0:T(8,128)S(1)} %get-tuple-element.30), channel_id=1, source_target_pairs={{8,16},{24,32},{40,48},{56,64},{72,80},{88,96},{104,112},{120,128}... | collective-permute-start | bytes 208904 | tf_op jit(solution)/shard_map/ppermute | solution.py:421
  23.6 1.9 %rest_0.1 = (f32[5,8,128]{2,1,0:T(8,128)S(1)}, f32[16,8,128]{2,1,0:T(8,128)S(1)}) custom-call(bf16[800,512]{1,0:T(8,128)(2,1)S(1)} %get-tuple-element.27.tab_ref, f32[104,8,128]{2,1,0:T(8,128)S(1)} %bitcast.7, s32[104,128]{1,0:T(8,128)S(1)} %bitcast.12, f32[5,8,128]{2,1,0:T(8,128)S(1)} %get-tuple-element.31.refs_0_), custom_call_target="tpu_custom_call", output_to_operand_aliasing={{0}: (3, {})} | custom-call | flops 1677721600 | bytes 1048576 | tf_op jit(solution)/shard_map/rest_0/pallas_call | solution.py:502
  25.5 0.3 collective-permute-start.6
  25.8 1.9 %rest_1.1 = (f32[5,8,128]{2,1,0:T(8,128)S(1)}, f32[16,8,128]{2,1,0:T(8,128)S(1)}) custom-call(bf16[800,512]{1,0:T(8,128)(2,1)S(1)} %get-tuple-element.27.tab_ref, f32[104,8,128]{2,1,0:T(8,128)S(1)} %bitcast.8, s32[104,128]{1,0:T(8,128)S(1)} %bitcast.13, f32[5,8,128]{2,1,0:T(8,128)S(1)} %get-tuple-element.33.refs_0_), custom_call_target="tpu_custom_call", output_to_operand_aliasing={{0}: (3, {})} | custom-call | flops 1677721600 | bytes 1048576 | tf_op jit(solution)/shard_map/rest_1/pallas_call | solution.py:502
  27.7 1.9 %rest_2.1 = (f32[17,8,128]{2,1,0:T(8,128)S(1)}, f32[16,8,128]{2,1,0:T(8,128)S(1)}) custom-call(bf16[800,512]{1,0:T(8,128)(2,1)S(1)} %get-tuple-element.27.tab_ref, f32[104,8,128]{2,1,0:T(8,128)S(1)} %bitcast.9, s32[104,128]{1,0:T(8,128)S(1)} %bitcast.14, f32[17,8,128]{2,1,0:T(8,128)S(1)} %get-tuple-element.28.refs_0_), custom_call_target="tpu_custom_call", output_to_operand_aliasing={{0}: (3, {})} | custom-call | flops 1677721600 | bytes 1048576 | tf_op jit(solution)/shard_map/rest_2/pallas_call | solution.py:502
  29.7 3.7 %collective-permute-start.7 = (f32[5,8,128]{2,1,0:T(8,128)S(1)}, f32[5,8,128]{2,1,0:T(8,128)S(1)}, u32[]{:S(2)}, u32[]{:S(2)}) collective-permute-start(f32[5,8,128]{2,1,0:T(8,128)S(1)} %get-tuple-element.34), channel_id=1, source_target_pairs={{1,2},{3,4},{5,6},{9,10},{11,12},{13,14},{17,18},{19,20},{21,22},{... | collective-permute-start | bytes 61448 | tf_op jit(solution)/shard_map/ppermute | solution.py:421
  33.3 3.6 %collective-permute-start.4 = (f32[17,8,128]{2,1,0:T(8,128)S(1)}, f32[17,8,128]{2,1,0:T(8,128)S(1)}, u32[]{:S(2)}, u32[]{:S(2)}) collective-permute-start(f32[17,8,128]{2,1,0:T(8,128)S(1)} %get-tuple-element.29), channel_id=1, source_target_pairs={{0,8},{16,24},{32,40},{48,56},{64,72},{80,88},{96,104},{112,120},{... | collective-permute-start | bytes 208904 | tf_op jit(solution)/shard_map/ppermute | solution.py:421
  37.0 1.9 %rest_3.1.refs_4_ = f32[16,8,128]{2,1,0:T(8,128)S(1)} custom-call(bf16[800,512]{1,0:T(8,128)(2,1)S(1)} %get-tuple-element.27.tab_ref, f32[104,8,128]{2,1,0:T(8,128)S(1)} %bitcast.10, s32[104,128]{1,0:T(8,128)S(1)} %bitcast.15), custom_call_target="tpu_custom_call" | custom-call | flops 1677721600 | bytes 1048576 | tf_op jit(solution)/shard_map/rest_3/pallas_call | solution.py:502
  38.9 0.0 collective-permute-done.6.ye_ref
  38.9 0.0 collective-permute-done.7.yo_ref
  38.9 0.0 collective-permute-done.5.xo_ref
  38.9 0.0 collective-permute-done.4.xe_ref
  38.9 1.5 %arrive.1 = (f32[144,8,128]{2,1,0:T(8,128)}, f32[16,256]{1,0:T(8,128)}) custom-call(s32[24,128]{1,0:T(8,128)S(1)} %pad_add_fusion.small_ref, f32[17,8,128]{2,1,0:T(8,128)S(1)} %collective-permute-done.4.xe_ref, f32[17,8,128]{2,1,0:T(8,128)S(1)} %collective-permute-done.5.xo_ref, f32[5,8,128]{2,1,0:T(8,128)S(1)} %collective-permute-done.6.ye_ref, ...), custom_call_target="tpu_custom_call" | custom-call | tf_op jit(solution)/shard_map/arrive/pallas_call | solution.py:518
  (11 shorter events, 0.0 us)
Async XLA Ops:
  0.6 8.1 %copy-start.3 = (f32[10,16,256]{2,1,0:T(8,128)S(1)}, f32[10,16,256]{2,1,0:T(8,128)}, u32[]{:S(2)}) copy-start(f32[10,16,256]{2,1,0:T(8,128)} %q_ref.3) | copy-start | bytes 491524
  0.6 8.1 %copy-start.2 = (f32[10,16,256]{2,1,0:T(8,128)S(1)}, f32[10,16,256]{2,1,0:T(8,128)}, u32[]{:S(2)}) copy-start(f32[10,16,256]{2,1,0:T(8,128)} %s_ref.3) | copy-start | bytes 491524
  0.7 8.1 %copy-start.1 = (f32[10,16,256]{2,1,0:T(8,128)S(1)}, f32[10,16,256]{2,1,0:T(8,128)}, u32[]{:S(2)}) copy-start(f32[10,16,256]{2,1,0:T(8,128)} %c_ref.3) | copy-start | bytes 491524
  0.7 8.1 %copy-start = (f32[10,16,256]{2,1,0:T(8,128)S(1)}, f32[10,16,256]{2,1,0:T(8,128)}, u32[]{:S(2)}) copy-start(f32[10,16,256]{2,1,0:T(8,128)} %p_ref.3) | copy-start | bytes 491524
  2.7 2.1 %collective-permute-start = (f32[10,16,256]{2,1,0:T(8,128)}, f32[10,16,256]{2,1,0:T(8,128)S(1)}, u32[]{:S(2)}, u32[]{:S(2)}) collective-permute-start(f32[10,16,256]{2,1,0:T(8,128)} %get-tuple-element.22), channel_id=1, source_target_pairs={{0,8},{16,24},{32,40},{48,56},{64,72},{80,88},{96,104},{112,120},{... | collective-permute-start | bytes 491528 | tf_op jit(solution)/shard_map/ppermute | solution.py:421
  3.5 10.3 %copy-start.4 = (f32[1,1,104,8,128]{4,3,2,1,0:T(8,128)S(1)}, f32[1,1,104,8,128]{4,3,2,1,0:T(8,128)}, u32[]{:S(2)}) copy-start(f32[1,1,104,8,128]{4,3,2,1,0:T(8,128)} %param.13) | copy-start | bytes 1277956
  3.5 5.2 %collective-permute-start.1 = (f32[10,16,256]{2,1,0:T(8,128)}, f32[10,16,256]{2,1,0:T(8,128)S(1)}, u32[]{:S(2)}, u32[]{:S(2)}) collective-permute-start(f32[10,16,256]{2,1,0:T(8,128)} %get-tuple-element.23), channel_id=1, source_target_pairs={{8,16},{24,32},{40,48},{56,64},{72,80},{88,96},{104,112},{120,128}... | collective-permute-start | bytes 491528 | tf_op jit(solution)/shard_map/ppermute | solution.py:421
  8.8 5.0 %copy-start.5 = (s32[1,1,104,128]{3,2,1,0:T(8,128)S(1)}, s32[1,1,104,128]{3,2,1,0:T(8,128)}, u32[]{:S(2)}) copy-start(s32[1,1,104,128]{3,2,1,0:T(8,128)} %param.15) | copy-start | bytes 159748
  9.2 3.4 %copy-start.7 = (s32[1,1,4,2,128]{4,3,2,1,0:T(2,128)S(1)}, s32[1,1,4,2,128]{4,3,2,1,0:T(2,128)}, u32[]{:S(2)}) copy-start(s32[1,1,4,2,128]{4,3,2,1,0:T(2,128)} %param.16) | copy-start | bytes 12292
  9.2 3.4 %copy-start.6 = (s32[1,1,4,2,128]{4,3,2,1,0:T(2,128)S(1)}, s32[1,1,4,2,128]{4,3,2,1,0:T(2,128)}, u32[]{:S(2)}) copy-start(s32[1,1,4,2,128]{4,3,2,1,0:T(2,128)} %param.17) | copy-start | bytes 12292
  9.3 4.0 %collective-permute-start.2 = (f32[4,8,128]{2,1,0:T(8,128)S(1)}, f32[4,8,128]{2,1,0:T(8,128)S(1)}, u32[]{:S(2)}, u32[]{:S(2)}) collective-permute-start(f32[4,8,128]{2,1,0:T(8,128)S(1)} %get-tuple-element.24), channel_id=1, source_target_pairs={{0,1},{2,3},{4,5},{6,7},{8,9},{10,11},{12,13},{14,15},{16,17},{18,... | collective-permute-start | bytes 49160 | tf_op jit(solution)/shard_map/ppermute | solution.py:421
  9.4 4.4 %collective-permute-start.3 = (f32[4,8,128]{2,1,0:T(8,128)S(1)}, f32[4,8,128]{2,1,0:T(8,128)S(1)}, u32[]{:S(2)}, u32[]{:S(2)}) collective-permute-start(f32[4,8,128]{2,1,0:T(8,128)S(1)} %get-tuple-element.25), channel_id=1, source_target_pairs={{1,2},{3,4},{5,6},{9,10},{11,12},{13,14},{17,18},{19,20},{21,22},{... | collective-permute-start | bytes 49160 | tf_op jit(solution)/shard_map/ppermute | solution.py:421
  12.6 0.7 %copy-start.8 = (s32[1,1,4]{2,1,0:T(1,128)S(1)}, s32[1,1,4]{2,1,0:T(1,128)}, u32[]{:S(2)}) copy-start(s32[1,1,4]{2,1,0:T(1,128)} %param.14) | copy-start | bytes 52
  21.4 17.5 %collective-permute-start.5 = (f32[17,8,128]{2,1,0:T(8,128)S(1)}, f32[17,8,128]{2,1,0:T(8,128)S(1)}, u32[]{:S(2)}, u32[]{:S(2)}) collective-permute-start(f32[17,8,128]{2,1,0:T(8,128)S(1)} %get-tuple-element.30), channel_id=1, source_target_pairs={{8,16},{24,32},{40,48},{56,64},{72,80},{88,96},{104,112},{120,128}... | collective-permute-start | bytes 208904 | tf_op jit(solution)/shard_map/ppermute | solution.py:421
  25.5 13.4 %collective-permute-start.6 = (f32[5,8,128]{2,1,0:T(8,128)S(1)}, f32[5,8,128]{2,1,0:T(8,128)S(1)}, u32[]{:S(2)}, u32[]{:S(2)}) collective-permute-start(f32[5,8,128]{2,1,0:T(8,128)S(1)} %get-tuple-element.32), channel_id=1, source_target_pairs={{0,1},{2,3},{4,5},{6,7},{8,9},{10,11},{12,13},{14,15},{16,17},{18,... | collective-permute-start | bytes 61448 | tf_op jit(solution)/shard_map/ppermute | solution.py:421
  29.7 9.2 %collective-permute-start.7 = (f32[5,8,128]{2,1,0:T(8,128)S(1)}, f32[5,8,128]{2,1,0:T(8,128)S(1)}, u32[]{:S(2)}, u32[]{:S(2)}) collective-permute-start(f32[5,8,128]{2,1,0:T(8,128)S(1)} %get-tuple-element.34), channel_id=1, source_target_pairs={{1,2},{3,4},{5,6},{9,10},{11,12},{13,14},{17,18},{19,20},{21,22},{... | collective-permute-start | bytes 61448 | tf_op jit(solution)/shard_map/ppermute | solution.py:421
  33.3 5.6 %collective-permute-start.4 = (f32[17,8,128]{2,1,0:T(8,128)S(1)}, f32[17,8,128]{2,1,0:T(8,128)S(1)}, u32[]{:S(2)}, u32[]{:S(2)}) collective-permute-start(f32[17,8,128]{2,1,0:T(8,128)S(1)} %get-tuple-element.29), channel_id=1, source_target_pairs={{0,8},{16,24},{32,40},{48,56},{64,72},{80,88},{96,104},{112,120},{... | collective-permute-start | bytes 208904 | tf_op jit(solution)/shard_map/ppermute | solution.py:421

commit v5 on v4

--- a/solution.py
+++ b/solution.py
@@ -21,7 +21,7 @@
 KEEP = PB - SENT
 OUT = PB + SENT
 GROUP_SENT = 20
-GROUP_KEEP = 16
+GROUPS_KEEP = (16, 16, 32)
 
 OMEGA_RELAX = 0.8
 VERTICAL = 4.0
@@ -66,38 +66,41 @@
     return lax.rem(lax.axis_index("gx"), 2), lax.rem(lax.axis_index("gy"), 2)
 
 
-def edge_rows_kernel(p_hbm, c_hbm, s_hbm, q_hbm, even_hbm, odd_hbm, p_ref, c_ref, s_ref, q_ref, even_ref, odd_ref, sems):
-    halves = (slice(0, NZ // 2), slice(NZ // 2, NZ))
-    loads = []
-    for h, part in enumerate(halves):
-        pairs = ((p_hbm, p_ref), (c_hbm, c_ref), (s_hbm, s_ref), (q_hbm, q_ref))
-        loads.append([pltpu.make_async_copy(a.at[part], b.at[part], sems.at[h, n]) for n, (a, b) in enumerate(pairs)])
-        for copy in loads[h]:
-            copy.start()
+def edge_of(p, c, s, q, low):
+    step, outer = (-1, 3) if low else (1, 4)
+    weight = jnp.where(index_of((1, 8, CY), 1) == outer, harmonic(c, roll(c, step, 1)), 0.0)
+    rhs = s * p + q + weight * roll(p, step, 1)
+    side = slice(0, 4) if low else slice(4, 8)
+    return jnp.concatenate([p[:, side], c[:, side], (s + weight)[:, side], rhs[:, side]], axis=1)
+
+
+def odd_rows_kernel(p_hbm, c_hbm, s_hbm, q_hbm, odd_ref, p_ref, c_ref, s_ref, q_ref, sems):
     parity = parities()[0]
     within = in_grid("gx")
-    row = index_of((1, 8, CY), 1)
-    stores = []
-    for h, part in enumerate(halves):
-        for copy in loads[h]:
-            copy.wait()
-        pieces = []
-        for start, step, outer in ((0, -1, 3), (8, 1, 4)):
-            tile = slice(start, start + 8)
-            p, c, s, q = (ref[part, tile, :] for ref in (p_ref, c_ref, s_ref, q_ref))
-            weight = jnp.where(row == outer, harmonic(c, roll(c, step, 1)), 0.0)
-            rhs = s * p + q + weight * roll(p, step, 1)
-            side = slice(0, 4) if start == 0 else slice(4, 8)
-            pieces.append(jnp.concatenate([p[:, side], c[:, side], (s + weight)[:, side], rhs[:, side]], axis=1))
-        west, east = pieces
-        even_ref[part] = jnp.where(parity == 0, east, west)
-        odd_ref[part] = jnp.where(within == 0, 0.0, jnp.where(parity == 0, west, east))
-        for n, (a, b) in enumerate(((even_ref, even_hbm), (odd_ref, odd_hbm))):
-            copy = pltpu.make_async_copy(a.at[part], b.at[part], sems.at[h, 4 + n])
+    pairs = ((p_hbm, p_ref), (c_hbm, c_ref), (s_hbm, s_ref), (q_hbm, q_ref))
+    loads = []
+    for h, tile in enumerate((parity, 1 - parity)):
+        rows = pl.ds(pl.multiple_of(8 * tile, 8), 8)
+        for n, (source, ref) in enumerate(pairs):
+            copy = pltpu.make_async_copy(source.at[:, rows, :], ref.at[:, rows, :], sems.at[h, n])
             copy.start()
-            stores.append(copy)
-    for copy in stores:
+            loads.append(copy)
+    for copy in loads[:4]:
         copy.wait()
+    rows = pl.ds(pl.multiple_of(8 * parity, 8), 8)
+    fields = [ref[:, rows, :] for _, ref in pairs]
+    edge = jnp.where(parity == 0, edge_of(*fields, True), edge_of(*fields, False))
+    odd_ref[...] = jnp.where(within == 0, 0.0, edge)
+    for copy in loads[4:]:
+        copy.wait()
+
+
+def even_rows_kernel(p_ref, c_ref, s_ref, q_ref, even_ref):
+    parity = parities()[0]
+    refs = (p_ref, c_ref, s_ref, q_ref)
+    west = edge_of(*(ref[:, 0:8, :] for ref in refs), True)
+    east = edge_of(*(ref[:, 8:16, :] for ref in refs), False)
+    even_ref[...] = jnp.where(parity == 0, east, west)
 
 
 def beside_rows(from_even, from_odd, par_x):
@@ -345,13 +348,13 @@
     head_copy.wait()
 
 
-def rest_kernel(first, tab_ref, rec_ref, cell_ref, *refs):
+def rest_kernel(first, size, tab_ref, rec_ref, cell_ref, *refs):
     kept, found = refs[-2:]
 
     def store(slot, record):
         kept[slot - first] = record
 
-    advance_group(tab_ref, cell_ref, rec_ref, found, first, GROUP_KEEP, store)
+    advance_group(tab_ref, cell_ref, rec_ref, found, first, size, store)
 
 
 def arrive_kernel(small_ref, xe_ref, xo_ref, ye_ref, yo_ref, *refs):
@@ -366,8 +369,10 @@
         copies.append(copy)
 
     send(kept[0], 0, SENT)
-    for n, ref in enumerate(kept[1:]):
-        send(ref, SENT + n * GROUP_KEEP, GROUP_KEEP)
+    first = SENT
+    for ref, size in zip(kept[1:], GROUPS_KEEP):
+        send(ref, first, size)
+        first += size
     for ref, par, base, cap in (
         (xe_ref, 1 - par_x, PB, CAPX),
         (xo_ref, par_x, PB, CAPX),
@@ -438,16 +443,25 @@
     small = jnp.concatenate([river_source.reshape(8, 128), river_target.reshape(8, 128), counts], axis=0)
     grid = (pressure, conductivity, storage, source)
     tile = pltpu.VMEM((NZ, CX, CY), F32)
-    x_even, x_odd = pl.pallas_call(
-        edge_rows_kernel,
-        out_shape=(shape(NZ, CX, CY), shape(NZ, CX, CY)),
+    x_odd, *grid = pl.pallas_call(
+        odd_rows_kernel,
+        out_shape=(shape(NZ, CX, CY),) * 5,
         in_specs=[ANY] * 4,
-        out_specs=(ANY, ANY),
-        scratch_shapes=[tile] * 6 + [pltpu.SemaphoreType.DMA((2, 6))],
-        compiler_params=pltpu.CompilerParams(vmem_limit_bytes=60 << 20),
-        name="edge_rows",
+        out_specs=(VMEM,) * 5,
+        scratch_shapes=[pltpu.SemaphoreType.DMA((2, 4))],
+        compiler_params=pltpu.CompilerParams(vmem_limit_bytes=54400 << 10),
+        name="odd_rows",
     )(*grid)
-    halo_x = exchange(x_even, x_odd, "gx")
+    from_odd = swap(x_odd, "gx", 1)
+    x_even = pl.pallas_call(
+        even_rows_kernel,
+        out_shape=shape(NZ, CX, CY),
+        in_specs=[VMEM] * 4,
+        out_specs=VMEM,
+        compiler_params=LIMIT,
+        name="even_rows",
+    )(*grid)
+    halo_x = (swap(x_even, "gx", 0), from_odd)
     y_even, y_odd = pl.pallas_call(
         edge_lanes_kernel,
         out_shape=(shape(4, 8, 128), shape(4, 8, 128)),
@@ -487,34 +501,36 @@
         compiler_params=LIMIT,
         name="sweep",
     )(small, *grid, *halo_x, *halo_y, records, cells)
-    payloads = [
-        (x_odd, "gx", 1),
-        (y_even, "gy", 0),
-        (y_odd, "gy", 1),
-        (x_even, "gx", 0),
-    ]
-    received = []
+    stages = (
+        (("x_odd", "gx", 1),),
+        (("y_even", "gy", 0),),
+        (("y_odd", "gy", 1), ("x_even", "gx", 0)),
+    )
+    waiting = {"x_odd": x_odd, "y_even": y_even, "y_odd": y_odd, "x_even": x_even}
+    received = {}
     done = [kept]
-    waiting = payloads[0][0]
-    for n, (_, axis, first) in enumerate(payloads):
-        received.append(swap(waiting, axis, first))
-        later = [payloads[n + 1][0]] if n + 1 < len(payloads) else []
+    first = SENT
+    for n, stage in enumerate(stages):
+        for name, axis, parity in stage:
+            received[name] = swap(waiting[name], axis, parity)
+        later = [name for name, _, _ in stages[n + 1]] if n + 1 < len(stages) else []
+        size = GROUPS_KEEP[n]
         outs = pl.pallas_call(
-            functools.partial(rest_kernel, SENT + n * GROUP_KEEP),
-            out_shape=[jax.ShapeDtypeStruct(v.shape, v.dtype) for v in later] + [shape(GROUP_KEEP, 8, 128)],
+            functools.partial(rest_kernel, first, size),
+            out_shape=[jax.ShapeDtypeStruct(waiting[v].shape, F32) for v in later] + [shape(size, 8, 128)],
             in_specs=[VMEM] * (3 + len(later)),
             out_specs=[VMEM] * (1 + len(later)),
-            scratch_shapes=[pltpu.VMEM((TABLE, 128 * GROUP_KEEP), F32)],
-            input_output_aliases={3: 0} if later else {},
+            scratch_shapes=[pltpu.VMEM((TABLE, 128 * size), F32)],
+            input_output_aliases={3 + i: i for i in range(len(later))},
             compiler_params=LIMIT,
             cost_estimate=pl.CostEstimate(
-                flops=2 * TABLE * 512 * 128 * GROUP_KEEP, bytes_accessed=1 << 20, transcendentals=0
+                flops=2 * TABLE * 512 * 128 * size, bytes_accessed=1 << 20, transcendentals=0
             ),
             name=f"rest_{n}",
-        )(table, records, cells, *later)
+        )(table, records, cells, *(waiting[v] for v in later))
         done.append(outs[-1])
-        waiting = outs[0]
-    from_x_odd, from_y_even, from_y_odd, from_x_even = received
+        waiting.update(zip(later, outs))
+        first += size
     moved, inflow = pl.pallas_call(
         arrive_kernel,
         out_shape=(shape(OUT, 8, 128), shape(CX, CY)),
@@ -523,7 +539,7 @@
         scratch_shapes=[pltpu.SemaphoreType.DMA((4 + len(done),))],
         compiler_params=LIMIT,
         name="arrive",
-    )(small, from_x_even, from_x_odd, from_y_even, from_y_odd, *done)
+    )(small, *(received[v] for v in ("x_even", "x_odd", "y_even", "y_odd")), *done)
     return head, moved[None, None], inflow
 
 

time: 40.7 us -> 39.4 us (0.968)
  Pallas kernels: 19.3 us -> 18.4 us
    pallas_call x5, Pallas kernels: 9.74 us -> 8.84 us  [the longest x3 7.46 us: body(): pl.pallas_call(functools.partial(rest_kernel, first, size), out_shape=[ja...]
where the time goes in v5:
time: 39.4 us; the launch traced here: 39.2 us
  Pallas kernels  18.4 us (47%)
  starting transfers between devices  15 us (38%)
  waiting for transfers between devices  4.22 us (11%)
  between operations  0.92 us (2%)
  local copies, waits for them, and re-layouts  0.67 us (2%)
    ppermute x8, starting transfers between devices, swap(): return lax.ppermute(value, AXES, pairs + [(b, a) for a, b in pairs])  15 us
    pallas_call x1, Pallas kernels, body(): pl.pallas_call(sweep_kernel, out_shape=(shape(NZ, CX, CY), shape(TABLE, 2...  7.59 us
    pallas_call x3, Pallas kernels, body(): pl.pallas_call(functools.partial(rest_kernel, first, size), out_shape=[ja...  7.46 us
    ppermute x8, waiting for transfers between devices, swap(): return lax.ppermute(value, AXES, pairs + [(b, a) for a, b in pairs])  4.22 us
    pallas_call x1, Pallas kernels, body(): pl.pallas_call(arrive_kernel, out_shape=(shape(OUT, 8, 128), shape(CX, CY...  1.49 us
    pallas_call x1, Pallas kernels, body(): pl.pallas_call(odd_rows_kernel, out_shape=(shape(NZ, CX, CY),) * 5, in_sp...  1.25 us
  transfers between devices with their start and end apart: 8, of which 2 were waited for; matrix products, arithmetic and copies ran while one was open for 0% of the time, Pallas kernels for 19%

profile of v5, /device:TPU:39, one launch (start us, length us, event | category | flops | bytes accessed | tf_op | source)
XLA Modules:
  0.0 39.2 jit_solution(14718243259518863406)
XLA Ops:
  0.6 1.3 %odd_rows.1 = (f32[10,16,256]{2,1,0:T(8,128)S(1)}, f32[10,16,256]{2,1,0:T(8,128)S(1)}, f32[10,16,256]{2,1,0:T(8,128)S(1)}, f32[10,16,256]{2,1,0:T(8,128)S(1)}, f32[10,16,256]{2,1,0:T(8,128)S(1)}) custom-call(f32[10,16,256]{2,1,0:T(8,128)} %p_hbm.1, f32[10,16,256]{2,1,0:T(8,128)} %c_hbm.1, f32[10,16,256]{2,1,0:T(8,128)} %s_hbm.1, f32[10,16,256]{2,1,0:T(8,128)} %q_hbm.1), custom_call_target="tpu_custom_call" | custom-call | tf_op jit(solution)/shard_map/odd_rows/pallas_call | solution.py:446
  1.9 0.1 even_rows.1
  2.0 0.8 %collective-permute-start = (f32[10,16,256]{2,1,0:T(8,128)S(1)}, f32[10,16,256]{2,1,0:T(8,128)S(1)}, u32[]{:S(2)}, u32[]{:S(2)}) collective-permute-start(f32[10,16,256]{2,1,0:T(8,128)S(1)} %even_rows.1), channel_id=1, source_target_pairs={{0,8},{16,24},{32,40},{48,56},{64,72},{80,88},{96,104},{112,120},{... | collective-permute-start | bytes 491528 | tf_op jit(solution)/shard_map/ppermute | solution.py:426
  2.8 1.3 %collective-permute-start.1 = (f32[10,16,256]{2,1,0:T(8,128)S(1)}, f32[10,16,256]{2,1,0:T(8,128)S(1)}, u32[]{:S(2)}, u32[]{:S(2)}) collective-permute-start(f32[10,16,256]{2,1,0:T(8,128)S(1)} %get-tuple-element.28), channel_id=1, source_target_pairs={{8,16},{24,32},{40,48},{56,64},{72,80},{88,96},{104,112},{120,128}... | collective-permute-start | bytes 491528 | tf_op jit(solution)/shard_map/ppermute | solution.py:426
  4.1 0.0 collective-permute-done.re_ref.rxe_ref
  4.1 3.7 %collective-permute-done.1.ro_ref.rxo_ref = f32[10,16,256]{2,1,0:T(8,128)S(1)} collective-permute-done((f32[10,16,256]{2,1,0:T(8,128)S(1)}, f32[10,16,256]{2,1,0:T(8,128)S(1)}, u32[]{:S(2)}, u32[]{:S(2)}) %collective-permute-start.1) | collective-permute-done | bytes 163872 | tf_op jit(solution)/shard_map/ppermute | solution.py:426
  7.8 0.0 copy-start.1
  7.8 0.4 %edge_lanes.1 = (f32[4,8,128]{2,1,0:T(8,128)S(1)}, f32[4,8,128]{2,1,0:T(8,128)S(1)}) custom-call(f32[10,16,256]{2,1,0:T(8,128)S(1)} %get-tuple-element.24.p_ref, f32[10,16,256]{2,1,0:T(8,128)S(1)} %get-tuple-element.25.c_ref, f32[10,16,256]{2,1,0:T(8,128)S(1)} %get-tuple-element.26.s_ref, f32[10,16,256]{2,1,0:T(8,128)S(1)} %get-tuple-element.27.q_ref, ...), custom_call_target="tpu_custom_call" | custom-call | tf_op jit(solution)/shard_map/edge_lanes/pallas_call | solution.py:465
  8.3 0.0 copy-start.3
  8.3 0.0 copy-start.2
  8.3 0.1 collective-permute-start.2
  8.4 3.3 %collective-permute-start.3 = (f32[4,8,128]{2,1,0:T(8,128)S(1)}, f32[4,8,128]{2,1,0:T(8,128)S(1)}, u32[]{:S(2)}, u32[]{:S(2)}) collective-permute-start(f32[4,8,128]{2,1,0:T(8,128)S(1)} %get-tuple-element.30), channel_id=1, source_target_pairs={{1,2},{3,4},{5,6},{9,10},{11,12},{13,14},{17,18},{19,20},{21,22},{... | collective-permute-start | bytes 49160 | tf_op jit(solution)/shard_map/ppermute | solution.py:426
  11.7 0.0 copy-done.3
  11.7 0.0 copy-done.2
  11.7 0.6 %copy-done.4 = s32[1,1,4]{2,1,0:T(1,128)S(1)} copy-done((s32[1,1,4]{2,1,0:T(1,128)S(1)}, s32[1,1,4]{2,1,0:T(1,128)}, u32[]{:S(2)}) %copy-start.4) | copy-done | bytes 40
  12.3 0.0 collective-permute-done.2.rye_ref
  12.3 0.5 %collective-permute-done.3.ryo_ref = f32[4,8,128]{2,1,0:T(8,128)S(1)} collective-permute-done((f32[4,8,128]{2,1,0:T(8,128)S(1)}, f32[4,8,128]{2,1,0:T(8,128)S(1)}, u32[]{:S(2)}, u32[]{:S(2)}) %collective-permute-start.3) | collective-permute-done | bytes 16416 | tf_op jit(solution)/shard_map/ppermute | solution.py:426
  12.8 0.0 copy-done
  12.8 0.0 copy-done.1
  12.8 7.6 %sweep.1 = (f32[10,16,256]{2,1,0:T(8,128)}, bf16[800,512]{1,0:T(8,128)(2,1)S(1)}, f32[40,8,128]{2,1,0:T(8,128)S(1)}, f32[17,8,128]{2,1,0:T(8,128)S(1)}, f32[17,8...) custom-call(s32[24,128]{1,0:T(8,128)S(1)} %pad_add_fusion.small_ref, ...), custom_call_target="tpu_custom_call" | custom-call | tf_op jit(solution)/shard_map/sweep/pallas_call | solution.py:478
  20.4 2.2 %collective-permute-start.5 = (f32[17,8,128]{2,1,0:T(8,128)S(1)}, f32[17,8,128]{2,1,0:T(8,128)S(1)}, u32[]{:S(2)}, u32[]{:S(2)}) collective-permute-start(f32[17,8,128]{2,1,0:T(8,128)S(1)} %get-tuple-element.36), channel_id=1, source_target_pairs={{8,16},{24,32},{40,48},{56,64},{72,80},{88,96},{104,112},{120,128}... | collective-permute-start | bytes 208904 | tf_op jit(solution)/shard_map/ppermute | solution.py:426
  22.6 1.9 %rest_0.1 = (f32[5,8,128]{2,1,0:T(8,128)S(1)}, f32[16,8,128]{2,1,0:T(8,128)S(1)}) custom-call(bf16[800,512]{1,0:T(8,128)(2,1)S(1)} %get-tuple-element.32.tab_ref, f32[104,8,128]{2,1,0:T(8,128)S(1)} %bitcast.7, s32[104,128]{1,0:T(8,128)S(1)} %bitcast.11, f32[5,8,128]{2,1,0:T(8,128)S(1)} %get-tuple-element.37.refs_0_), custom_call_target="tpu_custom_call", output_to_operand_aliasing={{0}: (3, {})} | custom-call | flops 1677721600 | bytes 1048576 | tf_op jit(solution)/shard_map/rest_0/pallas_call | solution.py:518
  24.5 0.1 collective-permute-start.6
  24.6 1.9 %rest_1.1 = (f32[5,8,128]{2,1,0:T(8,128)S(1)}, f32[17,8,128]{2,1,0:T(8,128)S(1)}, f32[16,8,128]{2,1,0:T(8,128)S(1)}) custom-call(bf16[800,512]{1,0:T(8,128)(2,1)S(1)} %get-tuple-element.32.tab_ref, f32[104,8,128]{2,1,0:T(8,128)S(1)} %bitcast.8, s32[104,128]{1,0:T(8,128)S(1)} %bitcast.12, ...), custom_call_target="tpu_custom_call", output_to_operand_aliasing={{0}: (3, {}), {1}: (4, {})} | custom-call | flops 1677721600 | bytes 1048576 | tf_op jit(solution)/shard_map/rest_1/pallas_call | solution.py:518
  26.6 3.7 %collective-permute-start.7 = (f32[5,8,128]{2,1,0:T(8,128)S(1)}, f32[5,8,128]{2,1,0:T(8,128)S(1)}, u32[]{:S(2)}, u32[]{:S(2)}) collective-permute-start(f32[5,8,128]{2,1,0:T(8,128)S(1)} %get-tuple-element.39), channel_id=1, source_target_pairs={{1,2},{3,4},{5,6},{9,10},{11,12},{13,14},{17,18},{19,20},{21,22},{... | collective-permute-start | bytes 61448 | tf_op jit(solution)/shard_map/ppermute | solution.py:426
  30.2 3.6 %collective-permute-start.4 = (f32[17,8,128]{2,1,0:T(8,128)S(1)}, f32[17,8,128]{2,1,0:T(8,128)S(1)}, u32[]{:S(2)}, u32[]{:S(2)}) collective-permute-start(f32[17,8,128]{2,1,0:T(8,128)S(1)} %get-tuple-element.35), channel_id=1, source_target_pairs={{0,8},{16,24},{32,40},{48,56},{64,72},{80,88},{96,104},{112,120},{... | collective-permute-start | bytes 208904 | tf_op jit(solution)/shard_map/ppermute | solution.py:426
  33.8 3.6 %rest_2.1.refs_3_ = f32[32,8,128]{2,1,0:T(8,128)S(1)} custom-call(bf16[800,512]{1,0:T(8,128)(2,1)S(1)} %get-tuple-element.32.tab_ref, f32[104,8,128]{2,1,0:T(8,128)S(1)} %bitcast.9, s32[104,128]{1,0:T(8,128)S(1)} %bitcast.13), custom_call_target="tpu_custom_call" | custom-call | flops 3355443200 | bytes 1048576 | tf_op jit(solution)/shard_map/rest_2/pallas_call | solution.py:518
  37.5 0.0 collective-permute-done.6.ye_ref
  37.5 0.0 collective-permute-done.7.yo_ref
  37.5 0.0 collective-permute-done.5.xo_ref
  37.5 0.0 collective-permute-done.4.xe_ref
  37.5 1.5 %arrive.1 = (f32[144,8,128]{2,1,0:T(8,128)}, f32[16,256]{1,0:T(8,128)}) custom-call(s32[24,128]{1,0:T(8,128)S(1)} %pad_add_fusion.small_ref, f32[17,8,128]{2,1,0:T(8,128)S(1)} %collective-permute-done.4.xe_ref, f32[17,8,128]{2,1,0:T(8,128)S(1)} %collective-permute-done.5.xo_ref, f32[5,8,128]{2,1,0:T(8,128)S(1)} %collective-permute-done.6.ye_ref, ...), custom_call_target="tpu_custom_call" | custom-call | tf_op jit(solution)/shard_map/arrive/pallas_call | solution.py:534
  (3 shorter events, 0.0 us)
Async XLA Ops:
  2.0 2.1 %collective-permute-start = (f32[10,16,256]{2,1,0:T(8,128)S(1)}, f32[10,16,256]{2,1,0:T(8,128)S(1)}, u32[]{:S(2)}, u32[]{:S(2)}) collective-permute-start(f32[10,16,256]{2,1,0:T(8,128)S(1)} %even_rows.1), channel_id=1, source_target_pairs={{0,8},{16,24},{32,40},{48,56},{64,72},{80,88},{96,104},{112,120},{... | collective-permute-start | bytes 491528 | tf_op jit(solution)/shard_map/ppermute | solution.py:426
  2.8 10.0 %copy-start = (f32[1,1,104,8,128]{4,3,2,1,0:T(8,128)S(1)}, f32[1,1,104,8,128]{4,3,2,1,0:T(8,128)}, u32[]{:S(2)}) copy-start(f32[1,1,104,8,128]{4,3,2,1,0:T(8,128)} %param.13) | copy-start | bytes 1277956
  2.8 5.0 %collective-permute-start.1 = (f32[10,16,256]{2,1,0:T(8,128)S(1)}, f32[10,16,256]{2,1,0:T(8,128)S(1)}, u32[]{:S(2)}, u32[]{:S(2)}) collective-permute-start(f32[10,16,256]{2,1,0:T(8,128)S(1)} %get-tuple-element.28), channel_id=1, source_target_pairs={{8,16},{24,32},{40,48},{56,64},{72,80},{88,96},{104,112},{120,128}... | collective-permute-start | bytes 491528 | tf_op jit(solution)/shard_map/ppermute | solution.py:426
  7.8 5.0 %copy-start.1 = (s32[1,1,104,128]{3,2,1,0:T(8,128)S(1)}, s32[1,1,104,128]{3,2,1,0:T(8,128)}, u32[]{:S(2)}) copy-start(s32[1,1,104,128]{3,2,1,0:T(8,128)} %param.15) | copy-start | bytes 159748
  8.3 3.4 %copy-start.3 = (s32[1,1,4,2,128]{4,3,2,1,0:T(2,128)S(1)}, s32[1,1,4,2,128]{4,3,2,1,0:T(2,128)}, u32[]{:S(2)}) copy-start(s32[1,1,4,2,128]{4,3,2,1,0:T(2,128)} %param.16) | copy-start | bytes 12292
  8.3 3.4 %copy-start.2 = (s32[1,1,4,2,128]{4,3,2,1,0:T(2,128)S(1)}, s32[1,1,4,2,128]{4,3,2,1,0:T(2,128)}, u32[]{:S(2)}) copy-start(s32[1,1,4,2,128]{4,3,2,1,0:T(2,128)} %param.17) | copy-start | bytes 12292
  8.3 4.0 %collective-permute-start.2 = (f32[4,8,128]{2,1,0:T(8,128)S(1)}, f32[4,8,128]{2,1,0:T(8,128)S(1)}, u32[]{:S(2)}, u32[]{:S(2)}) collective-permute-start(f32[4,8,128]{2,1,0:T(8,128)S(1)} %get-tuple-element.29), channel_id=1, source_target_pairs={{0,1},{2,3},{4,5},{6,7},{8,9},{10,11},{12,13},{14,15},{16,17},{18,... | collective-permute-start | bytes 49160 | tf_op jit(solution)/shard_map/ppermute | solution.py:426
  8.4 4.4 %collective-permute-start.3 = (f32[4,8,128]{2,1,0:T(8,128)S(1)}, f32[4,8,128]{2,1,0:T(8,128)S(1)}, u32[]{:S(2)}, u32[]{:S(2)}) collective-permute-start(f32[4,8,128]{2,1,0:T(8,128)S(1)} %get-tuple-element.30), channel_id=1, source_target_pairs={{1,2},{3,4},{5,6},{9,10},{11,12},{13,14},{17,18},{19,20},{21,22},{... | collective-permute-start | bytes 49160 | tf_op jit(solution)/shard_map/ppermute | solution.py:426
  11.7 0.7 %copy-start.4 = (s32[1,1,4]{2,1,0:T(1,128)S(1)}, s32[1,1,4]{2,1,0:T(1,128)}, u32[]{:S(2)}) copy-start(s32[1,1,4]{2,1,0:T(1,128)} %param.14) | copy-start | bytes 52
  20.4 17.1 %collective-permute-start.5 = (f32[17,8,128]{2,1,0:T(8,128)S(1)}, f32[17,8,128]{2,1,0:T(8,128)S(1)}, u32[]{:S(2)}, u32[]{:S(2)}) collective-permute-start(f32[17,8,128]{2,1,0:T(8,128)S(1)} %get-tuple-element.36), channel_id=1, source_target_pairs={{8,16},{24,32},{40,48},{56,64},{72,80},{88,96},{104,112},{120,128}... | collective-permute-start | bytes 208904 | tf_op jit(solution)/shard_map/ppermute | solution.py:426
  24.5 13.0 %collective-permute-start.6 = (f32[5,8,128]{2,1,0:T(8,128)S(1)}, f32[5,8,128]{2,1,0:T(8,128)S(1)}, u32[]{:S(2)}, u32[]{:S(2)}) collective-permute-start(f32[5,8,128]{2,1,0:T(8,128)S(1)} %get-tuple-element.38), channel_id=1, source_target_pairs={{0,1},{2,3},{4,5},{6,7},{8,9},{10,11},{12,13},{14,15},{16,17},{18,... | collective-permute-start | bytes 61448 | tf_op jit(solution)/shard_map/ppermute | solution.py:426
  26.6 10.9 %collective-permute-start.7 = (f32[5,8,128]{2,1,0:T(8,128)S(1)}, f32[5,8,128]{2,1,0:T(8,128)S(1)}, u32[]{:S(2)}, u32[]{:S(2)}) collective-permute-start(f32[5,8,128]{2,1,0:T(8,128)S(1)} %get-tuple-element.39), channel_id=1, source_target_pairs={{1,2},{3,4},{5,6},{9,10},{11,12},{13,14},{17,18},{19,20},{21,22},{... | collective-permute-start | bytes 61448 | tf_op jit(solution)/shard_map/ppermute | solution.py:426
  30.2 7.3 %collective-permute-start.4 = (f32[17,8,128]{2,1,0:T(8,128)S(1)}, f32[17,8,128]{2,1,0:T(8,128)S(1)}, u32[]{:S(2)}, u32[]{:S(2)}) collective-permute-start(f32[17,8,128]{2,1,0:T(8,128)S(1)} %get-tuple-element.35), channel_id=1, source_target_pairs={{0,8},{16,24},{32,40},{48,56},{64,72},{80,88},{96,104},{112,120},{... | collective-permute-start | bytes 208904 | tf_op jit(solution)/shard_map/ppermute | solution.py:426

commit v6 on v5

--- a/solution.py
+++ b/solution.py
@@ -9,6 +9,7 @@
 
 F32 = jnp.float32
 BF16 = jnp.bfloat16
+F8 = jnp.float8_e4m3fn
 
 ITERS = 4
 CAPX = 16
@@ -20,8 +21,8 @@
 SENT = 2 * CAPX + 2 * CAPY
 KEEP = PB - SENT
 OUT = PB + SENT
-GROUP_SENT = 20
-GROUPS_KEEP = (16, 16, 32)
+GROUP_SENT = 40
+GROUPS_KEEP = (64,)
 
 OMEGA_RELAX = 0.8
 VERTICAL = 4.0
@@ -42,6 +43,12 @@
 LEVEL = 496
 SATUR = 640
 TABLE = 800
+
+PARTS = 3
+STEP_DOWN = 0.0625
+SIDE_SCALE = 0.5
+LEVEL_SCALE = 0.125
+SATUR_SCALE = 256.0
 
 
 def harmonic(left, right):
@@ -152,7 +159,8 @@
 def sample(tab_ref, cells, found_ref):
     lanes = cells.shape[1]
     hot = one_hot(cells & (CY - 1), lanes)
-    found_ref[...] = jnp.dot(tab_ref[...], jnp.concatenate([hot, hot], 0), preferred_element_type=F32)
+    hot = jnp.concatenate([(hot * jnp.asarray(STEP_DOWN**n, BF16)).astype(F8) for n in range(PARTS)], axis=0)
+    found_ref[...] = jnp.dot(tab_ref[...], hot, preferred_element_type=F32)
     high = cells >> 8
     column = high & (CX - 1)
     west_row = jnp.where(column == 0, NZ * CX + (high >> 4), high - 1)
@@ -180,7 +188,9 @@
     def pick(mask, rows):
         return jnp.sum(jnp.where(mask, rows, 0.0), axis=0, keepdims=True)
 
-    return [pick(other, west)] + [pick(own, v) for v in (east, south, north, bottom, top, satur)]
+    values = [(other, west), (own, east), (own, south), (own, north), (own, bottom), (own, top), (own, satur)]
+    scales = [SIDE_SCALE] * 4 + [LEVEL_SCALE] * 2 + [SATUR_SCALE]
+    return [pick(mask, v) * (1.0 / scale) for (mask, v), scale in zip(values, scales)]
 
 
 def advance(record, sampled):
@@ -293,19 +303,21 @@
                 flat[first + CX * k : first + CX * k + CX, lanes] = value
 
             final[k, :, lanes] = h[j]
-            put(EAST, -wx[k, j, OWN, :] * (old[k, j, 13 : 13 + CX, :] - h[j]))
-            flat[NZ * CX + k : NZ * CX + k + 1, lanes] = -wx[k, j, 11:12, :] * (h[j][0:1] - old[k, j, 11:12, :])
-            put(NORTH, -wy[k, j, INNER, :] * (after[j] - h[j]))
-            put(SOUTH, -wy_back[k, j, INNER, :] * (h[j] - before[j]))
+            put(EAST, -SIDE_SCALE * wx[k, j, OWN, :] * (old[k, j, 13 : 13 + CX, :] - h[j]))
+            flat[NZ * CX + k : NZ * CX + k + 1, lanes] = -SIDE_SCALE * wx[k, j, 11:12, :] * (h[j][0:1] - old[k, j, 11:12, :])
+            put(NORTH, -SIDE_SCALE * wy[k, j, INNER, :] * (after[j] - h[j]))
+            put(SOUTH, -SIDE_SCALE * wy_back[k, j, INNER, :] * (h[j] - before[j]))
             if k < NZ - 1:
-                put(LEVEL, -wz[k, j, INNER, :] * (old[k + 1, j, OWN, :] - h[j] + 1.0))
+                put(LEVEL, -LEVEL_SCALE * wz[k, j, INNER, :] * (old[k + 1, j, OWN, :] - h[j] + 1.0))
             suction = jnp.maximum(-h[j], 0.0)
-            put(SATUR, RESIDUAL_SAT + (1.0 - RESIDUAL_SAT) * lax.rsqrt(1.0 + suction * suction))
+            put(SATUR, SATUR_SCALE * (RESIDUAL_SAT + (1.0 - RESIDUAL_SAT) * lax.rsqrt(1.0 + suction * suction)))
     head_copy = pltpu.make_async_copy(final, head_ref, sem)
     head_copy.start()
-    coarse, fine = split(flat[...], 2)
-    tab_ref[:, 0:CY] = coarse
-    tab_ref[:, CY : 2 * CY] = fine
+    rest = flat[...]
+    for n in range(PARTS):
+        piece = rest.astype(F8)
+        tab_ref[:, CY * n : CY * n + CY] = piece
+        rest = (rest - piece.astype(F32)) * (1.0 / STEP_DOWN)
     counts = small_ref[16:17, :]
     first = 0
     for d, cap in enumerate((CAPX, CAPX, CAPY, CAPY)):
@@ -401,7 +413,7 @@
 
 VMEM = pl.BlockSpec(memory_space=pltpu.VMEM)
 ANY = pl.BlockSpec(memory_space=pl.ANY)
-LIMIT = pltpu.CompilerParams(vmem_limit_bytes=32 << 20)
+LIMIT = pltpu.CompilerParams(vmem_limit_bytes=44 << 20)
 
 
 AXES = ("gx", "gy")
@@ -479,7 +491,7 @@
         sweep_kernel,
         out_shape=(
             shape(NZ, CX, CY),
-            shape(TABLE, 2 * CY, dtype=BF16),
+            shape(TABLE, PARTS * CY, dtype=F8),
             shape(SENT, 8, 128),
             shape(CAPX + 1, 8, 128),
             shape(CAPX + 1, 8, 128),
@@ -501,11 +513,7 @@
         compiler_params=LIMIT,
         name="sweep",
     )(small, *grid, *halo_x, *halo_y, records, cells)
-    stages = (
-        (("x_odd", "gx", 1),),
-        (("y_even", "gy", 0),),
-        (("y_odd", "gy", 1), ("x_even", "gx", 0)),
-    )
+    stages = ((("x_odd", "gx", 1), ("y_even", "gy", 0), ("y_odd", "gy", 1), ("x_even", "gx", 0)),)
     waiting = {"x_odd": x_odd, "y_even": y_even, "y_odd": y_odd, "x_even": x_even}
     received = {}
     done = [kept]

time: 39.4 us -> 35.4 us (0.90)
  the two profiles are of different devices: /device:TPU:39 before, /device:TPU:38 now
where the time goes in v6:
time: 35.4 us; the launch traced here: 35.2 us
  Pallas kernels  15.8 us (45%)
  starting transfers between devices  13.2 us (37%)
  waiting for transfers between devices  4.63 us (13%)
  between operations  0.91 us (3%)
  local copies, waits for them, and re-layouts  0.67 us (2%)
    ppermute x8, starting transfers between devices, swap(): return lax.ppermute(value, AXES, pairs + [(b, a) for a, b in pairs])  13.2 us
    pallas_call x1, Pallas kernels, body(): pl.pallas_call(functools.partial(rest_kernel, first, size), out_shape=[ja...  6.45 us
    pallas_call x1, Pallas kernels, body(): pl.pallas_call(sweep_kernel, out_shape=(shape(NZ, CX, CY), shape(TABLE, P...  6.07 us
    ppermute x8, waiting for transfers between devices, swap(): return lax.ppermute(value, AXES, pairs + [(b, a) for a, b in pairs])  4.63 us
    pallas_call x1, Pallas kernels, body(): pl.pallas_call(arrive_kernel, out_shape=(shape(OUT, 8, 128), shape(CX, CY...  1.47 us
    pallas_call x1, Pallas kernels, body(): pl.pallas_call(odd_rows_kernel, out_shape=(shape(NZ, CX, CY),) * 5, in_sp...  1.25 us
  transfers between devices with their start and end apart: 8, of which 2 were waited for; matrix products, arithmetic and copies ran while one was open for 0% of the time, Pallas kernels for 18%

profile of v6, /device:TPU:38, one launch (start us, length us, event | category | flops | bytes accessed | tf_op | source)
XLA Modules:
  0.0 35.2 jit_solution(4531062232969179720)
XLA Ops:
  0.6 1.3 %odd_rows.1 = (f32[10,16,256]{2,1,0:T(8,128)S(1)}, f32[10,16,256]{2,1,0:T(8,128)S(1)}, f32[10,16,256]{2,1,0:T(8,128)S(1)}, f32[10,16,256]{2,1,0:T(8,128)S(1)}, f32[10,16,256]{2,1,0:T(8,128)S(1)}) custom-call(f32[10,16,256]{2,1,0:T(8,128)} %p_hbm.1, f32[10,16,256]{2,1,0:T(8,128)} %c_hbm.1, f32[10,16,256]{2,1,0:T(8,128)} %s_hbm.1, f32[10,16,256]{2,1,0:T(8,128)} %q_hbm.1), custom_call_target="tpu_custom_call" | custom-call | tf_op jit(solution)/shard_map/odd_rows/pallas_call | solution.py:458
  1.9 0.1 even_rows.1
  2.0 0.1 collective-permute-start
  2.1 0.0 copy-start
  2.1 3.4 %collective-permute-start.1 = (f32[10,16,256]{2,1,0:T(8,128)S(1)}, f32[10,16,256]{2,1,0:T(8,128)S(1)}, u32[]{:S(2)}, u32[]{:S(2)}) collective-permute-start(f32[10,16,256]{2,1,0:T(8,128)S(1)} %get-tuple-element.23), channel_id=1, source_target_pairs={{8,16},{24,32},{40,48},{56,64},{72,80},{88,96},{104,112},{120,128}... | collective-permute-start | bytes 491528 | tf_op jit(solution)/shard_map/ppermute | solution.py:438
  5.5 0.0 collective-permute-done.re_ref.rxe_ref
  5.5 3.6 %collective-permute-done.1.ro_ref.rxo_ref = f32[10,16,256]{2,1,0:T(8,128)S(1)} collective-permute-done((f32[10,16,256]{2,1,0:T(8,128)S(1)}, f32[10,16,256]{2,1,0:T(8,128)S(1)}, u32[]{:S(2)}, u32[]{:S(2)}) %collective-permute-start.1) | collective-permute-done | bytes 163872 | tf_op jit(solution)/shard_map/ppermute | solution.py:438
  9.1 0.0 copy-start.1
  9.1 0.4 %edge_lanes.1 = (f32[4,8,128]{2,1,0:T(8,128)S(1)}, f32[4,8,128]{2,1,0:T(8,128)S(1)}) custom-call(f32[10,16,256]{2,1,0:T(8,128)S(1)} %get-tuple-element.19.p_ref, f32[10,16,256]{2,1,0:T(8,128)S(1)} %get-tuple-element.20.c_ref, f32[10,16,256]{2,1,0:T(8,128)S(1)} %get-tuple-element.21.s_ref, f32[10,16,256]{2,1,0:T(8,128)S(1)} %get-tuple-element.22.q_ref, ...), custom_call_target="tpu_custom_call" | custom-call | tf_op jit(solution)/shard_map/edge_lanes/pallas_call | solution.py:477
  9.5 0.0 copy-start.3
  9.5 0.0 copy-start.2
  9.5 0.2 collective-permute-start.2
  9.7 3.7 %collective-permute-start.3 = (f32[4,8,128]{2,1,0:T(8,128)S(1)}, f32[4,8,128]{2,1,0:T(8,128)S(1)}, u32[]{:S(2)}, u32[]{:S(2)}) collective-permute-start(f32[4,8,128]{2,1,0:T(8,128)S(1)} %get-tuple-element.25), channel_id=1, source_target_pairs={{1,2},{3,4},{5,6},{9,10},{11,12},{13,14},{17,18},{19,20},{21,22},{... | collective-permute-start | bytes 49160 | tf_op jit(solution)/shard_map/ppermute | solution.py:438
  13.5 0.0 copy-start.4
  13.5 0.0 copy-done.3
  13.5 0.0 copy-done.2
  13.5 0.6 %copy-done.4 = s32[1,1,4]{2,1,0:T(1,128)S(1)} copy-done((s32[1,1,4]{2,1,0:T(1,128)S(1)}, s32[1,1,4]{2,1,0:T(1,128)}, u32[]{:S(2)}) %copy-start.4) | copy-done | bytes 40
  14.1 0.0 collective-permute-done.2.rye_ref
  14.1 1.0 %collective-permute-done.3.ryo_ref = f32[4,8,128]{2,1,0:T(8,128)S(1)} collective-permute-done((f32[4,8,128]{2,1,0:T(8,128)S(1)}, f32[4,8,128]{2,1,0:T(8,128)S(1)}, u32[]{:S(2)}, u32[]{:S(2)}) %collective-permute-start.3) | collective-permute-done | bytes 16416 | tf_op jit(solution)/shard_map/ppermute | solution.py:438
  15.2 0.0 copy-done
  15.2 0.0 copy-done.1
  15.2 6.1 %sweep.1 = (f32[10,16,256]{2,1,0:T(8,128)}, f8e4m3fn[800,768]{1,0:T(32,128)(4,1)S(1)}, f32[40,8,128]{2,1,0:T(8,128)S(1)}, f32[17,8,128]{2,1,0:T(8,128)S(1)}, f32...) custom-call(s32[24,128]{1,0:T(8,128)S(1)} %pad_add_fusion.small_ref, ...), custom_call_target="tpu_custom_call" | custom-call | tf_op jit(solution)/shard_map/sweep/pallas_call | solution.py:490
  21.3 0.1 collective-permute-start.6
  21.4 4.1 %collective-permute-start.7 = (f32[5,8,128]{2,1,0:T(8,128)S(1)}, f32[5,8,128]{2,1,0:T(8,128)S(1)}, u32[]{:S(2)}, u32[]{:S(2)}) collective-permute-start(f32[5,8,128]{2,1,0:T(8,128)S(1)} %get-tuple-element.30), channel_id=1, source_target_pairs={{1,2},{3,4},{5,6},{9,10},{11,12},{13,14},{17,18},{19,20},{21,22},{... | collective-permute-start | bytes 61448 | tf_op jit(solution)/shard_map/ppermute | solution.py:438
  25.5 0.0 collective-permute-start.4
  25.5 1.6 %collective-permute-start.5 = (f32[17,8,128]{2,1,0:T(8,128)S(1)}, f32[17,8,128]{2,1,0:T(8,128)S(1)}, u32[]{:S(2)}, u32[]{:S(2)}) collective-permute-start(f32[17,8,128]{2,1,0:T(8,128)S(1)} %get-tuple-element.28), channel_id=1, source_target_pairs={{8,16},{24,32},{40,48},{56,64},{72,80},{88,96},{104,112},{120,128}... | collective-permute-start | bytes 208904 | tf_op jit(solution)/shard_map/ppermute | solution.py:438
  27.1 6.5 %rest_0.1.refs_1_ = f32[64,8,128]{2,1,0:T(8,128)S(1)} custom-call(f8e4m3fn[800,768]{1,0:T(32,128)(4,1)S(1)} %get-tuple-element.32.tab_ref, f32[104,8,128]{2,1,0:T(8,128)S(1)} %bitcast.7, s32[104,128]{1,0:T(8,128)S(1)} %bitcast.9), custom_call_target="tpu_custom_call" | custom-call | flops 6710886400 | bytes 1048576 | tf_op jit(solution)/shard_map/rest_0/pallas_call | solution.py:526
  33.6 0.0 collective-permute-done.6.ye_ref
  33.6 0.0 collective-permute-done.7.yo_ref
  33.6 0.0 collective-permute-done.4.xe_ref
  33.6 0.0 collective-permute-done.5.xo_ref
  33.6 1.5 %arrive.1 = (f32[144,8,128]{2,1,0:T(8,128)}, f32[16,256]{1,0:T(8,128)}) custom-call(s32[24,128]{1,0:T(8,128)S(1)} %pad_add_fusion.small_ref, f32[17,8,128]{2,1,0:T(8,128)S(1)} %collective-permute-done.4.xe_ref, f32[17,8,128]{2,1,0:T(8,128)S(1)} %collective-permute-done.5.xo_ref, f32[5,8,128]{2,1,0:T(8,128)S(1)} %collective-permute-done.6.ye_ref, ...), custom_call_target="tpu_custom_call" | custom-call | tf_op jit(solution)/shard_map/arrive/pallas_call | solution.py:542
  (1 shorter events, 0.0 us)
Async XLA Ops:
  2.0 3.5 %collective-permute-start = (f32[10,16,256]{2,1,0:T(8,128)S(1)}, f32[10,16,256]{2,1,0:T(8,128)S(1)}, u32[]{:S(2)}, u32[]{:S(2)}) collective-permute-start(f32[10,16,256]{2,1,0:T(8,128)S(1)} %even_rows.1), channel_id=1, source_target_pairs={{0,8},{16,24},{32,40},{48,56},{64,72},{80,88},{96,104},{112,120},{... | collective-permute-start | bytes 491528 | tf_op jit(solution)/shard_map/ppermute | solution.py:438
  2.1 13.1 %copy-start = (f32[1,1,104,8,128]{4,3,2,1,0:T(8,128)S(1)}, f32[1,1,104,8,128]{4,3,2,1,0:T(8,128)}, u32[]{:S(2)}) copy-start(f32[1,1,104,8,128]{4,3,2,1,0:T(8,128)} %param.13) | copy-start | bytes 1277956
  2.1 6.9 %collective-permute-start.1 = (f32[10,16,256]{2,1,0:T(8,128)S(1)}, f32[10,16,256]{2,1,0:T(8,128)S(1)}, u32[]{:S(2)}, u32[]{:S(2)}) collective-permute-start(f32[10,16,256]{2,1,0:T(8,128)S(1)} %get-tuple-element.23), channel_id=1, source_target_pairs={{8,16},{24,32},{40,48},{56,64},{72,80},{88,96},{104,112},{120,128}... | collective-permute-start | bytes 491528 | tf_op jit(solution)/shard_map/ppermute | solution.py:438
  9.1 6.1 %copy-start.1 = (s32[1,1,104,128]{3,2,1,0:T(8,128)S(1)}, s32[1,1,104,128]{3,2,1,0:T(8,128)}, u32[]{:S(2)}) copy-start(s32[1,1,104,128]{3,2,1,0:T(8,128)} %param.15) | copy-start | bytes 159748
  9.5 3.9 %copy-start.3 = (s32[1,1,4,2,128]{4,3,2,1,0:T(2,128)S(1)}, s32[1,1,4,2,128]{4,3,2,1,0:T(2,128)}, u32[]{:S(2)}) copy-start(s32[1,1,4,2,128]{4,3,2,1,0:T(2,128)} %param.16) | copy-start | bytes 12292
  9.5 3.9 %copy-start.2 = (s32[1,1,4,2,128]{4,3,2,1,0:T(2,128)S(1)}, s32[1,1,4,2,128]{4,3,2,1,0:T(2,128)}, u32[]{:S(2)}) copy-start(s32[1,1,4,2,128]{4,3,2,1,0:T(2,128)} %param.17) | copy-start | bytes 12292
  9.5 4.6 %collective-permute-start.2 = (f32[4,8,128]{2,1,0:T(8,128)S(1)}, f32[4,8,128]{2,1,0:T(8,128)S(1)}, u32[]{:S(2)}, u32[]{:S(2)}) collective-permute-start(f32[4,8,128]{2,1,0:T(8,128)S(1)} %get-tuple-element.24), channel_id=1, source_target_pairs={{0,1},{2,3},{4,5},{6,7},{8,9},{10,11},{12,13},{14,15},{16,17},{18,... | collective-permute-start | bytes 49160 | tf_op jit(solution)/shard_map/ppermute | solution.py:438
  9.7 5.4 %collective-permute-start.3 = (f32[4,8,128]{2,1,0:T(8,128)S(1)}, f32[4,8,128]{2,1,0:T(8,128)S(1)}, u32[]{:S(2)}, u32[]{:S(2)}) collective-permute-start(f32[4,8,128]{2,1,0:T(8,128)S(1)} %get-tuple-element.25), channel_id=1, source_target_pairs={{1,2},{3,4},{5,6},{9,10},{11,12},{13,14},{17,18},{19,20},{21,22},{... | collective-permute-start | bytes 49160 | tf_op jit(solution)/shard_map/ppermute | solution.py:438
  13.5 0.7 %copy-start.4 = (s32[1,1,4]{2,1,0:T(1,128)S(1)}, s32[1,1,4]{2,1,0:T(1,128)}, u32[]{:S(2)}) copy-start(s32[1,1,4]{2,1,0:T(1,128)} %param.14) | copy-start | bytes 52
  21.3 12.3 %collective-permute-start.6 = (f32[5,8,128]{2,1,0:T(8,128)S(1)}, f32[5,8,128]{2,1,0:T(8,128)S(1)}, u32[]{:S(2)}, u32[]{:S(2)}) collective-permute-start(f32[5,8,128]{2,1,0:T(8,128)S(1)} %get-tuple-element.29), channel_id=1, source_target_pairs={{0,1},{2,3},{4,5},{6,7},{8,9},{10,11},{12,13},{14,15},{16,17},{18,... | collective-permute-start | bytes 61448 | tf_op jit(solution)/shard_map/ppermute | solution.py:438
  21.4 12.2 %collective-permute-start.7 = (f32[5,8,128]{2,1,0:T(8,128)S(1)}, f32[5,8,128]{2,1,0:T(8,128)S(1)}, u32[]{:S(2)}, u32[]{:S(2)}) collective-permute-start(f32[5,8,128]{2,1,0:T(8,128)S(1)} %get-tuple-element.30), channel_id=1, source_target_pairs={{1,2},{3,4},{5,6},{9,10},{11,12},{13,14},{17,18},{19,20},{21,22},{... | collective-permute-start | bytes 61448 | tf_op jit(solution)/shard_map/ppermute | solution.py:438
  25.5 8.1 %collective-permute-start.4 = (f32[17,8,128]{2,1,0:T(8,128)S(1)}, f32[17,8,128]{2,1,0:T(8,128)S(1)}, u32[]{:S(2)}, u32[]{:S(2)}) collective-permute-start(f32[17,8,128]{2,1,0:T(8,128)S(1)} %get-tuple-element.27), channel_id=1, source_target_pairs={{0,8},{16,24},{32,40},{48,56},{64,72},{80,88},{96,104},{112,120},{... | collective-permute-start | bytes 208904 | tf_op jit(solution)/shard_map/ppermute | solution.py:438
  25.5 8.1 %collective-permute-start.5 = (f32[17,8,128]{2,1,0:T(8,128)S(1)}, f32[17,8,128]{2,1,0:T(8,128)S(1)}, u32[]{:S(2)}, u32[]{:S(2)}) collective-permute-start(f32[17,8,128]{2,1,0:T(8,128)S(1)} %get-tuple-element.28), channel_id=1, source_target_pairs={{8,16},{24,32},{40,48},{56,64},{72,80},{88,96},{104,112},{120,128}... | collective-permute-start | bytes 208904 | tf_op jit(solution)/shard_map/ppermute | solution.py:438

commit v7 on v6

--- a/solution.py
+++ b/solution.py
@@ -360,8 +360,10 @@
     head_copy.wait()
 
 
-def rest_kernel(first, size, tab_ref, rec_ref, cell_ref, *refs):
-    kept, found = refs[-2:]
+def rest_kernel(first, size, tab_ref, rec_ref, cell_ref, small_ref, *refs):
+    kept, hot_ref, found = refs[-3:]
+    links = jnp.concatenate([small_ref[j : j + 1, :] for j in range(8, 16)], axis=1)
+    hot_ref[...] = one_hot(links & (CY - 1), 1024)
 
     def store(slot, record):
         kept[slot - first] = record
@@ -369,7 +371,7 @@
     advance_group(tab_ref, cell_ref, rec_ref, found, first, size, store)
 
 
-def arrive_kernel(small_ref, xe_ref, xo_ref, ye_ref, yo_ref, *refs):
+def arrive_kernel(small_ref, hot_ref, xe_ref, xo_ref, ye_ref, yo_ref, *refs):
     kept = refs[:-3]
     next_ref, inflow_ref, sems = refs[-3:]
     par_x, par_y = parities()
@@ -404,8 +406,7 @@
     links = jnp.concatenate([small_ref[j : j + 1, :] for j in range(8, 16)], axis=1)
     spread = jnp.where(index_of((CX, 1024), 0) == (links >> 8), flow, 0.0)
     parts = jnp.concatenate(split(spread, 3), axis=0)
-    hot = one_hot(links & (CY - 1), 1024)
-    total = lax.dot_general(parts, hot, (((1,), (1,)), ((), ())), preferred_element_type=F32)
+    total = lax.dot_general(parts, hot_ref[...], (((1,), (1,)), ((), ())), preferred_element_type=F32)
     inflow_ref[...] = total[0:CX] + total[CX : 2 * CX] + total[2 * CX : 3 * CX]
     for copy in copies:
         copy.wait()
@@ -525,29 +526,30 @@
         size = GROUPS_KEEP[n]
         outs = pl.pallas_call(
             functools.partial(rest_kernel, first, size),
-            out_shape=[jax.ShapeDtypeStruct(waiting[v].shape, F32) for v in later] + [shape(size, 8, 128)],
-            in_specs=[VMEM] * (3 + len(later)),
-            out_specs=[VMEM] * (1 + len(later)),
+            out_shape=[jax.ShapeDtypeStruct(waiting[v].shape, F32) for v in later] + [shape(size, 8, 128), shape(CY, 1024, dtype=BF16)],
+            in_specs=[VMEM] * (4 + len(later)),
+            out_specs=[VMEM] * (2 + len(later)),
             scratch_shapes=[pltpu.VMEM((TABLE, 128 * size), F32)],
-            input_output_aliases={3 + i: i for i in range(len(later))},
+            input_output_aliases={4 + i: i for i in range(len(later))},
             compiler_params=LIMIT,
             cost_estimate=pl.CostEstimate(
                 flops=2 * TABLE * 512 * 128 * size, bytes_accessed=1 << 20, transcendentals=0
             ),
             name=f"rest_{n}",
-        )(table, records, cells, *(waiting[v] for v in later))
-        done.append(outs[-1])
+        )(table, records, cells, small, *(waiting[v] for v in later))
+        done.append(outs[-2])
+        hot = outs[-1]
         waiting.update(zip(later, outs))
         first += size
     moved, inflow = pl.pallas_call(
         arrive_kernel,
         out_shape=(shape(OUT, 8, 128), shape(CX, CY)),
-        in_specs=[VMEM] * (5 + len(done)),
+        in_specs=[VMEM] * (6 + len(done)),
         out_specs=(ANY, VMEM),
         scratch_shapes=[pltpu.SemaphoreType.DMA((4 + len(done),))],
         compiler_params=LIMIT,
         name="arrive",
-    )(small, *(received[v] for v in ("x_even", "x_odd", "y_even", "y_odd")), *done)
+    )(small, hot, *(received[v] for v in ("x_even", "x_odd", "y_even", "y_odd")), *done)
     return head, moved[None, None], inflow
 
 

time: 35.4 us -> 35.4 us (level)
  no operation moved by 1% of the time
where the time goes in v7:
time: 35.4 us; the launch traced here: 35.3 us
  Pallas kernels  15.9 us (45%)
  starting transfers between devices  13.2 us (37%)
  waiting for transfers between devices  4.63 us (13%)
  between operations  0.91 us (3%)
  local copies, waits for them, and re-layouts  0.67 us (2%)
    ppermute x8, starting transfers between devices, swap(): return lax.ppermute(value, AXES, pairs + [(b, a) for a, b in pairs])  13.2 us
    pallas_call x1, Pallas kernels, body(): pl.pallas_call(functools.partial(rest_kernel, first, size), out_shape=[ja...  6.5 us
    pallas_call x1, Pallas kernels, body(): pl.pallas_call(sweep_kernel, out_shape=(shape(NZ, CX, CY), shape(TABLE, P...  6.07 us
    ppermute x8, waiting for transfers between devices, swap(): return lax.ppermute(value, AXES, pairs + [(b, a) for a, b in pairs])  4.63 us
    pallas_call x1, Pallas kernels, body(): pl.pallas_call(arrive_kernel, out_shape=(shape(OUT, 8, 128), shape(CX, CY...  1.47 us
    pallas_call x1, Pallas kernels, body(): pl.pallas_call(odd_rows_kernel, out_shape=(shape(NZ, CX, CY),) * 5, in_sp...  1.25 us
  transfers between devices with their start and end apart: 8, of which 2 were waited for; matrix products, arithmetic and copies ran while one was open for 0% of the time, Pallas kernels for 18%

profile of v7, /device:TPU:38, one launch (start us, length us, event | category | flops | bytes accessed | tf_op | source)
XLA Modules:
  0.0 35.3 jit_solution(4944033212511805257)
XLA Ops:
  0.6 1.3 %odd_rows.1 = (f32[10,16,256]{2,1,0:T(8,128)S(1)}, f32[10,16,256]{2,1,0:T(8,128)S(1)}, f32[10,16,256]{2,1,0:T(8,128)S(1)}, f32[10,16,256]{2,1,0:T(8,128)S(1)}, f32[10,16,256]{2,1,0:T(8,128)S(1)}) custom-call(f32[10,16,256]{2,1,0:T(8,128)} %p_hbm.1, f32[10,16,256]{2,1,0:T(8,128)} %c_hbm.1, f32[10,16,256]{2,1,0:T(8,128)} %s_hbm.1, f32[10,16,256]{2,1,0:T(8,128)} %q_hbm.1), custom_call_target="tpu_custom_call" | custom-call | tf_op jit(solution)/shard_map/odd_rows/pallas_call | solution.py:459
  1.9 0.1 even_rows.1
  2.0 0.1 collective-permute-start
  2.1 0.0 copy-start
  2.1 3.4 %collective-permute-start.1 = (f32[10,16,256]{2,1,0:T(8,128)S(1)}, f32[10,16,256]{2,1,0:T(8,128)S(1)}, u32[]{:S(2)}, u32[]{:S(2)}) collective-permute-start(f32[10,16,256]{2,1,0:T(8,128)S(1)} %get-tuple-element.25), channel_id=1, source_target_pairs={{8,16},{24,32},{40,48},{56,64},{72,80},{88,96},{104,112},{120,128}... | collective-permute-start | bytes 491528 | tf_op jit(solution)/shard_map/ppermute | solution.py:439
  5.5 0.0 collective-permute-done.re_ref.rxe_ref
  5.5 3.6 %collective-permute-done.1.ro_ref.rxo_ref = f32[10,16,256]{2,1,0:T(8,128)S(1)} collective-permute-done((f32[10,16,256]{2,1,0:T(8,128)S(1)}, f32[10,16,256]{2,1,0:T(8,128)S(1)}, u32[]{:S(2)}, u32[]{:S(2)}) %collective-permute-start.1) | collective-permute-done | bytes 163872 | tf_op jit(solution)/shard_map/ppermute | solution.py:439
  9.1 0.0 copy-start.1
  9.1 0.4 %edge_lanes.1 = (f32[4,8,128]{2,1,0:T(8,128)S(1)}, f32[4,8,128]{2,1,0:T(8,128)S(1)}) custom-call(f32[10,16,256]{2,1,0:T(8,128)S(1)} %get-tuple-element.21.p_ref, f32[10,16,256]{2,1,0:T(8,128)S(1)} %get-tuple-element.22.c_ref, f32[10,16,256]{2,1,0:T(8,128)S(1)} %get-tuple-element.23.s_ref, f32[10,16,256]{2,1,0:T(8,128)S(1)} %get-tuple-element.24.q_ref, ...), custom_call_target="tpu_custom_call" | custom-call | tf_op jit(solution)/shard_map/edge_lanes/pallas_call | solution.py:478
  9.5 0.0 copy-start.3
  9.5 0.0 copy-start.2
  9.5 0.2 collective-permute-start.2
  9.7 3.7 %collective-permute-start.3 = (f32[4,8,128]{2,1,0:T(8,128)S(1)}, f32[4,8,128]{2,1,0:T(8,128)S(1)}, u32[]{:S(2)}, u32[]{:S(2)}) collective-permute-start(f32[4,8,128]{2,1,0:T(8,128)S(1)} %get-tuple-element.27), channel_id=1, source_target_pairs={{1,2},{3,4},{5,6},{9,10},{11,12},{13,14},{17,18},{19,20},{21,22},{... | collective-permute-start | bytes 49160 | tf_op jit(solution)/shard_map/ppermute | solution.py:439
  13.5 0.0 copy-start.4
  13.5 0.0 copy-done.3
  13.5 0.0 copy-done.2
  13.5 0.6 %copy-done.4 = s32[1,1,4]{2,1,0:T(1,128)S(1)} copy-done((s32[1,1,4]{2,1,0:T(1,128)S(1)}, s32[1,1,4]{2,1,0:T(1,128)}, u32[]{:S(2)}) %copy-start.4) | copy-done | bytes 40
  14.1 0.0 collective-permute-done.2.rye_ref
  14.1 1.0 %collective-permute-done.3.ryo_ref = f32[4,8,128]{2,1,0:T(8,128)S(1)} collective-permute-done((f32[4,8,128]{2,1,0:T(8,128)S(1)}, f32[4,8,128]{2,1,0:T(8,128)S(1)}, u32[]{:S(2)}, u32[]{:S(2)}) %collective-permute-start.3) | collective-permute-done | bytes 16416 | tf_op jit(solution)/shard_map/ppermute | solution.py:439
  15.2 0.0 copy-done
  15.2 0.0 copy-done.1
  15.2 6.1 %sweep.1 = (f32[10,16,256]{2,1,0:T(8,128)}, f8e4m3fn[800,768]{1,0:T(32,128)(4,1)S(1)}, f32[40,8,128]{2,1,0:T(8,128)S(1)}, f32[17,8,128]{2,1,0:T(8,128)S(1)}, f32...) custom-call(s32[24,128]{1,0:T(8,128)S(1)} %pad_add_fusion.small_ref, ...), custom_call_target="tpu_custom_call" | custom-call | tf_op jit(solution)/shard_map/sweep/pallas_call | solution.py:491
  21.3 0.1 collective-permute-start.6
  21.4 4.1 %collective-permute-start.7 = (f32[5,8,128]{2,1,0:T(8,128)S(1)}, f32[5,8,128]{2,1,0:T(8,128)S(1)}, u32[]{:S(2)}, u32[]{:S(2)}) collective-permute-start(f32[5,8,128]{2,1,0:T(8,128)S(1)} %get-tuple-element.34), channel_id=1, source_target_pairs={{1,2},{3,4},{5,6},{9,10},{11,12},{13,14},{17,18},{19,20},{21,22},{... | collective-permute-start | bytes 61448 | tf_op jit(solution)/shard_map/ppermute | solution.py:439
  25.5 0.0 collective-permute-start.4
  25.5 1.6 %collective-permute-start.5 = (f32[17,8,128]{2,1,0:T(8,128)S(1)}, f32[17,8,128]{2,1,0:T(8,128)S(1)}, u32[]{:S(2)}, u32[]{:S(2)}) collective-permute-start(f32[17,8,128]{2,1,0:T(8,128)S(1)} %get-tuple-element.32), channel_id=1, source_target_pairs={{8,16},{24,32},{40,48},{56,64},{72,80},{88,96},{104,112},{120,128}... | collective-permute-start | bytes 208904 | tf_op jit(solution)/shard_map/ppermute | solution.py:439
  27.1 6.5 %rest_0.1 = (f32[64,8,128]{2,1,0:T(8,128)S(1)}, bf16[256,1024]{1,0:T(8,128)(2,1)S(1)}) custom-call(f8e4m3fn[800,768]{1,0:T(32,128)(4,1)S(1)} %get-tuple-element.29.tab_ref, f32[104,8,128]{2,1,0:T(8,128)S(1)} %bitcast.7, s32[104,128]{1,0:T(8,128)S(1)} %bitcast.9, s32[24,128]{1,0:T(8,128)S(1)} %pad_add_fusion.small_ref), custom_call_target="tpu_custom_call" | custom-call | flops 6710886400 | bytes 1048576 | tf_op jit(solution)/shard_map/rest_0/pallas_call | solution.py:527
  33.6 0.0 collective-permute-done.6.ye_ref
  33.6 0.0 collective-permute-done.7.yo_ref
  33.6 0.0 collective-permute-done.4.xe_ref
  33.6 0.0 collective-permute-done.5.xo_ref
  33.6 1.5 %arrive.1 = (f32[144,8,128]{2,1,0:T(8,128)}, f32[16,256]{1,0:T(8,128)}) custom-call(s32[24,128]{1,0:T(8,128)S(1)} %pad_add_fusion.small_ref, bf16[256,1024]{1,0:T(8,128)(2,1)S(1)} %get-tuple-element.30.hot_ref, f32[17,8,128]{2,1,0:T(8,128)S(1)} %collective-permute-done.4.xe_ref, f32[17,8,128]{2,1,0:T(8,128)S(1)} %collective-permute-done.5.xo_ref, ...), custom_call_target="tpu_custom_call" | custom-call | tf_op jit(solution)/shard_map/arrive/pallas_call | solution.py:544
  (1 shorter events, 0.0 us)
Async XLA Ops:
  2.0 3.5 %collective-permute-start = (f32[10,16,256]{2,1,0:T(8,128)S(1)}, f32[10,16,256]{2,1,0:T(8,128)S(1)}, u32[]{:S(2)}, u32[]{:S(2)}) collective-permute-start(f32[10,16,256]{2,1,0:T(8,128)S(1)} %even_rows.1), channel_id=1, source_target_pairs={{0,8},{16,24},{32,40},{48,56},{64,72},{80,88},{96,104},{112,120},{... | collective-permute-start | bytes 491528 | tf_op jit(solution)/shard_map/ppermute | solution.py:439
  2.1 13.1 %copy-start = (f32[1,1,104,8,128]{4,3,2,1,0:T(8,128)S(1)}, f32[1,1,104,8,128]{4,3,2,1,0:T(8,128)}, u32[]{:S(2)}) copy-start(f32[1,1,104,8,128]{4,3,2,1,0:T(8,128)} %param.13) | copy-start | bytes 1277956
  2.1 6.9 %collective-permute-start.1 = (f32[10,16,256]{2,1,0:T(8,128)S(1)}, f32[10,16,256]{2,1,0:T(8,128)S(1)}, u32[]{:S(2)}, u32[]{:S(2)}) collective-permute-start(f32[10,16,256]{2,1,0:T(8,128)S(1)} %get-tuple-element.25), channel_id=1, source_target_pairs={{8,16},{24,32},{40,48},{56,64},{72,80},{88,96},{104,112},{120,128}... | collective-permute-start | bytes 491528 | tf_op jit(solution)/shard_map/ppermute | solution.py:439
  9.1 6.1 %copy-start.1 = (s32[1,1,104,128]{3,2,1,0:T(8,128)S(1)}, s32[1,1,104,128]{3,2,1,0:T(8,128)}, u32[]{:S(2)}) copy-start(s32[1,1,104,128]{3,2,1,0:T(8,128)} %param.15) | copy-start | bytes 159748
  9.5 3.9 %copy-start.3 = (s32[1,1,4,2,128]{4,3,2,1,0:T(2,128)S(1)}, s32[1,1,4,2,128]{4,3,2,1,0:T(2,128)}, u32[]{:S(2)}) copy-start(s32[1,1,4,2,128]{4,3,2,1,0:T(2,128)} %param.16) | copy-start | bytes 12292
  9.5 3.9 %copy-start.2 = (s32[1,1,4,2,128]{4,3,2,1,0:T(2,128)S(1)}, s32[1,1,4,2,128]{4,3,2,1,0:T(2,128)}, u32[]{:S(2)}) copy-start(s32[1,1,4,2,128]{4,3,2,1,0:T(2,128)} %param.17) | copy-start | bytes 12292
  9.5 4.6 %collective-permute-start.2 = (f32[4,8,128]{2,1,0:T(8,128)S(1)}, f32[4,8,128]{2,1,0:T(8,128)S(1)}, u32[]{:S(2)}, u32[]{:S(2)}) collective-permute-start(f32[4,8,128]{2,1,0:T(8,128)S(1)} %get-tuple-element.26), channel_id=1, source_target_pairs={{0,1},{2,3},{4,5},{6,7},{8,9},{10,11},{12,13},{14,15},{16,17},{18,... | collective-permute-start | bytes 49160 | tf_op jit(solution)/shard_map/ppermute | solution.py:439
  9.7 5.4 %collective-permute-start.3 = (f32[4,8,128]{2,1,0:T(8,128)S(1)}, f32[4,8,128]{2,1,0:T(8,128)S(1)}, u32[]{:S(2)}, u32[]{:S(2)}) collective-permute-start(f32[4,8,128]{2,1,0:T(8,128)S(1)} %get-tuple-element.27), channel_id=1, source_target_pairs={{1,2},{3,4},{5,6},{9,10},{11,12},{13,14},{17,18},{19,20},{21,22},{... | collective-permute-start | bytes 49160 | tf_op jit(solution)/shard_map/ppermute | solution.py:439
  13.5 0.7 %copy-start.4 = (s32[1,1,4]{2,1,0:T(1,128)S(1)}, s32[1,1,4]{2,1,0:T(1,128)}, u32[]{:S(2)}) copy-start(s32[1,1,4]{2,1,0:T(1,128)} %param.14) | copy-start | bytes 52
  21.3 12.3 %collective-permute-start.6 = (f32[5,8,128]{2,1,0:T(8,128)S(1)}, f32[5,8,128]{2,1,0:T(8,128)S(1)}, u32[]{:S(2)}, u32[]{:S(2)}) collective-permute-start(f32[5,8,128]{2,1,0:T(8,128)S(1)} %get-tuple-element.33), channel_id=1, source_target_pairs={{0,1},{2,3},{4,5},{6,7},{8,9},{10,11},{12,13},{14,15},{16,17},{18,... | collective-permute-start | bytes 61448 | tf_op jit(solution)/shard_map/ppermute | solution.py:439
  21.4 12.2 %collective-permute-start.7 = (f32[5,8,128]{2,1,0:T(8,128)S(1)}, f32[5,8,128]{2,1,0:T(8,128)S(1)}, u32[]{:S(2)}, u32[]{:S(2)}) collective-permute-start(f32[5,8,128]{2,1,0:T(8,128)S(1)} %get-tuple-element.34), channel_id=1, source_target_pairs={{1,2},{3,4},{5,6},{9,10},{11,12},{13,14},{17,18},{19,20},{21,22},{... | collective-permute-start | bytes 61448 | tf_op jit(solution)/shard_map/ppermute | solution.py:439
  25.5 8.1 %collective-permute-start.4 = (f32[17,8,128]{2,1,0:T(8,128)S(1)}, f32[17,8,128]{2,1,0:T(8,128)S(1)}, u32[]{:S(2)}, u32[]{:S(2)}) collective-permute-start(f32[17,8,128]{2,1,0:T(8,128)S(1)} %get-tuple-element.31), channel_id=1, source_target_pairs={{0,8},{16,24},{32,40},{48,56},{64,72},{80,88},{96,104},{112,120},{... | collective-permute-start | bytes 208904 | tf_op jit(solution)/shard_map/ppermute | solution.py:439
  25.5 8.1 %collective-permute-start.5 = (f32[17,8,128]{2,1,0:T(8,128)S(1)}, f32[17,8,128]{2,1,0:T(8,128)S(1)}, u32[]{:S(2)}, u32[]{:S(2)}) collective-permute-start(f32[17,8,128]{2,1,0:T(8,128)S(1)} %get-tuple-element.32), channel_id=1, source_target_pairs={{8,16},{24,32},{40,48},{56,64},{72,80},{88,96},{104,112},{120,128}... | collective-permute-start | bytes 208904 | tf_op jit(solution)/shard_map/ppermute | solution.py:439
